TPU v7x, 256 devices: a whole 4x4x8 slice. The times are simulated.
256 devices in a mesh: ctx: 64 (over x_lo, y, z), fsdp: 4 (over x_hi, core).
Axes of the slice: x: 4 (x_hi: 2, x_lo: 2; x = x_hi * 2 + x_lo), y: 4, z: 8, core: 2. Of those that a mesh axis runs over, the one named last changes fastest.
Arguments:
- query_rows: bfloat16 [8192, 2048], P('ctx', 'fsdp'), may hold values from -6 to 6
- key_rows: bfloat16 [8192, 2048], P('ctx', 'fsdp'), may hold values from -6 to 6
- value_rows: bfloat16 [8192, 2048], P('ctx', 'fsdp'), may hold values from -6 to 6
- out_proj: bfloat16 [2048, 4096], P('fsdp'), may hold values from -3 to 3
- cotangent: bfloat16 [8192, 4096], P('ctx', 'fsdp'), may hold values from -0.875 to 0.875
Outputs:
- layer_out: bfloat16 [8192, 4096], P('ctx', 'fsdp')
- grad_query: bfloat16 [8192, 2048], P('ctx', 'fsdp')
- grad_key: bfloat16 [8192, 2048], P('ctx', 'fsdp')
- grad_value: bfloat16 [8192, 2048], P('ctx', 'fsdp')
- proj_grad: float32 [4096, 2048], P('ctx', 'fsdp')
All inputs are finite; a program needn't handle non-finite values.
Results may differ from a plain program's by a relative error of at most 0.015.
Values may be sent and summed in bfloat16 or wider, within the bound.
No kernel may reach another device: no remote copies, remote signals or barrier semaphores. Data moves between devices by JAX's collectives and lax.ppermute only.
A program may use at most 128 MiB of HBM per device.

v0:
```python
import jax
import jax.numpy as jnp
from jax import lax
from jax.sharding import PartitionSpec as P

HEAD = 128


NEG_BIG = -1e30


def swapped(block, axis, apart):
    count = lax.axis_size(axis)
    route = []
    for low in range(count):
        high = low | 1 << apart
        if high != low and high < count:
            route += [(low, high), (high, low)]
    return lax.ppermute(block, axis, route)


def passed_along(block, axis, distance):
    devices = range(lax.axis_size(axis))
    route = [(i - distance, i) for i in devices if i - distance in devices]
    return lax.ppermute(block, axis, route)


def take_at(array_in, index_in):
    return lax.dynamic_index_in_dim(array_in, index_in, 0, keepdims=False)


def add_at(accum, index_in, q_term):
    return lax.dynamic_update_index_in_dim(accum, take_at(accum, index_in) + q_term, index_in, 0)


def head_view(block_in):
    return block_in.reshape(block_in.shape[0], -1, HEAD)


def pair_scores(q_blk, k_blk):
    return jnp.einsum(
        "ihd,jhd->hij", head_view(q_blk), head_view(k_blk), preferred_element_type=jnp.float32
    ) * HEAD ** (-0.5)


def causal_mask(q_part, k_part, tok_rows):
    q_pos = q_part * tok_rows + jnp.arange(tok_rows)
    k_pos = k_part * tok_rows + jnp.arange(tok_rows)
    return k_pos[None, :] <= q_pos[:, None]


def stats_pair(stats_state, q_half, k_half, q_all, kv_pack, allowed):
    run_max, run_sum = stats_state
    scores = jnp.where(
        allowed, pair_scores(take_at(q_all, q_half), take_at(kv_pack[0], k_half)), NEG_BIG
    )
    old_max = take_at(run_max, q_half)
    new_max = jnp.maximum(old_max, jnp.max(scores, axis=-1))
    weights = jnp.where(allowed, jnp.exp(scores - new_max[:, :, None]), 0.0)
    new_sum = jnp.exp(old_max - new_max) * take_at(run_sum, q_half) + jnp.sum(weights, axis=-1)
    return (
        lax.dynamic_update_index_in_dim(run_max, new_max, q_half, 0),
        lax.dynamic_update_index_in_dim(run_sum, new_sum, q_half, 0),
    )


def attend_pair(accum, q_half, k_half, q_all, log_total, kv_pack, allowed):
    q_blk = take_at(q_all, q_half)
    scores = pair_scores(q_blk, take_at(kv_pack[0], k_half))
    weights = jnp.where(allowed, jnp.exp(scores - take_at(log_total, q_half)[:, :, None]), 0.0)
    update = jnp.einsum(
        "hij,jhd->ihd",
        weights.astype(jnp.bfloat16),
        head_view(take_at(kv_pack[1], k_half)),
        preferred_element_type=jnp.float32,
    ).reshape(q_blk.shape[0], -1)
    return add_at(accum, q_half, update)


def grad_pair(q_blk, do_blk, lse_blk, delta_blk, k_blk, v_blk, allowed, want_query, want_keys):
    tok_rows = q_blk.shape[0]
    scores = pair_scores(q_blk, k_blk)
    weights = jnp.where(allowed, jnp.exp(scores - lse_blk[:, :, None]), 0.0)
    grad_prob = jnp.einsum(
        "ihd,jhd->hij", head_view(do_blk), head_view(v_blk), preferred_element_type=jnp.float32
    )
    dscore = (weights * (grad_prob - delta_blk[:, :, None])).astype(jnp.bfloat16)
    results = []
    if want_query:
        results.append(
            jnp.einsum(
                "hij,jhd->ihd", dscore, head_view(k_blk), preferred_element_type=jnp.float32
            ).reshape(tok_rows, -1)
            * HEAD ** (-0.5)
        )
    if want_keys:
        results.append(
            jnp.einsum(
                "hij,ihd->jhd", dscore, head_view(q_blk), preferred_element_type=jnp.float32
            ).reshape(tok_rows, -1)
            * HEAD ** (-0.5)
        )
        results.append(
            jnp.einsum(
                "hij,ihd->jhd",
                weights.astype(jnp.bfloat16),
                head_view(do_blk),
                preferred_element_type=jnp.float32,
            ).reshape(tok_rows, -1)
        )
    return tuple(results)


def per_device(query_rows, key_rows, value_rows, out_proj, cotangent):
    tok_rows = query_rows.shape[0]
    width_dev = query_rows.shape[1]
    half_w = width_dev // 2
    heads_half = half_w // HEAD
    ctx_size = lax.axis_size("ctx")
    my_index = lax.axis_index("ctx")
    is_even = my_index % 2 == 0
    full_cot = lax.all_gather(cotangent, "fsdp", axis=1, tiled=True)
    grad_attn = lax.dot_general(
        full_cot, out_proj, (((1,), (1,)), ((), ())), preferred_element_type=jnp.float32
    ).astype(jnp.bfloat16)
    inputs = jnp.stack([query_rows, key_rows, value_rows, grad_attn])
    kept_part = jnp.where(is_even, inputs[:, :, :half_w], inputs[:, :, half_w:])
    given_part = jnp.where(is_even, inputs[:, :, half_w:], inputs[:, :, :half_w])
    arrived = swapped(given_part, "ctx", 0)
    partner = my_index + 1 - 2 * (my_index % 2)
    local_parts = jnp.stack([kept_part, arrived], axis=1)
    q_all, k_all, v_all, do_all = (local_parts[0], local_parts[1], local_parts[2], local_parts[3])
    own_parts = jnp.stack([my_index, partner])
    kv_own = jnp.stack([k_all, v_all])
    stats_state = (
        jnp.full((2, heads_half, tok_rows), NEG_BIG, jnp.float32),
        jnp.zeros((2, heads_half, tok_rows), jnp.float32),
    )
    for q_half in (0, 1):
        for k_half in (q_half, 1 - q_half):
            allowed = causal_mask(own_parts[q_half], own_parts[k_half], tok_rows)
            stats_state = stats_pair(stats_state, q_half, k_half, q_all, kv_own, allowed)
    key_store = jnp.zeros((ctx_size // 2,) + kv_own.shape, jnp.bfloat16)

    def forward_hop(hop_idx, carried):
        kv_pack, current_state, stored = carried
        kv_pack = passed_along(kv_pack, "ctx", 2)
        stored = lax.dynamic_update_index_in_dim(stored, kv_pack, hop_idx, 0)

        def stats_all(current):
            for q_half in (0, 1):
                for k_half in (0, 1):
                    current = stats_pair(current, q_half, k_half, q_all, kv_pack, True)
            return current

        current_state = lax.cond(
            my_index - 2 * hop_idx >= 0, stats_all, lambda current: current, current_state
        )
        return (kv_pack, current_state, stored)

    kv_final, stats_state, key_store = lax.fori_loop(
        1, ctx_size // 2, forward_hop, (kv_own, stats_state, key_store)
    )
    run_max, run_sum = stats_state
    log_total = run_max + jnp.log(run_sum)
    attn_acc = jnp.zeros((2, tok_rows, half_w), jnp.float32)
    for q_half in (0, 1):
        for k_half in (q_half, 1 - q_half):
            allowed = causal_mask(own_parts[q_half], own_parts[k_half], tok_rows)
            attn_acc = attend_pair(attn_acc, q_half, k_half, q_all, log_total, kv_own, allowed)

    def attend_hop(hop_idx, accum):
        kv_pack = take_at(key_store, hop_idx)

        def attend_all(current):
            for q_half in (0, 1):
                for k_half in (0, 1):
                    current = attend_pair(current, q_half, k_half, q_all, log_total, kv_pack, True)
            return current

        accum = lax.cond(my_index - 2 * hop_idx >= 0, attend_all, lambda current: current, accum)
        return accum

    attn_acc = lax.fori_loop(1, ctx_size // 2, attend_hop, attn_acc)
    attended = attn_acc.astype(jnp.bfloat16)
    row_delta = jnp.swapaxes(
        jnp.sum(
            (do_all.astype(jnp.float32) * attended.astype(jnp.float32)).reshape(
                2, tok_rows, heads_half, HEAD
            ),
            axis=-1,
        ),
        1,
        2,
    )
    dq_acc = jnp.zeros((2, tok_rows, half_w), jnp.float32)
    dk_acc = jnp.zeros((2, tok_rows, half_w), jnp.float32)
    dv_acc = jnp.zeros((2, tok_rows, half_w), jnp.float32)
    for q_half in (0, 1):
        for k_half in (0, 1):
            allowed = causal_mask(own_parts[q_half], own_parts[k_half], tok_rows)
            dq_term, dk_term, dv_term = grad_pair(
                q_all[q_half],
                do_all[q_half],
                log_total[q_half],
                row_delta[q_half],
                k_all[k_half],
                v_all[k_half],
                allowed,
                True,
                True,
            )
            dq_acc = dq_acc.at[q_half].add(dq_term)
            dk_acc = dk_acc.at[k_half].add(dk_term)
            dv_acc = dv_acc.at[k_half].add(dv_term)
    qd_own = jnp.stack([q_all, do_all])

    def backward_hop(hop_idx, carried):
        qd_pack, stat_lse, stat_delta, dq_now, dk_now, dv_now = carried
        qd_pack = passed_along(qd_pack, "ctx", -2)
        stat_lse, stat_delta = passed_along((stat_lse, stat_delta), "ctx", -2)
        kv_pack = take_at(key_store, hop_idx)

        def query_side(accum, q_half, k_half):
            q_term = grad_pair(
                take_at(q_all, q_half),
                take_at(do_all, q_half),
                take_at(log_total, q_half),
                take_at(row_delta, q_half),
                take_at(kv_pack[0], k_half),
                take_at(kv_pack[1], k_half),
                True,
                True,
                False,
            )[0]
            return add_at(accum, q_half, q_term)

        def key_side(key_accs, q_half, k_half):
            dk_term, dv_term = grad_pair(
                take_at(qd_pack[0], q_half),
                take_at(qd_pack[1], q_half),
                take_at(stat_lse, q_half),
                take_at(stat_delta, q_half),
                take_at(k_all, k_half),
                take_at(v_all, k_half),
                True,
                False,
                True,
            )
            return (add_at(key_accs[0], k_half, dk_term), add_at(key_accs[1], k_half, dv_term))

        def query_all(accum):
            for q_half in (0, 1):
                for k_half in (0, 1):
                    accum = query_side(accum, q_half, k_half)
            return accum

        def keys_all(key_accs):
            for q_half in (0, 1):
                for k_half in (0, 1):
                    key_accs = key_side(key_accs, q_half, k_half)
            return key_accs

        dq_now = lax.cond(my_index - 2 * hop_idx >= 0, query_all, lambda current: current, dq_now)
        key_accs = lax.cond(
            my_index + 2 * hop_idx < ctx_size, keys_all, lambda current: current, (dk_now, dv_now)
        )
        return (qd_pack, stat_lse, stat_delta, dq_now, key_accs[0], key_accs[1])

    looped = lax.fori_loop(
        1, ctx_size // 2, backward_hop, (qd_own, log_total, row_delta, dq_acc, dk_acc, dv_acc)
    )
    grad_q = looped[3].astype(jnp.bfloat16)
    grad_k = looped[4].astype(jnp.bfloat16)
    grad_v = looped[5].astype(jnp.bfloat16)
    mine_part = jnp.stack([attended[0], grad_q[0], grad_k[0], grad_v[0]])
    home_part = jnp.stack([attended[1], grad_q[1], grad_k[1], grad_v[1]])
    returned = swapped(home_part, "ctx", 0)
    merged = jnp.where(
        is_even,
        jnp.concatenate([mine_part, returned], axis=-1),
        jnp.concatenate([returned, mine_part], axis=-1),
    )
    attn_full = merged[0]
    partial_value = jnp.dot(attn_full, out_proj, preferred_element_type=jnp.float32)
    layer_out = lax.psum_scatter(
        partial_value.astype(jnp.bfloat16), "fsdp", scatter_dimension=1, tiled=True
    )
    proj_grad = lax.psum_scatter(
        lax.dot_general(
            full_cot, attn_full, (((0,), (0,)), ((), ())), preferred_element_type=jnp.float32
        ),
        "ctx",
        scatter_dimension=0,
        tiled=True,
    )
    return (layer_out, merged[1], merged[2], merged[3], proj_grad)


def solution(mesh):
    in_specs = (
        P("ctx", "fsdp"),
        P("ctx", "fsdp"),
        P("ctx", "fsdp"),
        P("fsdp", None),
        P("ctx", "fsdp"),
    )
    out_specs = (
        P("ctx", "fsdp"),
        P("ctx", "fsdp"),
        P("ctx", "fsdp"),
        P("ctx", "fsdp"),
        P("ctx", "fsdp"),
    )
    return jax.shard_map(
        per_device, mesh=mesh, in_specs=in_specs, out_specs=out_specs, check_vma=False
    )
```

profile of v0, /device:TPU:32, one launch (start us, length us, event | category | flops | bytes accessed | tf_op | source)
XLA Modules:
  0.0 1952.7 jit_solution(9153340040638319867)
XLA Ops:
  8.1 27.6 %all-gather.2.cloned.1.call-done = bf16[128,4096]{1,0:T(8,128)(2,1)} async-done(((bf16[128,1024]{1,0:T(8,128)(2,1)}), bf16[128,4096]{1,0:T(8,128)(2,1)}) %all-gather.2.cloned.1.call-update) | async-done | bytes 1048592 | tf_op jit(solution)/shard_map/all_gather | solution.py:122
  58.9 559.8 %while.75 = (s32[]{:T(128)}, bf16[2,2,128,256]{2,3,1,0:T(8,128)(2,1)S(1)}, f32[2,2,128]{2,1,0:T(2,128)S(1)}, f32[2,2,128]{2,1,0:T(2,128)}, bf16[32,2,2,128,256]{...) while((s32[]{:T(128)}, ...), condition=%wide.region_19.20_spmd, body=%wide.region_8.19_spmd.sunk | while | flops 34083844 | bytes 4260145 | solution.py:161
  156.9 16.7 collective-permute-start
  181.2 15.5 collective-permute-start
  298.2 15.2 collective-permute-start
  529.0 15.5 collective-permute-start
  572.4 15.5 collective-permute-start
  596.2 15.5 collective-permute-start
  638.0 883.4 %while.77 = (s32[]{:T(128)}, bf16[2,2,128,256]{2,3,1,0:T(8,128)(2,1)}, f32[2,2,128]{2,1,0:T(2,128)S(1)}, f32[2,2,128]{2,1,0:T(2,128)S(1)}, f32[2,128,256]{1,2,0:...) while((s32[]{:T(128)}, ...), condition=%wide.region_30.31_spmd, body=%wide.region_25.30_spmd.sunk | while | flops 236978176 | bytes 18670124 | solution.py:270
  642.1 16.2 collective-permute-done.2
  667.9 21.2 %collective-permute-done.2 = f32[2,2,128]{2,1,0:T(2,128)S(1)} collective-permute-done((f32[2,2,128]{2,1,0:T(2,128)S(1)}, f32[2,2,128]{2,1,0:T(2,128)S(1)}, u32[]{:S(2)}, u32[]{:S(2)}) %collective-permute-start.2) | collective-permute-done | bytes 2080 | tf_op jit(solution)/shard_map/while/body/eval_jaxpr/ppermute | solution.py:25
  697.8 20.8 %collective-permute-done.2 = f32[2,2,128]{2,1,0:T(2,128)S(1)} collective-permute-done((f32[2,2,128]{2,1,0:T(2,128)S(1)}, f32[2,2,128]{2,1,0:T(2,128)S(1)}, u32[]{:S(2)}, u32[]{:S(2)}) %collective-permute-start.2) | collective-permute-done | bytes 2080 | tf_op jit(solution)/shard_map/while/body/eval_jaxpr/ppermute | solution.py:25
  750.7 29.1 %collective-permute-done.2 = f32[2,2,128]{2,1,0:T(2,128)S(1)} collective-permute-done((f32[2,2,128]{2,1,0:T(2,128)S(1)}, f32[2,2,128]{2,1,0:T(2,128)S(1)}, u32[]{:S(2)}, u32[]{:S(2)}) %collective-permute-start.2) | collective-permute-done | bytes 2080 | tf_op jit(solution)/shard_map/while/body/eval_jaxpr/ppermute | solution.py:25
  788.5 24.9 %collective-permute-done.2 = f32[2,2,128]{2,1,0:T(2,128)S(1)} collective-permute-done((f32[2,2,128]{2,1,0:T(2,128)S(1)}, f32[2,2,128]{2,1,0:T(2,128)S(1)}, u32[]{:S(2)}, u32[]{:S(2)}) %collective-permute-start.2) | collective-permute-done | bytes 2080 | tf_op jit(solution)/shard_map/while/body/eval_jaxpr/ppermute | solution.py:25
  822.1 16.6 collective-permute-done.2
  847.4 24.4 %collective-permute-done.2 = f32[2,2,128]{2,1,0:T(2,128)S(1)} collective-permute-done((f32[2,2,128]{2,1,0:T(2,128)S(1)}, f32[2,2,128]{2,1,0:T(2,128)S(1)}, u32[]{:S(2)}, u32[]{:S(2)}) %collective-permute-start.2) | collective-permute-done | bytes 2080 | tf_op jit(solution)/shard_map/while/body/eval_jaxpr/ppermute | solution.py:25
  880.4 20.8 %collective-permute-done.2 = f32[2,2,128]{2,1,0:T(2,128)S(1)} collective-permute-done((f32[2,2,128]{2,1,0:T(2,128)S(1)}, f32[2,2,128]{2,1,0:T(2,128)S(1)}, u32[]{:S(2)}, u32[]{:S(2)}) %collective-permute-start.2) | collective-permute-done | bytes 2080 | tf_op jit(solution)/shard_map/while/body/eval_jaxpr/ppermute | solution.py:25
  909.9 24.6 %collective-permute-done.2 = f32[2,2,128]{2,1,0:T(2,128)S(1)} collective-permute-done((f32[2,2,128]{2,1,0:T(2,128)S(1)}, f32[2,2,128]{2,1,0:T(2,128)S(1)}, u32[]{:S(2)}, u32[]{:S(2)}) %collective-permute-start.2) | collective-permute-done | bytes 2080 | tf_op jit(solution)/shard_map/while/body/eval_jaxpr/ppermute | solution.py:25
  961.0 33.8 %collective-permute-done.2 = f32[2,2,128]{2,1,0:T(2,128)S(1)} collective-permute-done((f32[2,2,128]{2,1,0:T(2,128)S(1)}, f32[2,2,128]{2,1,0:T(2,128)S(1)}, u32[]{:S(2)}, u32[]{:S(2)}) %collective-permute-start.2) | collective-permute-done | bytes 2080 | tf_op jit(solution)/shard_map/while/body/eval_jaxpr/ppermute | solution.py:25
  1004.3 19.2 collective-permute-done.2
  1033.0 17.6 collective-permute-done.2
  1060.1 19.9 %collective-permute-done.2 = f32[2,2,128]{2,1,0:T(2,128)S(1)} collective-permute-done((f32[2,2,128]{2,1,0:T(2,128)S(1)}, f32[2,2,128]{2,1,0:T(2,128)S(1)}, u32[]{:S(2)}, u32[]{:S(2)}) %collective-permute-start.2) | collective-permute-done | bytes 2080 | tf_op jit(solution)/shard_map/while/body/eval_jaxpr/ppermute | solution.py:25
  1089.4 15.2 collective-permute-done.2
  1114.1 22.4 %collective-permute-done.2 = f32[2,2,128]{2,1,0:T(2,128)S(1)} collective-permute-done((f32[2,2,128]{2,1,0:T(2,128)S(1)}, f32[2,2,128]{2,1,0:T(2,128)S(1)}, u32[]{:S(2)}, u32[]{:S(2)}) %collective-permute-start.2) | collective-permute-done | bytes 2080 | tf_op jit(solution)/shard_map/while/body/eval_jaxpr/ppermute | solution.py:25
  1223.4 27.2 %collective-permute-done.2 = f32[2,2,128]{2,1,0:T(2,128)S(1)} collective-permute-done((f32[2,2,128]{2,1,0:T(2,128)S(1)}, f32[2,2,128]{2,1,0:T(2,128)S(1)}, u32[]{:S(2)}, u32[]{:S(2)}) %collective-permute-start.2) | collective-permute-done | bytes 2080 | tf_op jit(solution)/shard_map/while/body/eval_jaxpr/ppermute | solution.py:25
  1278.0 27.4 %collective-permute-done.2 = f32[2,2,128]{2,1,0:T(2,128)S(1)} collective-permute-done((f32[2,2,128]{2,1,0:T(2,128)S(1)}, f32[2,2,128]{2,1,0:T(2,128)S(1)}, u32[]{:S(2)}, u32[]{:S(2)}) %collective-permute-start.2) | collective-permute-done | bytes 2080 | tf_op jit(solution)/shard_map/while/body/eval_jaxpr/ppermute | solution.py:25
  1353.4 29.3 %collective-permute-done.2 = f32[2,2,128]{2,1,0:T(2,128)S(1)} collective-permute-done((f32[2,2,128]{2,1,0:T(2,128)S(1)}, f32[2,2,128]{2,1,0:T(2,128)S(1)}, u32[]{:S(2)}, u32[]{:S(2)}) %collective-permute-start.2) | collective-permute-done | bytes 2080 | tf_op jit(solution)/shard_map/while/body/eval_jaxpr/ppermute | solution.py:25
  1412.8 44.5 %collective-permute-done.2 = f32[2,2,128]{2,1,0:T(2,128)S(1)} collective-permute-done((f32[2,2,128]{2,1,0:T(2,128)S(1)}, f32[2,2,128]{2,1,0:T(2,128)S(1)}, u32[]{:S(2)}, u32[]{:S(2)}) %collective-permute-start.2) | collective-permute-done | bytes 2080 | tf_op jit(solution)/shard_map/while/body/eval_jaxpr/ppermute | solution.py:25
  1466.7 23.8 %collective-permute-done.2 = f32[2,2,128]{2,1,0:T(2,128)S(1)} collective-permute-done((f32[2,2,128]{2,1,0:T(2,128)S(1)}, f32[2,2,128]{2,1,0:T(2,128)S(1)}, u32[]{:S(2)}, u32[]{:S(2)}) %collective-permute-start.2) | collective-permute-done | bytes 2080 | tf_op jit(solution)/shard_map/while/body/eval_jaxpr/ppermute | solution.py:25
  1500.0 15.8 collective-permute-done.2
  1547.0 68.2 %reduce-scatter.5.cloned.1.call-done = bf16[128,1024]{1,0:T(8,128)(2,1)} async-done(((bf16[128,4096]{1,0:T(8,128)(2,1)}), bf16[128,1024]{1,0:T(8,128)(2,1)}) %reduce-scatter.5.cloned.1.call-update) | async-done | bytes 262160 | tf_op jit(solution)/shard_map/reduce_scatter | solution.py:286
  1615.2 330.9 %reduce-scatter.7.cloned.1.call-done = f32[64,512]{1,0:T(8,128)} async-done(((f32[4096,512]{1,0:T(8,128)}), f32[64,512]{1,0:T(8,128)}) %reduce-scatter.7.cloned.1.call-update) | async-done | bytes 131088
  (1507 shorter events, 1039.7 us)
Async XLA Ops:
  7.2 28.6 %all-gather.2.cloned.1.call-start = ((), (), s32[]{:S(2)}) async-start(), calls=%async_computation.2 | async-start | bytes 1310720 | tf_op jit(solution)/shard_map/all_gather | solution.py:122
  7.9 1607.3 %reduce-scatter.5.cloned.1.call-start = ((), (), s32[]{:S(2)}) async-start(), calls=%async_computation.3 | async-start | bytes 1310720 | tf_op jit(solution)/shard_map/reduce_scatter | solution.py:286
  746.8 33.1 %collective-permute-start.1 = (bf16[2,2,128,256]{2,3,1,0:T(8,128)(2,1)}, bf16[2,2,128,256]{2,3,1,0:T(8,128)(2,1)S(1)}, u32[]{:S(2)}, u32[]{:S(2)}) collective-permute-start(bf16[2,2,128,256]{2,3,1,0:T(8,128)(2,1)} %get-tuple-element.1425), channel_id=1, source_target_pairs={{8,0},{12,4},{16,8},{20,12},{24,16},{28,20},{32,24},{36,28},{40,32... | collective-permute-start | bytes 786440 | tf_op jit(solution)/shard_map/while/body/eval_jaxpr/ppermute | solution.py:25
  748.1 31.8 %collective-permute-start.2 = (f32[2,2,128]{2,1,0:T(2,128)S(1)}, f32[2,2,128]{2,1,0:T(2,128)S(1)}, u32[]{:S(2)}, u32[]{:S(2)}) collective-permute-start(f32[2,2,128]{2,1,0:T(2,128)S(1)} %get-tuple-element.1426), channel_id=1, source_target_pairs={{8,0},{12,4},{16,8},{20,12},{24,16},{28,20},{32,24},{36,28},{40,32... | collective-permute-start | bytes 6152 | tf_op jit(solution)/shard_map/while/body/eval_jaxpr/ppermute | solution.py:25
  749.4 30.5 %collective-permute-start.3 = (f32[2,2,128]{2,1,0:T(2,128)S(1)}, f32[2,2,128]{2,1,0:T(2,128)S(1)}, u32[]{:S(2)}, u32[]{:S(2)}) collective-permute-start(f32[2,2,128]{2,1,0:T(2,128)S(1)} %get-tuple-element.1427), channel_id=1, source_target_pairs={{8,0},{12,4},{16,8},{20,12},{24,16},{28,20},{32,24},{36,28},{40,32... | collective-permute-start | bytes 6152 | tf_op jit(solution)/shard_map/while/body/eval_jaxpr/ppermute | solution.py:25
  784.6 28.8 %collective-permute-start.1 = (bf16[2,2,128,256]{2,3,1,0:T(8,128)(2,1)}, bf16[2,2,128,256]{2,3,1,0:T(8,128)(2,1)S(1)}, u32[]{:S(2)}, u32[]{:S(2)}) collective-permute-start(bf16[2,2,128,256]{2,3,1,0:T(8,128)(2,1)} %get-tuple-element.1425), channel_id=1, source_target_pairs={{8,0},{12,4},{16,8},{20,12},{24,16},{28,20},{32,24},{36,28},{40,32... | collective-permute-start | bytes 786440 | tf_op jit(solution)/shard_map/while/body/eval_jaxpr/ppermute | solution.py:25
  785.9 27.5 %collective-permute-start.2 = (f32[2,2,128]{2,1,0:T(2,128)S(1)}, f32[2,2,128]{2,1,0:T(2,128)S(1)}, u32[]{:S(2)}, u32[]{:S(2)}) collective-permute-start(f32[2,2,128]{2,1,0:T(2,128)S(1)} %get-tuple-element.1426), channel_id=1, source_target_pairs={{8,0},{12,4},{16,8},{20,12},{24,16},{28,20},{32,24},{36,28},{40,32... | collective-permute-start | bytes 6152 | tf_op jit(solution)/shard_map/while/body/eval_jaxpr/ppermute | solution.py:25
  787.2 26.3 %collective-permute-start.3 = (f32[2,2,128]{2,1,0:T(2,128)S(1)}, f32[2,2,128]{2,1,0:T(2,128)S(1)}, u32[]{:S(2)}, u32[]{:S(2)}) collective-permute-start(f32[2,2,128]{2,1,0:T(2,128)S(1)} %get-tuple-element.1427), channel_id=1, source_target_pairs={{8,0},{12,4},{16,8},{20,12},{24,16},{28,20},{32,24},{36,28},{40,32... | collective-permute-start | bytes 6152 | tf_op jit(solution)/shard_map/while/body/eval_jaxpr/ppermute | solution.py:25
  843.5 28.3 %collective-permute-start.1 = (bf16[2,2,128,256]{2,3,1,0:T(8,128)(2,1)}, bf16[2,2,128,256]{2,3,1,0:T(8,128)(2,1)S(1)}, u32[]{:S(2)}, u32[]{:S(2)}) collective-permute-start(bf16[2,2,128,256]{2,3,1,0:T(8,128)(2,1)} %get-tuple-element.1425), channel_id=1, source_target_pairs={{8,0},{12,4},{16,8},{20,12},{24,16},{28,20},{32,24},{36,28},{40,32... | collective-permute-start | bytes 786440 | tf_op jit(solution)/shard_map/while/body/eval_jaxpr/ppermute | solution.py:25
  844.8 27.0 %collective-permute-start.2 = (f32[2,2,128]{2,1,0:T(2,128)S(1)}, f32[2,2,128]{2,1,0:T(2,128)S(1)}, u32[]{:S(2)}, u32[]{:S(2)}) collective-permute-start(f32[2,2,128]{2,1,0:T(2,128)S(1)} %get-tuple-element.1426), channel_id=1, source_target_pairs={{8,0},{12,4},{16,8},{20,12},{24,16},{28,20},{32,24},{36,28},{40,32... | collective-permute-start | bytes 6152 | tf_op jit(solution)/shard_map/while/body/eval_jaxpr/ppermute | solution.py:25
  906.0 28.6 %collective-permute-start.1 = (bf16[2,2,128,256]{2,3,1,0:T(8,128)(2,1)}, bf16[2,2,128,256]{2,3,1,0:T(8,128)(2,1)S(1)}, u32[]{:S(2)}, u32[]{:S(2)}) collective-permute-start(bf16[2,2,128,256]{2,3,1,0:T(8,128)(2,1)} %get-tuple-element.1425), channel_id=1, source_target_pairs={{8,0},{12,4},{16,8},{20,12},{24,16},{28,20},{32,24},{36,28},{40,32... | collective-permute-start | bytes 786440 | tf_op jit(solution)/shard_map/while/body/eval_jaxpr/ppermute | solution.py:25
  907.3 27.2 %collective-permute-start.2 = (f32[2,2,128]{2,1,0:T(2,128)S(1)}, f32[2,2,128]{2,1,0:T(2,128)S(1)}, u32[]{:S(2)}, u32[]{:S(2)}) collective-permute-start(f32[2,2,128]{2,1,0:T(2,128)S(1)} %get-tuple-element.1426), channel_id=1, source_target_pairs={{8,0},{12,4},{16,8},{20,12},{24,16},{28,20},{32,24},{36,28},{40,32... | collective-permute-start | bytes 6152 | tf_op jit(solution)/shard_map/while/body/eval_jaxpr/ppermute | solution.py:25
  957.1 38.6 %collective-permute-start.1 = (bf16[2,2,128,256]{2,3,1,0:T(8,128)(2,1)}, bf16[2,2,128,256]{2,3,1,0:T(8,128)(2,1)S(1)}, u32[]{:S(2)}, u32[]{:S(2)}) collective-permute-start(bf16[2,2,128,256]{2,3,1,0:T(8,128)(2,1)} %get-tuple-element.1425), channel_id=1, source_target_pairs={{8,0},{12,4},{16,8},{20,12},{24,16},{28,20},{32,24},{36,28},{40,32... | collective-permute-start | bytes 786440 | tf_op jit(solution)/shard_map/while/body/eval_jaxpr/ppermute | solution.py:25
  958.4 36.4 %collective-permute-start.2 = (f32[2,2,128]{2,1,0:T(2,128)S(1)}, f32[2,2,128]{2,1,0:T(2,128)S(1)}, u32[]{:S(2)}, u32[]{:S(2)}) collective-permute-start(f32[2,2,128]{2,1,0:T(2,128)S(1)} %get-tuple-element.1426), channel_id=1, source_target_pairs={{8,0},{12,4},{16,8},{20,12},{24,16},{28,20},{32,24},{36,28},{40,32... | collective-permute-start | bytes 6152 | tf_op jit(solution)/shard_map/while/body/eval_jaxpr/ppermute | solution.py:25
  959.7 36.0 %collective-permute-start.3 = (f32[2,2,128]{2,1,0:T(2,128)S(1)}, f32[2,2,128]{2,1,0:T(2,128)S(1)}, u32[]{:S(2)}, u32[]{:S(2)}) collective-permute-start(f32[2,2,128]{2,1,0:T(2,128)S(1)} %get-tuple-element.1427), channel_id=1, source_target_pairs={{8,0},{12,4},{16,8},{20,12},{24,16},{28,20},{32,24},{36,28},{40,32... | collective-permute-start | bytes 6152 | tf_op jit(solution)/shard_map/while/body/eval_jaxpr/ppermute | solution.py:25
  1110.2 27.1 %collective-permute-start.1 = (bf16[2,2,128,256]{2,3,1,0:T(8,128)(2,1)}, bf16[2,2,128,256]{2,3,1,0:T(8,128)(2,1)S(1)}, u32[]{:S(2)}, u32[]{:S(2)}) collective-permute-start(bf16[2,2,128,256]{2,3,1,0:T(8,128)(2,1)} %get-tuple-element.1425), channel_id=1, source_target_pairs={{8,0},{12,4},{16,8},{20,12},{24,16},{28,20},{32,24},{36,28},{40,32... | collective-permute-start | bytes 786440 | tf_op jit(solution)/shard_map/while/body/eval_jaxpr/ppermute | solution.py:25
  1219.5 32.0 %collective-permute-start.1 = (bf16[2,2,128,256]{2,3,1,0:T(8,128)(2,1)}, bf16[2,2,128,256]{2,3,1,0:T(8,128)(2,1)S(1)}, u32[]{:S(2)}, u32[]{:S(2)}) collective-permute-start(bf16[2,2,128,256]{2,3,1,0:T(8,128)(2,1)} %get-tuple-element.1425), channel_id=1, source_target_pairs={{8,0},{12,4},{16,8},{20,12},{24,16},{28,20},{32,24},{36,28},{40,32... | collective-permute-start | bytes 786440 | tf_op jit(solution)/shard_map/while/body/eval_jaxpr/ppermute | solution.py:25
  1220.8 29.9 %collective-permute-start.2 = (f32[2,2,128]{2,1,0:T(2,128)S(1)}, f32[2,2,128]{2,1,0:T(2,128)S(1)}, u32[]{:S(2)}, u32[]{:S(2)}) collective-permute-start(f32[2,2,128]{2,1,0:T(2,128)S(1)} %get-tuple-element.1426), channel_id=1, source_target_pairs={{8,0},{12,4},{16,8},{20,12},{24,16},{28,20},{32,24},{36,28},{40,32... | collective-permute-start | bytes 6152 | tf_op jit(solution)/shard_map/while/body/eval_jaxpr/ppermute | solution.py:25
  1222.1 29.4 %collective-permute-start.3 = (f32[2,2,128]{2,1,0:T(2,128)S(1)}, f32[2,2,128]{2,1,0:T(2,128)S(1)}, u32[]{:S(2)}, u32[]{:S(2)}) collective-permute-start(f32[2,2,128]{2,1,0:T(2,128)S(1)} %get-tuple-element.1427), channel_id=1, source_target_pairs={{8,0},{12,4},{16,8},{20,12},{24,16},{28,20},{32,24},{36,28},{40,32... | collective-permute-start | bytes 6152 | tf_op jit(solution)/shard_map/while/body/eval_jaxpr/ppermute | solution.py:25
  1274.1 32.2 %collective-permute-start.1 = (bf16[2,2,128,256]{2,3,1,0:T(8,128)(2,1)}, bf16[2,2,128,256]{2,3,1,0:T(8,128)(2,1)S(1)}, u32[]{:S(2)}, u32[]{:S(2)}) collective-permute-start(bf16[2,2,128,256]{2,3,1,0:T(8,128)(2,1)} %get-tuple-element.1425), channel_id=1, source_target_pairs={{8,0},{12,4},{16,8},{20,12},{24,16},{28,20},{32,24},{36,28},{40,32... | collective-permute-start | bytes 786440 | tf_op jit(solution)/shard_map/while/body/eval_jaxpr/ppermute | solution.py:25
  1275.4 30.1 %collective-permute-start.2 = (f32[2,2,128]{2,1,0:T(2,128)S(1)}, f32[2,2,128]{2,1,0:T(2,128)S(1)}, u32[]{:S(2)}, u32[]{:S(2)}) collective-permute-start(f32[2,2,128]{2,1,0:T(2,128)S(1)} %get-tuple-element.1426), channel_id=1, source_target_pairs={{8,0},{12,4},{16,8},{20,12},{24,16},{28,20},{32,24},{36,28},{40,32... | collective-permute-start | bytes 6152 | tf_op jit(solution)/shard_map/while/body/eval_jaxpr/ppermute | solution.py:25
  1276.7 29.6 %collective-permute-start.3 = (f32[2,2,128]{2,1,0:T(2,128)S(1)}, f32[2,2,128]{2,1,0:T(2,128)S(1)}, u32[]{:S(2)}, u32[]{:S(2)}) collective-permute-start(f32[2,2,128]{2,1,0:T(2,128)S(1)} %get-tuple-element.1427), channel_id=1, source_target_pairs={{8,0},{12,4},{16,8},{20,12},{24,16},{28,20},{32,24},{36,28},{40,32... | collective-permute-start | bytes 6152 | tf_op jit(solution)/shard_map/while/body/eval_jaxpr/ppermute | solution.py:25
  1349.5 33.2 %collective-permute-start.1 = (bf16[2,2,128,256]{2,3,1,0:T(8,128)(2,1)}, bf16[2,2,128,256]{2,3,1,0:T(8,128)(2,1)S(1)}, u32[]{:S(2)}, u32[]{:S(2)}) collective-permute-start(bf16[2,2,128,256]{2,3,1,0:T(8,128)(2,1)} %get-tuple-element.1425), channel_id=1, source_target_pairs={{8,0},{12,4},{16,8},{20,12},{24,16},{28,20},{32,24},{36,28},{40,32... | collective-permute-start | bytes 786440 | tf_op jit(solution)/shard_map/while/body/eval_jaxpr/ppermute | solution.py:25
  1350.8 31.9 %collective-permute-start.2 = (f32[2,2,128]{2,1,0:T(2,128)S(1)}, f32[2,2,128]{2,1,0:T(2,128)S(1)}, u32[]{:S(2)}, u32[]{:S(2)}) collective-permute-start(f32[2,2,128]{2,1,0:T(2,128)S(1)} %get-tuple-element.1426), channel_id=1, source_target_pairs={{8,0},{12,4},{16,8},{20,12},{24,16},{28,20},{32,24},{36,28},{40,32... | collective-permute-start | bytes 6152 | tf_op jit(solution)/shard_map/while/body/eval_jaxpr/ppermute | solution.py:25
  1352.1 30.6 %collective-permute-start.3 = (f32[2,2,128]{2,1,0:T(2,128)S(1)}, f32[2,2,128]{2,1,0:T(2,128)S(1)}, u32[]{:S(2)}, u32[]{:S(2)}) collective-permute-start(f32[2,2,128]{2,1,0:T(2,128)S(1)} %get-tuple-element.1427), channel_id=1, source_target_pairs={{8,0},{12,4},{16,8},{20,12},{24,16},{28,20},{32,24},{36,28},{40,32... | collective-permute-start | bytes 6152 | tf_op jit(solution)/shard_map/while/body/eval_jaxpr/ppermute | solution.py:25
  1408.8 49.3 %collective-permute-start.1 = (bf16[2,2,128,256]{2,3,1,0:T(8,128)(2,1)}, bf16[2,2,128,256]{2,3,1,0:T(8,128)(2,1)S(1)}, u32[]{:S(2)}, u32[]{:S(2)}) collective-permute-start(bf16[2,2,128,256]{2,3,1,0:T(8,128)(2,1)} %get-tuple-element.1425), channel_id=1, source_target_pairs={{8,0},{12,4},{16,8},{20,12},{24,16},{28,20},{32,24},{36,28},{40,32... | collective-permute-start | bytes 786440 | tf_op jit(solution)/shard_map/while/body/eval_jaxpr/ppermute | solution.py:25
  1410.1 47.1 %collective-permute-start.2 = (f32[2,2,128]{2,1,0:T(2,128)S(1)}, f32[2,2,128]{2,1,0:T(2,128)S(1)}, u32[]{:S(2)}, u32[]{:S(2)}) collective-permute-start(f32[2,2,128]{2,1,0:T(2,128)S(1)} %get-tuple-element.1426), channel_id=1, source_target_pairs={{8,0},{12,4},{16,8},{20,12},{24,16},{28,20},{32,24},{36,28},{40,32... | collective-permute-start | bytes 6152 | tf_op jit(solution)/shard_map/while/body/eval_jaxpr/ppermute | solution.py:25
  1411.4 46.7 %collective-permute-start.3 = (f32[2,2,128]{2,1,0:T(2,128)S(1)}, f32[2,2,128]{2,1,0:T(2,128)S(1)}, u32[]{:S(2)}, u32[]{:S(2)}) collective-permute-start(f32[2,2,128]{2,1,0:T(2,128)S(1)} %get-tuple-element.1427), channel_id=1, source_target_pairs={{8,0},{12,4},{16,8},{20,12},{24,16},{28,20},{32,24},{36,28},{40,32... | collective-permute-start | bytes 6152 | tf_op jit(solution)/shard_map/while/body/eval_jaxpr/ppermute | solution.py:25
  1462.8 28.6 %collective-permute-start.1 = (bf16[2,2,128,256]{2,3,1,0:T(8,128)(2,1)}, bf16[2,2,128,256]{2,3,1,0:T(8,128)(2,1)S(1)}, u32[]{:S(2)}, u32[]{:S(2)}) collective-permute-start(bf16[2,2,128,256]{2,3,1,0:T(8,128)(2,1)} %get-tuple-element.1425), channel_id=1, source_target_pairs={{8,0},{12,4},{16,8},{20,12},{24,16},{28,20},{32,24},{36,28},{40,32... | collective-permute-start | bytes 786440 | tf_op jit(solution)/shard_map/while/body/eval_jaxpr/ppermute | solution.py:25
  1464.1 26.4 %collective-permute-start.2 = (f32[2,2,128]{2,1,0:T(2,128)S(1)}, f32[2,2,128]{2,1,0:T(2,128)S(1)}, u32[]{:S(2)}, u32[]{:S(2)}) collective-permute-start(f32[2,2,128]{2,1,0:T(2,128)S(1)} %get-tuple-element.1426), channel_id=1, source_target_pairs={{8,0},{12,4},{16,8},{20,12},{24,16},{28,20},{32,24},{36,28},{40,32... | collective-permute-start | bytes 6152 | tf_op jit(solution)/shard_map/while/body/eval_jaxpr/ppermute | solution.py:25
  1465.4 26.0 %collective-permute-start.3 = (f32[2,2,128]{2,1,0:T(2,128)S(1)}, f32[2,2,128]{2,1,0:T(2,128)S(1)}, u32[]{:S(2)}, u32[]{:S(2)}) collective-permute-start(f32[2,2,128]{2,1,0:T(2,128)S(1)} %get-tuple-element.1427), channel_id=1, source_target_pairs={{8,0},{12,4},{16,8},{20,12},{24,16},{28,20},{32,24},{36,28},{40,32... | collective-permute-start | bytes 6152 | tf_op jit(solution)/shard_map/while/body/eval_jaxpr/ppermute | solution.py:25
  1532.6 413.6 %reduce-scatter.7.cloned.1.call-start = ((), (), s32[]{:S(2)}) async-start(), calls=%async_computation.4 | async-start | bytes 8519680
  (105 other events, 5331.8 us)
Sparse Core Ops, SparseCore 0:
  9.8 25.9 all-gather.1
  1532.7 82.5 reduce-scatter.4
  1618.5 327.6 reduce-scatter.6
where the time goes:
time: 1970 us; the launch traced here: 1950 us
  waiting for transfers between devices  1320 us (67%)
  starting transfers between devices  394 us (20%)
  matrix products  117 us (6%)
  local copies, waits for them, and re-layouts  83.8 us (4%)
    ppermute x124, waiting for transfers between devices, passed_along(): return lax.ppermute(block, axis, route)  877 us
    ppermute x124, starting transfers between devices, passed_along(): return lax.ppermute(block, axis, route)  393 us
    unnamed x4, waiting for transfers between devices  332 us
    reduce_scatter x1, waiting for transfers between devices, per_device(): lax.psum_scatter(partial_value.astype(jnp.bfloat16), 'fsdp', scatter_dime...  68.2 us
    dot_general x128, matrix products, grad_pair(): jnp.einsum('hij,ihd->jhd', dscore, head_view(q_blk), preferred_element_ty...  51 us
  transfers between devices with their start and end apart: 129, of which 88 were waited for; matrix products, arithmetic and copies ran while one was open for 1% of the time, Pallas kernels for 0%

commit v1 on v0

v1 whole, which is shorter than its diff:
```python
import functools

import jax
import jax.numpy as jnp
from jax import lax
from jax.experimental import pallas as pl
from jax.experimental.pallas import tpu as pltpu
from jax.sharding import PartitionSpec as P

HEAD = 128
BLK = 128
SPAN = 4 * BLK
PIECE = BLK + 16
SCALE = HEAD ** -0.5
LOG2E = 1.4426950408889634
NEG_BIG = -1e30
F32 = jnp.float32
BF16 = jnp.bfloat16
VMEM_LIMIT = 48 * 1024 * 1024

NT = (((1,), (1,)), ((), ()))


def mm(lhs, rhs):
    return jnp.dot(lhs, rhs, preferred_element_type=F32)


def mm_nt(lhs, rhs):
    return lax.dot_general(lhs, rhs, NT, preferred_element_type=F32)


def spot(p, u, r):
    return 16 * p + 4 * u + r


def query_groups():
    return [
        [spot(p, a ^ (2 * (p & 1)), r) for p in range(4) for r in range(4)] for a in range(4)
    ]


def key_groups():
    return [[spot(p, u, r) for p in range(4) for u in range(4)] for r in range(4)]


def exchange(pieces, groups):
    return lax.all_to_all(pieces, "ctx", 0, 0, axis_index_groups=groups, tiled=True)


def fwd_kernel(place_ref, q_ref, kv_ref, o_ref, lse_ref, vt_ref, m_ref, l_ref, acc_ref):
    r_key = place_ref[4]
    for j in range(16):
        vt_ref[:, j * BLK : (j + 1) * BLK] = kv_ref[j, BLK:, :].T
    gap = lax.broadcasted_iota(jnp.int32, (BLK, SPAN), 1) - lax.broadcasted_iota(
        jnp.int32, (BLK, SPAN), 0
    )
    allowed = gap >= r_key * BLK

    def span(p, _):
        q = q_ref[pl.ds(4 * p, 4)].reshape(SPAN, HEAD)
        m_ref[...] = jnp.full((1, SPAN), NEG_BIG, F32)
        l_ref[...] = jnp.zeros((1, SPAN), F32)
        acc_ref[...] = jnp.zeros((HEAD, SPAN), F32)

        def chunk(j, count, masked):
            k = kv_ref[pl.ds(j, count), :BLK, :].reshape(count * BLK, HEAD)
            s = mm_nt(k, q) * (SCALE * LOG2E)
            if masked:
                s = jnp.where(allowed, s, NEG_BIG)
            m_old = m_ref[...]
            m_new = jnp.maximum(m_old, jnp.max(s, axis=0, keepdims=True))
            w = jnp.exp2(s - m_new)
            if masked:
                w = jnp.where(allowed, w, 0.0)
            alpha = jnp.exp2(m_old - m_new)
            m_ref[...] = m_new
            l_ref[...] = l_ref[...] * alpha + jnp.sum(w, axis=0, keepdims=True)
            cols = pl.ds(pl.multiple_of(j * BLK, BLK), count * BLK)
            acc_ref[...] = acc_ref[...] * alpha + mm(vt_ref[:, cols], w.astype(BF16))

        @pl.loop(0, p)
        def _(i):
            chunk(4 * i, 4, False)

        last = place_ref[p]

        @pl.loop(0, last)
        def _(i):
            chunk(4 * p + i, 1, False)

        chunk(4 * p + last, 1, True)

        total = l_ref[...]
        some = total > 0.0
        safe = jnp.where(some, total, 1.0)
        lse = jnp.where(some, m_ref[...] + jnp.log2(safe), NEG_BIG)
        out = acc_ref[...] * jnp.where(some, 1.0 / safe, 0.0)
        lse_ref[:, pl.ds(pl.multiple_of(p * SPAN, SPAN), SPAN)] = lse
        high = lse.astype(BF16)
        rest = lse - high.astype(F32)
        mid = rest.astype(BF16)
        low = (rest - mid.astype(F32)).astype(BF16)
        row = lax.broadcasted_iota(jnp.int32, (16, BLK), 0)
        for r in range(4):
            at = slice(r * BLK, (r + 1) * BLK)
            o_ref[4 * p + r, :BLK, :] = out[:, at].T.astype(BF16)
            three = jnp.where(
                row == 0,
                high[:, at].astype(F32),
                jnp.where(
                    row == 1,
                    mid[:, at].astype(F32),
                    jnp.where(row == 2, low[:, at].astype(F32), 0.0),
                ),
            )
            o_ref[4 * p + r, BLK:, :] = three.astype(BF16)
        return 0

    lax.fori_loop(0, 4, span, 0)


def delta_kernel(do_ref, o_ref, lse_ref, out_ref):
    out_ref[0:1, :] = lse_ref[...]
    for j in range(16):
        prod = do_ref[j].astype(F32) * o_ref[j, :BLK, :].astype(F32)
        out_ref[1:2, j * BLK : (j + 1) * BLK] = jnp.sum(prod.T, axis=0, keepdims=True)


def bwd_kernel(
    place_ref, q_ref, kv_ref, do_ref, st0, st1, st2, st3, dq_ref, dkv_ref, kt_ref, lse_ref, delta_ref,
    dqt_ref, dk_ref, dv_ref
):
    r_key = place_ref[4]
    stats = [st[...] for st in (st0, st1, st2, st3)]
    top = functools.reduce(jnp.maximum, [st[0:1] for st in stats])
    lse = top + jnp.log2(sum(jnp.exp2(st[0:1] - top) for st in stats))
    lse_ref[...] = lse
    delta_ref[...] = sum(jnp.exp2(st[0:1] - lse) * st[1:2] for st in stats)
    for j in range(16):
        kt_ref[:, j * BLK : (j + 1) * BLK] = kv_ref[j, :BLK, :].T
    dk_ref[...] = jnp.zeros_like(dk_ref)
    dv_ref[...] = jnp.zeros_like(dv_ref)
    gap = lax.broadcasted_iota(jnp.int32, (BLK, SPAN), 1) - lax.broadcasted_iota(
        jnp.int32, (BLK, SPAN), 0
    )
    allowed = gap >= r_key * BLK

    def span(p, _):
        q = q_ref[pl.ds(4 * p, 4)].reshape(SPAN, HEAD)
        do = do_ref[pl.ds(4 * p, 4)].reshape(SPAN, HEAD)
        here = pl.ds(pl.multiple_of(p * SPAN, SPAN), SPAN)
        lse_now = lse_ref[:, here]
        delta_now = delta_ref[:, here]
        dqt_ref[...] = jnp.zeros((HEAD, SPAN), F32)

        def chunk(j, count, masked):
            k = kv_ref[pl.ds(j, count), :BLK, :].reshape(count * BLK, HEAD)
            v = kv_ref[pl.ds(j, count), BLK:, :].reshape(count * BLK, HEAD)
            w = jnp.exp2(mm_nt(k, q) * (SCALE * LOG2E) - lse_now)
            if masked:
                w = jnp.where(allowed, w, 0.0)
            ds = (w * (mm_nt(v, do) - delta_now)).astype(BF16)
            rows = pl.ds(pl.multiple_of(j * BLK, BLK), count * BLK)
            dv_ref[rows, :] += mm(w.astype(BF16), do)
            dk_ref[rows, :] += mm(ds, q)
            dqt_ref[...] += mm(kt_ref[:, rows], ds)

        @pl.loop(0, p)
        def _(i):
            chunk(4 * i, 4, False)

        last = place_ref[p]

        @pl.loop(0, last)
        def _(i):
            chunk(4 * p + i, 1, False)

        chunk(4 * p + last, 1, True)
        for r in range(4):
            part = dqt_ref[:, r * BLK : (r + 1) * BLK] * SCALE
            dq_ref[4 * p + r] = part.T.astype(BF16)
        return 0

    lax.fori_loop(0, 4, span, 0)
    for j in range(16):
        at = slice(j * BLK, (j + 1) * BLK)
        dkv_ref[j, :BLK, :] = (dk_ref[at, :] * SCALE).astype(BF16)
        dkv_ref[j, BLK:, :] = dv_ref[at, :].astype(BF16)


def in_vmem(count):
    return [pl.BlockSpec(memory_space=pltpu.VMEM)] * count


def on_device(kernel, out_shape, scratch, smem, flops, moved):
    def call(*args):
        specs = [pl.BlockSpec(memory_space=pltpu.SMEM)] * smem + in_vmem(len(args) - smem)
        return pl.pallas_call(
            kernel,
            out_shape=out_shape,
            in_specs=specs,
            out_specs=jax.tree.map(lambda _: pl.BlockSpec(memory_space=pltpu.VMEM), out_shape),
            scratch_shapes=scratch,
            compiler_params=pltpu.CompilerParams(vmem_limit_bytes=VMEM_LIMIT),
            cost_estimate=pl.CostEstimate(flops=flops, bytes_accessed=moved, transcendentals=0),
        )(*args)

    return call


def per_device(query_rows, key_rows, value_rows, out_proj, cotangent):
    me = lax.axis_index("ctx")
    my_p, my_u, my_r = me // 16, (me // 4) % 4, me % 4
    spans = jnp.arange(4)
    last = my_u ^ (2 * ((spans ^ my_p) & 1))
    place = jnp.concatenate([last, my_r[None], jnp.zeros((3,), last.dtype)]).astype(jnp.int32)
    by_query, by_key = query_groups(), key_groups()

    def to_heads(rows):
        return rows.reshape(BLK, 4, HEAD).transpose(1, 0, 2)

    def four_times(per_head):
        shape = per_head.shape
        return jnp.broadcast_to(per_head[:, None], (4, 4) + shape[1:]).reshape((16,) + shape[1:])

    full_cot = lax.all_gather(cotangent, "fsdp", axis=1, tiled=True)
    kv = exchange(
        four_times(jnp.concatenate([to_heads(key_rows), to_heads(value_rows)], axis=1)), by_key
    )
    q = exchange(four_times(to_heads(query_rows)), by_query)

    tokens = 16 * BLK
    o_part, lse_part = on_device(
        fwd_kernel,
        (
            jax.ShapeDtypeStruct((16, PIECE, HEAD), BF16),
            jax.ShapeDtypeStruct((1, tokens), F32),
        ),
        [
            pltpu.VMEM((HEAD, tokens), BF16),
            pltpu.VMEM((1, SPAN), F32),
            pltpu.VMEM((1, SPAN), F32),
            pltpu.VMEM((HEAD, SPAN), F32),
        ],
        1,
        1_200_000_000,
        2_600_000,
    )(place, q, kv)

    o_home = exchange(o_part, by_query)
    rest = o_home[:, BLK : BLK + 3, :].astype(F32)
    totals = (rest[:, 0] + rest[:, 1] + rest[:, 2]).reshape(4, 4, BLK)
    top = jnp.max(totals, axis=1, keepdims=True)
    powers = jnp.exp2(totals - top)
    shares = powers / jnp.sum(powers, axis=1, keepdims=True)
    attended = jnp.sum(
        o_home[:, :BLK, :].astype(F32).reshape(4, 4, BLK, HEAD) * shares[..., None], axis=1
    )
    attended = attended.transpose(1, 0, 2).reshape(BLK, 4 * HEAD).astype(BF16)

    grad_attn = mm_nt(full_cot, out_proj).astype(BF16)
    do = exchange(four_times(to_heads(grad_attn)), by_query)
    stats = on_device(
        delta_kernel, jax.ShapeDtypeStruct((2, tokens), F32), [], 0, 1_000_000, 1_100_000
    )(do, o_part, lse_part)
    others = [lax.ppermute(stats, "ctx", [(i, i ^ b) for i in range(64)]) for b in (1, 2, 3)]

    dq_part, dkv_part = on_device(
        bwd_kernel,
        (
            jax.ShapeDtypeStruct((16, BLK, HEAD), BF16),
            jax.ShapeDtypeStruct((16, 2 * BLK, HEAD), BF16),
        ),
        [
            pltpu.VMEM((HEAD, tokens), BF16),
            pltpu.VMEM((1, tokens), F32),
            pltpu.VMEM((1, tokens), F32),
            pltpu.VMEM((HEAD, SPAN), F32),
            pltpu.VMEM((tokens, HEAD), F32),
            pltpu.VMEM((tokens, HEAD), F32),
        ],
        1,
        3_000_000_000,
        3_600_000,
    )(place, q, kv, do, stats, *others)
    dq_home = exchange(dq_part, by_query)
    dkv_home = exchange(dkv_part, by_key)

    def gathered(parts):
        summed = jnp.sum(parts.astype(F32).reshape(4, 4, BLK, HEAD), axis=1)
        return summed.transpose(1, 0, 2).reshape(BLK, 4 * HEAD).astype(BF16)

    grad_query = gathered(dq_home)
    grad_key = gathered(dkv_home[:, :BLK])
    grad_value = gathered(dkv_home[:, BLK:])

    partial = mm(attended, out_proj).astype(BF16)
    layer_out = lax.psum_scatter(partial, "fsdp", scatter_dimension=1, tiled=True)

    along = [[8 * i + z for i in range(8)] for z in range(8)]
    across = [[8 * i + z for z in range(8)] for i in range(8)]
    cot_cols = exchange(full_cot.reshape(BLK, 8, 512).transpose(1, 0, 2), along)
    att_rows = exchange(jnp.broadcast_to(attended[None], (8, BLK, 512)), along)
    proj_part = lax.dot_general(
        cot_cols.reshape(8 * BLK, 512),
        att_rows.reshape(8 * BLK, 512),
        (((0,), (0,)), ((), ())),
        preferred_element_type=F32,
    ).astype(BF16)
    proj_home = exchange(proj_part.reshape(8, 64, 512), across)
    proj_grad = jnp.sum(proj_home.astype(F32), axis=0)
    return (layer_out, grad_query, grad_key, grad_value, proj_grad)


def solution(mesh):
    spec = P("ctx", "fsdp")
    return jax.shard_map(
        per_device,
        mesh=mesh,
        in_specs=(spec, spec, spec, P("fsdp", None), spec),
        out_specs=(spec, spec, spec, spec, spec),
        check_vma=False,
    )
```

time: 1970 us -> 251 us (0.13)
  waiting for transfers between devices: 1320 us -> 113 us
  starting transfers between devices: 394 us -> 58.6 us
  matrix products: 117 us -> 10.4 us
  local copies, waits for them, and re-layouts: 83.8 us -> 11.3 us
  Pallas kernels: 0 us -> 21.7 us
    ppermute x126 -> x3, waiting for transfers between devices: 891 us -> 10.3 us  [per_device(): lax.ppermute(stats, 'ctx', [(i, i ^ b) for i in range(64)])]
    ppermute x126 -> x3, starting transfers between devices: 394 us -> 3.58 us  [per_device(): lax.ppermute(stats, 'ctx', [(i, i ^ b) for i in range(64)])]
    unnamed x4 -> x2, waiting for transfers between devices: 332 us -> 0.7 us
    dot_general x399 -> x3, matrix products: 117 us -> 10.4 us  [the longest x1 3.93 us: mm(): return jnp.dot(lhs, rhs, preferred_element_type=F32)]
    all_to_all x0 -> x8, waiting for transfers between devices: none -> 71.3 us  [exchange(): lax.all_to_all(pieces, 'ctx', 0, 0, axis_index_groups=groups, tiled=True)]
    reduce_scatter x1, waiting for transfers between devices: 68.2 us -> 0.01 us  [per_device(): lax.psum_scatter(partial, 'fsdp', scatter_dimension=1, tiled=True)]
    all_to_all x0 -> x8, starting transfers between devices: none -> 54.9 us  [exchange(): lax.all_to_all(pieces, 'ctx', 0, 0, axis_index_groups=groups, tiled=True)]
    while x135 -> x0, local copies, waits for them, and re-layouts: 25.4 us -> none
  transfers between devices with their start and end apart: 129 -> 13, of which waited for: 88 -> 10; matrix products, arithmetic and copies ran while one was open for 1% -> 8% of each run, Pallas kernels for 0% -> 9%
where the time goes in v1:
time: 251 us; the launch traced here: 248 us
  waiting for transfers between devices  113 us (45%)
  starting transfers between devices  58.6 us (23%)
  Pallas kernels  21.7 us (9%)
  blocking collectives  17.3 us (7%)
  between operations  14.2 us (6%)
  local copies, waits for them, and re-layouts  11.3 us (5%)
  matrix products  10.4 us (4%)
    all_to_all x8, waiting for transfers between devices, exchange(): lax.all_to_all(pieces, 'ctx', 0, 0, axis_index_groups=groups, tiled=True)  71.3 us
    all_to_all x8, starting transfers between devices, exchange(): lax.all_to_all(pieces, 'ctx', 0, 0, axis_index_groups=groups, tiled=True)  54.9 us
    all_gather x1, waiting for transfers between devices, per_device(): full_cot = lax.all_gather(cotangent, 'fsdp', axis=1, tiled=True)  30.3 us
    pallas_call x3, Pallas kernels, call(): pl.pallas_call(kernel, out_shape=out_shape, in_specs=specs, out_specs=jax...  21.7 us
    all_to_all x1, blocking collectives, exchange(): lax.all_to_all(pieces, 'ctx', 0, 0, axis_index_groups=groups, tiled=True)  17.3 us
    ppermute x3, waiting for transfers between devices, per_device(): lax.ppermute(stats, 'ctx', [(i, i ^ b) for i in range(64)])  10.3 us
  transfers between devices with their start and end apart: 13, of which 10 were waited for; matrix products, arithmetic and copies ran while one was open for 8% of the time, Pallas kernels for 9%

profile of v1, /device:TPU:32, one launch (start us, length us, event | category | flops | bytes accessed | tf_op | source)
XLA Modules:
  0.0 247.7 jit_solution(17410225993951546919)
XLA Ops:
  7.2 0.9 reshape.109
  9.0 9.4 %all-to-all-start = ((bf16[16,128,128]{2,1,0:T(8,128)(2,1)}), bf16[16,128,128]{2,1,0:T(8,128)(2,1)S(1)}, u32[]{:S(2)}, u32[]{:S(2)}) async-start(bf16[16,128,128]{2,1,0:T(8,128)(2,1)} %bitcast.2), calls=%async_computation | async-start | bytes 1048576 | tf_op jit(solution)/shard_map/all_to_all | solution.py:47
  18.4 0.9 reshape.112
  19.4 0.9 reshape.111
  20.5 12.5 %all-to-all-done.q_ref = bf16[16,128,128]{2,1,0:T(8,128)(2,1)S(1)} async-done(((bf16[16,128,128]{2,1,0:T(8,128)(2,1)}), bf16[16,128,128]{2,1,0:T(8,128)(2,1)S(1)}, u32[]{:S(2)}, u32[]{:S(2)}) %all-to-all-start) | async-done | bytes 524320 | tf_op jit(solution)/shard_map/all_to_all | solution.py:47
  33.0 1.2 broadcast_in_dim.12
  34.2 7.0 %all-to-all-start.1 = ((bf16[16,256,128]{2,1,0:T(8,128)(2,1)}), bf16[16,256,128]{2,1,0:T(8,128)(2,1)S(1)}, u32[]{:S(2)}, u32[]{:S(2)}) async-start(bf16[16,256,128]{2,1,0:T(8,128)(2,1)} %bitcast.5), calls=%async_computation.1 | async-start | bytes 2097152 | tf_op jit(solution)/shard_map/all_to_all | solution.py:47
  41.9 30.3 %all-gather.2.cloned.1.call-done = bf16[128,4096]{1,0:T(8,128)(2,1)} async-done(((bf16[128,1024]{1,0:T(8,128)(2,1)}), bf16[128,4096]{1,0:T(8,128)(2,1)}) %all-gather.2.cloned.1.call-update) | async-done | bytes 1048592 | tf_op jit(solution)/shard_map/all_gather | solution.py:226
  72.2 2.4 copy.26
  74.6 4.2 %all-to-all-start.7 = ((bf16[8,128,512]{1,2,0:T(8,128)(2,1)}), bf16[8,128,512]{1,2,0:T(8,128)(2,1)}, u32[]{:S(2)}, u32[]{:S(2)}) async-start(bf16[8,128,512]{1,2,0:T(8,128)(2,1)} %bitcast.22), calls=%async_computation.8 | async-start | bytes 2097152 | tf_op jit(solution)/shard_map/all_to_all | solution.py:47
  78.9 3.7 %convolution_convert_fusion.1 = bf16[128,512]{1,0:T(8,128)(2,1)S(1)} fusion(bf16[128,4096]{1,0:T(8,128)(2,1)S(1)} %copy-done, bf16[512,4096]{1,0:T(8,128)(2,1)} %param.8), kind=kOutput, calls=%fused_computation.4 | convolution fusion | flops 536936448 | bytes 5373952 | tf_op jit(solution)/shard_map/dot_general | solution.py:29
  82.7 11.7 %all-to-all-done.7 = bf16[8,128,512]{1,2,0:T(8,128)(2,1)} async-done(((bf16[8,128,512]{1,2,0:T(8,128)(2,1)}), bf16[8,128,512]{1,2,0:T(8,128)(2,1)}, u32[]{:S(2)}, u32[]{:S(2)}) %all-to-all-start.7) | async-done | bytes 1048608 | tf_op jit(solution)/shard_map/all_to_all | solution.py:47
  94.3 0.9 broadcast_in_dim.13
  95.2 6.3 %all-to-all-start.3 = ((bf16[16,128,128]{2,1,0:T(8,128)(2,1)}), bf16[16,128,128]{2,1,0:T(8,128)(2,1)S(1)}, u32[]{:S(2)}, u32[]{:S(2)}) async-start(bf16[16,128,128]{2,1,0:T(8,128)(2,1)} %bitcast.11), calls=%async_computation.4 | async-start | bytes 1048576 | tf_op jit(solution)/shard_map/all_to_all | solution.py:47
  101.6 9.5 %shard_map.92 = (bf16[16,144,128]{2,1,0:T(8,128)(2,1)}, f32[1,2048]{1,0:T(1,128)S(1)}) custom-call(s32[8]{0:T(128)S(1)} %pad_add_fusion.place_ref, bf16[16,128,128]{2,1,0:T(8,128)(2,1)S(1)} %all-to-all-done.q_ref, bf16[16,256,128]{2,1,0:T(8,128)(2,1)S(1)} %all-to-all-done.1.kv_ref), custom_call_target="tpu_custom_call" | custom-call | flops 1200000000 | bytes 2600000 | tf_op jit(solution)/shard_map/pallas_call | solution.py:198
  111.2 5.2 %all-to-all-done.3.do_ref = bf16[16,128,128]{2,1,0:T(8,128)(2,1)S(1)} async-done(((bf16[16,128,128]{2,1,0:T(8,128)(2,1)}), bf16[16,128,128]{2,1,0:T(8,128)(2,1)S(1)}, u32[]{:S(2)}, u32[]{:S(2)}) %all-to-all-start.3) | async-done | bytes 524320 | tf_op jit(solution)/shard_map/all_to_all | solution.py:47
  116.3 6.3 %all-to-all-start.2 = ((bf16[16,144,128]{2,1,0:T(8,128)(2,1)}), bf16[16,144,128]{2,1,0:T(8,128)(2,1)S(1)}, u32[]{:S(2)}, u32[]{:S(2)}) async-start(bf16[16,144,128]{2,1,0:T(8,128)(2,1)} %get-tuple-element.9.o_ref), calls=%async_computation.2 | async-start | bytes 1179648 | tf_op jit(solution)/shard_map/all_to_all | solution.py:47
  122.6 1.4 shard_map.93.st0
  124.4 2.7 %collective-permute-start.1 = (f32[2,2048]{1,0:T(2,128)S(1)}, f32[2,2048]{1,0:T(2,128)S(1)}, u32[]{:S(2)}, u32[]{:S(2)}) collective-permute-start(f32[2,2048]{1,0:T(2,128)S(1)} %shard_map.93.st0), channel_id=1, source_target_pairs={{0,8},{4,12},{8,0},{12,4},{16,24},{20,28},{24,16},{28,20},{32,40},... | collective-permute-start | bytes 49160 | tf_op jit(solution)/shard_map/ppermute | solution.py:266
  127.6 5.3 %collective-permute-done.st1 = f32[2,2048]{1,0:T(2,128)S(1)} collective-permute-done((f32[2,2048]{1,0:T(2,128)S(1)}, f32[2,2048]{1,0:T(2,128)S(1)}, u32[]{:S(2)}, u32[]{:S(2)}) %collective-permute-start) | collective-permute-done | bytes 16416 | tf_op jit(solution)/shard_map/ppermute | solution.py:266
  132.9 2.7 %collective-permute-done.1.st2 = f32[2,2048]{1,0:T(2,128)S(1)} collective-permute-done((f32[2,2048]{1,0:T(2,128)S(1)}, f32[2,2048]{1,0:T(2,128)S(1)}, u32[]{:S(2)}, u32[]{:S(2)}) %collective-permute-start.1) | collective-permute-done | bytes 16416 | tf_op jit(solution)/shard_map/ppermute | solution.py:266
  135.6 2.4 collective-permute-done.2.st3
  138.0 10.7 %shard_map.94 = (bf16[16,128,128]{2,1,0:T(8,128)(2,1)}, bf16[16,256,128]{2,1,0:T(8,128)(2,1)}) custom-call(s32[8]{0:T(128)S(1)} %pad_add_fusion.place_ref, bf16[16,128,128]{2,1,0:T(8,128)(2,1)S(1)} %all-to-all-done.q_ref, bf16[16,256,128]{2,1,0:T(8,128)(2,1)S(1)} %all-to-all-done.1.kv_ref, bf16[16,128,128]{2,1,0:T(8,128)(2,1)S(1)} %all-to-all-done.3.do_ref, ...), custom_call_target="tpu_custom_call" | custom-call | flops 3000000000 | bytes 3600000 | tf_op jit(solution)/shard_map/pallas_call | solution.py:198
  148.7 7.1 %all-to-all-start.4 = ((bf16[16,128,128]{2,1,0:T(8,128)(2,1)}), bf16[16,128,128]{2,1,0:T(8,128)(2,1)S(1)}, u32[]{:S(2)}, u32[]{:S(2)}) async-start(bf16[16,128,128]{2,1,0:T(8,128)(2,1)} %get-tuple-element.11), calls=%async_computation.5 | async-start | bytes 1048576 | tf_op jit(solution)/shard_map/all_to_all | solution.py:47
  156.4 13.5 %all-to-all-done.4 = bf16[16,128,128]{2,1,0:T(8,128)(2,1)S(1)} async-done(((bf16[16,128,128]{2,1,0:T(8,128)(2,1)}), bf16[16,128,128]{2,1,0:T(8,128)(2,1)S(1)}, u32[]{:S(2)}, u32[]{:S(2)}) %all-to-all-start.4) | async-done | bytes 524320 | tf_op jit(solution)/shard_map/all_to_all | solution.py:47
  170.0 17.3 %all_to_all.45 = bf16[8,128,512]{2,1,0:T(8,128)(2,1)S(1)} all-to-all(bf16[8,128,512]{2,1,0:T(8,128)(2,1)S(1)} %broadcast_in_dim.14), channel_id=1, replica_groups={{0,32,64,96,128,160,192,224},{4,36,68,100,132,164,196,228},{8,40,72,104..., dimensions={0} | all-to-all | bytes 2097152 | tf_op jit(solution)/shard_map/all_to_all | solution.py:47
  187.4 7.4 %all-to-all-start.5 = ((bf16[16,256,128]{2,1,0:T(8,128)(2,1)}), bf16[16,256,128]{2,1,0:T(8,128)(2,1)S(1)}, u32[]{:S(2)}, u32[]{:S(2)}) async-start(bf16[16,256,128]{2,1,0:T(8,128)(2,1)} %get-tuple-element.12), calls=%async_computation.6 | async-start | bytes 2097152 | tf_op jit(solution)/shard_map/all_to_all | solution.py:47
  194.8 3.9 %convolution_convert_fusion = bf16[128,4096]{1,0:T(8,128)(2,1)} fusion(bf16[128,512]{0,1:T(8,128)(2,1)S(1)} %bitcast.46, bf16[512,4096]{1,0:T(8,128)(2,1)} %param.8), kind=kOutput, calls=%fused_computation.1 | convolution fusion | flops 537395200 | bytes 5373952 | tf_op jit(solution)/shard_map/dot_general | solution.py:25
  198.7 2.7 %fusion.1 = bf16[512,512]{0,1:T(8,128)(2,1)} fusion(bf16[8,128,512]{1,2,0:T(8,128)(2,1)} %all-to-all-done.7, bf16[8,128,512]{2,1,0:T(8,128)(2,1)S(1)} %all_to_all.45), kind=kOutput, calls=%fused_computation.3 | convolution fusion | flops 537133056 | bytes 2621440 | tf_op jit(solution)/shard_map/dot_general | solution.py:304
  201.5 20.2 %all-to-all-done.5 = bf16[16,256,128]{2,1,0:T(8,128)(2,1)S(1)} async-done(((bf16[16,256,128]{2,1,0:T(8,128)(2,1)}), bf16[16,256,128]{2,1,0:T(8,128)(2,1)S(1)}, u32[]{:S(2)}, u32[]{:S(2)}) %all-to-all-start.5) | async-done | bytes 1048608 | tf_op jit(solution)/shard_map/all_to_all | solution.py:47
  221.7 7.3 %all-to-all-start.8 = ((bf16[8,64,512]{2,1,0:T(8,128)(2,1)}), bf16[8,64,512]{2,1,0:T(8,128)(2,1)S(1)}, u32[]{:S(2)}, u32[]{:S(2)}) async-start(bf16[8,64,512]{2,1,0:T(8,128)(2,1)} %bitcast.25), calls=%async_computation.9 | async-start | bytes 1048576 | tf_op jit(solution)/shard_map/all_to_all | solution.py:47
  231.9 8.2 %all-to-all-done.8 = bf16[8,64,512]{2,1,0:T(8,128)(2,1)S(1)} async-done(((bf16[8,64,512]{2,1,0:T(8,128)(2,1)}), bf16[8,64,512]{2,1,0:T(8,128)(2,1)S(1)}, u32[]{:S(2)}, u32[]{:S(2)}) %all-to-all-start.8) | async-done | bytes 524320 | tf_op jit(solution)/shard_map/all_to_all | solution.py:47
  (36 shorter events, 7.3 us)
Async XLA Ops:
  9.0 24.0 %all-to-all-start = ((bf16[16,128,128]{2,1,0:T(8,128)(2,1)}), bf16[16,128,128]{2,1,0:T(8,128)(2,1)S(1)}, u32[]{:S(2)}, u32[]{:S(2)}) async-start(bf16[16,128,128]{2,1,0:T(8,128)(2,1)} %bitcast.2), calls=%async_computation | async-start | bytes 1048576 | tf_op jit(solution)/shard_map/all_to_all | solution.py:47
  34.2 40.4 %all-to-all-start.1 = ((bf16[16,256,128]{2,1,0:T(8,128)(2,1)}), bf16[16,256,128]{2,1,0:T(8,128)(2,1)S(1)}, u32[]{:S(2)}, u32[]{:S(2)}) async-start(bf16[16,256,128]{2,1,0:T(8,128)(2,1)} %bitcast.5), calls=%async_computation.1 | async-start | bytes 2097152 | tf_op jit(solution)/shard_map/all_to_all | solution.py:47
  41.2 31.1 %all-gather.2.cloned.1.call-start = ((), (), s32[]{:S(2)}) async-start(), calls=%async_computation.11 | async-start | bytes 1310720 | tf_op jit(solution)/shard_map/all_gather | solution.py:226
  72.2 6.6 %copy-start = (bf16[128,4096]{1,0:T(8,128)(2,1)S(1)}, bf16[128,4096]{1,0:T(8,128)(2,1)}, u32[]{:S(2)}) copy-start(bf16[128,4096]{1,0:T(8,128)(2,1)} %all-gather.2.cloned.1.call-done) | copy-start | bytes 3145732
  74.6 19.7 %all-to-all-start.7 = ((bf16[8,128,512]{1,2,0:T(8,128)(2,1)}), bf16[8,128,512]{1,2,0:T(8,128)(2,1)}, u32[]{:S(2)}, u32[]{:S(2)}) async-start(bf16[8,128,512]{1,2,0:T(8,128)(2,1)} %bitcast.22), calls=%async_computation.8 | async-start | bytes 2097152 | tf_op jit(solution)/shard_map/all_to_all | solution.py:47
  95.2 21.1 %all-to-all-start.3 = ((bf16[16,128,128]{2,1,0:T(8,128)(2,1)}), bf16[16,128,128]{2,1,0:T(8,128)(2,1)S(1)}, u32[]{:S(2)}, u32[]{:S(2)}) async-start(bf16[16,128,128]{2,1,0:T(8,128)(2,1)} %bitcast.11), calls=%async_computation.4 | async-start | bytes 1048576 | tf_op jit(solution)/shard_map/all_to_all | solution.py:47
  116.3 32.3 %all-to-all-start.2 = ((bf16[16,144,128]{2,1,0:T(8,128)(2,1)}), bf16[16,144,128]{2,1,0:T(8,128)(2,1)S(1)}, u32[]{:S(2)}, u32[]{:S(2)}) async-start(bf16[16,144,128]{2,1,0:T(8,128)(2,1)} %get-tuple-element.9.o_ref), calls=%async_computation.2 | async-start | bytes 1179648 | tf_op jit(solution)/shard_map/all_to_all | solution.py:47
  124.1 8.9 %collective-permute-start = (f32[2,2048]{1,0:T(2,128)S(1)}, f32[2,2048]{1,0:T(2,128)S(1)}, u32[]{:S(2)}, u32[]{:S(2)}) collective-permute-start(f32[2,2048]{1,0:T(2,128)S(1)} %shard_map.93.st0), channel_id=1, source_target_pairs={{0,4},{4,0},{8,12},{12,8},{16,20},{20,16},{24,28},{28,24},{32,36},... | collective-permute-start | bytes 49160 | tf_op jit(solution)/shard_map/ppermute | solution.py:266
  124.4 11.2 %collective-permute-start.1 = (f32[2,2048]{1,0:T(2,128)S(1)}, f32[2,2048]{1,0:T(2,128)S(1)}, u32[]{:S(2)}, u32[]{:S(2)}) collective-permute-start(f32[2,2048]{1,0:T(2,128)S(1)} %shard_map.93.st0), channel_id=1, source_target_pairs={{0,8},{4,12},{8,0},{12,4},{16,24},{20,28},{24,16},{28,20},{32,40},... | collective-permute-start | bytes 49160 | tf_op jit(solution)/shard_map/ppermute | solution.py:266
  127.1 10.9 %collective-permute-start.2 = (f32[2,2048]{1,0:T(2,128)S(1)}, f32[2,2048]{1,0:T(2,128)S(1)}, u32[]{:S(2)}, u32[]{:S(2)}) collective-permute-start(f32[2,2048]{1,0:T(2,128)S(1)} %shard_map.93.st0), channel_id=1, source_target_pairs={{0,12},{4,8},{8,4},{12,0},{16,28},{20,24},{24,20},{28,16},{32,44},... | collective-permute-start | bytes 49160 | tf_op jit(solution)/shard_map/ppermute | solution.py:266
  148.7 21.3 %all-to-all-start.4 = ((bf16[16,128,128]{2,1,0:T(8,128)(2,1)}), bf16[16,128,128]{2,1,0:T(8,128)(2,1)S(1)}, u32[]{:S(2)}, u32[]{:S(2)}) async-start(bf16[16,128,128]{2,1,0:T(8,128)(2,1)} %get-tuple-element.11), calls=%async_computation.5 | async-start | bytes 1048576 | tf_op jit(solution)/shard_map/all_to_all | solution.py:47
  187.4 34.4 %all-to-all-start.5 = ((bf16[16,256,128]{2,1,0:T(8,128)(2,1)}), bf16[16,256,128]{2,1,0:T(8,128)(2,1)S(1)}, u32[]{:S(2)}, u32[]{:S(2)}) async-start(bf16[16,256,128]{2,1,0:T(8,128)(2,1)} %get-tuple-element.12), calls=%async_computation.6 | async-start | bytes 2097152 | tf_op jit(solution)/shard_map/all_to_all | solution.py:47
  194.7 46.1 %reduce-scatter.2.cloned.1.call-start = ((), (), s32[]{:S(2)}) async-start(), calls=%async_computation.10 | async-start | bytes 1310720 | tf_op jit(solution)/shard_map/reduce_scatter | solution.py:298
  221.7 18.4 %all-to-all-start.8 = ((bf16[8,64,512]{2,1,0:T(8,128)(2,1)}), bf16[8,64,512]{2,1,0:T(8,128)(2,1)S(1)}, u32[]{:S(2)}, u32[]{:S(2)}) async-start(bf16[8,64,512]{2,1,0:T(8,128)(2,1)} %bitcast.25), calls=%async_computation.9 | async-start | bytes 1048576 | tf_op jit(solution)/shard_map/all_to_all | solution.py:47
Sparse Core Ops, SparseCore 0:
  43.8 28.3 all-gather.1
  198.9 39.1 reduce-scatter.1

commit v2 on v1

v2 whole, which is shorter than its diff:
```python
import functools

import jax
import jax.numpy as jnp
from jax import lax
from jax.experimental import pallas as pl
from jax.experimental.pallas import tpu as pltpu
from jax.sharding import PartitionSpec as P

HEAD = 128
BLK = 128
SPAN = 4 * BLK
PIECE = BLK + 16
TOKENS = 16 * BLK
SCALE = HEAD ** -0.5
LOG2E = 1.4426950408889634
NEG_BIG = -1e30
F32 = jnp.float32
BF16 = jnp.bfloat16
VMEM_LIMIT = 40 * 1024 * 1024

HEAD_STEP = (0, 24, 32, 56)
ROW_STEP = (0, 2, 4, 6)


def key_groups():
    return [
        [16 * p + 8 * y + 2 * r + z for p in range(4) for y in range(2) for z in range(2)]
        for r in range(4)
    ]


def exchange(pieces, groups):
    return lax.all_to_all(pieces, "ctx", 0, 0, axis_index_groups=groups, tiled=True)


def hop(block, step):
    return lax.ppermute(block, "ctx", [(i, i ^ step) for i in range(64)])


def over_heads(blocks):
    return [blocks[0]] + [hop(blocks[x], HEAD_STEP[x]) for x in (1, 2, 3)]


def over_rows(blocks):
    return [blocks[0]] + [hop(blocks[x], ROW_STEP[x]) for x in (1, 2, 3)]


def cot_hop(block, y):
    route = []
    for c in range(64):
        for f in range(4):
            p = c // 16
            goal = (c % 16) ^ (8 * ((p ^ f) & 1))
            route.append((4 * c + f, 4 * (16 * f + goal) + (p ^ y)))
    return lax.ppermute(block, ("ctx", "fsdp"), route)


def mm(lhs, rhs):
    return jnp.dot(lhs, rhs, preferred_element_type=F32)


def mm_nt(lhs, rhs):
    return lax.dot_general(lhs, rhs, (((1,), (1,)), ((), ())), preferred_element_type=F32)


def block_at(index, size=BLK):
    return pl.ds(pl.multiple_of(index * size, size), size)


def prep_kernel(place, q_ref, k_ref, v_ref, q0, q1, q2, q3, kv_ref):
    p = place[0]
    for x, out in enumerate((q0, q1, q2, q3)):
        out[...] = q_ref[:, block_at(p ^ x)]
    for j in range(16):
        at = slice((j // 4) * HEAD, (j // 4 + 1) * HEAD)
        kv_ref[j, :BLK, :] = k_ref[:, at]
        kv_ref[j, BLK:, :] = v_ref[:, at]


def grad_attn_kernel(place, c0, c1, c2, c3, w_ref, g0, g1, g2, g3, acc_ref):
    step = pl.program_id(0)
    for x, cot in enumerate((c0, c1, c2, c3)):

        @pl.when(step == x)
        def _():
            term = mm_nt(cot[...], w_ref[...])
            acc_ref[...] = term if x == 0 else acc_ref[...] + term

    @pl.when(step == 3)
    def _():
        for x, out in enumerate((g0, g1, g2, g3)):
            out[...] = acc_ref[:, block_at(place[0] ^ x)].astype(BF16)


def sort_rows(place, parts, out_ref):
    for xr, part in enumerate(parts):
        for xp in range(4):
            out_ref[4 * (place[0] ^ xp) + (place[1] ^ xr)] = part[xp]


def causal(place):
    row = lax.broadcasted_iota(jnp.int32, (2 * BLK, SPAN), 0) + 2 * BLK * place[1]
    col = lax.broadcasted_iota(jnp.int32, (2 * BLK, SPAN), 1)
    col = 2 * BLK * (col // BLK) + BLK * place[2] + col % BLK
    return row <= col


def for_chunks(place, p, chunk):
    @pl.loop(0, p)
    def _(i):
        chunk(4 * i, 4, False)

    y = place[4 + p]

    @pl.loop(0, y)
    def _(i):
        chunk(4 * p, 2, False)

    chunk(4 * p + 2 * y, 2, True)


def fwd_kernel(
    place, qa, qb, qc, qd, kv_ref, o0, o1, o2, o3, lse_ref, q_ref, vt_ref, m_ref, l_ref, acc_ref
):
    sort_rows(place, (qa, qb, qc, qd), q_ref)
    for j in range(16):
        vt_ref[:, j * BLK : (j + 1) * BLK] = kv_ref[j, BLK:, :].T
    allowed = causal(place)

    def span(p, _):
        q = q_ref[pl.ds(4 * p, 4)].reshape(SPAN, HEAD)
        m_ref[...] = jnp.full((1, SPAN), NEG_BIG, F32)
        l_ref[...] = jnp.zeros((1, SPAN), F32)
        acc_ref[...] = jnp.zeros((HEAD, SPAN), F32)

        def chunk(j, count, masked):
            k = kv_ref[pl.ds(j, count), :BLK, :].reshape(count * BLK, HEAD)
            s = mm_nt(k, q) * (SCALE * LOG2E)
            if masked:
                s = jnp.where(allowed, s, NEG_BIG)
            m_old = m_ref[...]
            m_new = jnp.maximum(m_old, jnp.max(s, axis=0, keepdims=True))
            w = jnp.exp2(s - m_new)
            if masked:
                w = jnp.where(allowed, w, 0.0)
            alpha = jnp.exp2(m_old - m_new)
            m_ref[...] = m_new
            l_ref[...] = l_ref[...] * alpha + jnp.sum(w, axis=0, keepdims=True)
            cols = pl.ds(pl.multiple_of(j * BLK, BLK), count * BLK)
            acc_ref[...] = acc_ref[...] * alpha + mm(vt_ref[:, cols], w.astype(BF16))

        for_chunks(place, p, chunk)
        total = l_ref[...]
        some = total > 0.0
        safe = jnp.where(some, total, 1.0)
        lse = jnp.where(some, m_ref[...] + jnp.log2(safe), NEG_BIG)
        lse_ref[:, block_at(p, SPAN)] = lse
        acc_ref[...] = acc_ref[...] * jnp.where(some, 1.0 / safe, 0.0)
        row = lax.broadcasted_iota(jnp.int32, (16, BLK), 0)
        for x, out in enumerate((o0, o1, o2, o3)):
            r = place[1] ^ x
            out[p, :BLK, :] = acc_ref[:, block_at(r)].T.astype(BF16)
            total_here = lse_ref[:, block_at(4 * p + r)]
            high = total_here.astype(BF16).astype(F32)
            rest = total_here - high
            mid = rest.astype(BF16).astype(F32)
            three = jnp.where(
                row == 0,
                high,
                jnp.where(row == 1, mid, jnp.where(row == 2, rest - mid, 0.0)),
            )
            out[p, BLK:, :] = three.astype(BF16)
        return 0

    lax.fori_loop(0, 4, span, 0)


def merge_kernel(o0, o1, o2, o3, out_ref):
    parts = (o0, o1, o2, o3)
    for p in range(4):
        sums = []
        for part in parts:
            three = part[p, BLK:, :].astype(F32)
            sums.append(three[0:1] + three[1:2] + three[2:3])
        top = functools.reduce(jnp.maximum, sums)
        powers = [jnp.exp2(s - top) for s in sums]
        whole = sum(powers)
        merged = 0.0
        for part, power in zip(parts, powers):
            share = jnp.broadcast_to(power / whole, (BLK, HEAD)).T
            merged = merged + share * part[p, :BLK, :].astype(F32)
        out_ref[p] = merged.astype(BF16)


def delta_kernel(place, d0, d1, d2, d3, o0, o1, o2, o3, lse_ref, out_ref):
    out_ref[0:1, :] = lse_ref[...]
    for xr, (do, o) in enumerate(zip((d0, d1, d2, d3), (o0, o1, o2, o3))):
        for xp in range(4):
            p, r = place[0] ^ xp, place[1] ^ xr
            prod = do[xp].astype(F32) * o[p, :BLK, :].astype(F32)
            out_ref[1:2, block_at(4 * p + r)] = jnp.sum(prod.T, axis=0, keepdims=True)


def bwd_kernel(
    place, qa, qb, qc, qd, da, db, dc, dd, kv_ref, st0, st1, st2, st3, dq0, dq1, dq2, dq3, dkv_ref,
    q_ref, do_ref, kt_ref, lse_ref, delta_ref, dqt_ref, dk_ref, dv_ref
):
    sort_rows(place, (qa, qb, qc, qd), q_ref)
    sort_rows(place, (da, db, dc, dd), do_ref)
    stats = [st[...] for st in (st0, st1, st2, st3)]
    top = functools.reduce(jnp.maximum, [st[0:1] for st in stats])
    lse = top + jnp.log2(sum(jnp.exp2(st[0:1] - top) for st in stats))
    lse_ref[...] = lse
    delta_ref[...] = sum(jnp.exp2(st[0:1] - lse) * st[1:2] for st in stats)
    for j in range(16):
        kt_ref[:, j * BLK : (j + 1) * BLK] = kv_ref[j, :BLK, :].T
    dk_ref[...] = jnp.zeros_like(dk_ref)
    dv_ref[...] = jnp.zeros_like(dv_ref)
    allowed = causal(place)

    def span(p, _):
        q = q_ref[pl.ds(4 * p, 4)].reshape(SPAN, HEAD)
        do = do_ref[pl.ds(4 * p, 4)].reshape(SPAN, HEAD)
        lse_now = lse_ref[:, block_at(p, SPAN)]
        delta_now = delta_ref[:, block_at(p, SPAN)]
        dqt_ref[...] = jnp.zeros((HEAD, SPAN), F32)

        def chunk(j, count, masked):
            k = kv_ref[pl.ds(j, count), :BLK, :].reshape(count * BLK, HEAD)
            v = kv_ref[pl.ds(j, count), BLK:, :].reshape(count * BLK, HEAD)
            w = jnp.exp2(mm_nt(k, q) * (SCALE * LOG2E) - lse_now)
            if masked:
                w = jnp.where(allowed, w, 0.0)
            ds = (w * (mm_nt(v, do) - delta_now)).astype(BF16)
            rows = pl.ds(pl.multiple_of(j * BLK, BLK), count * BLK)
            dv_ref[rows, :] += mm(w.astype(BF16), do)
            dk_ref[rows, :] += mm(ds, q)
            dqt_ref[...] += mm(kt_ref[:, rows], ds)

        for_chunks(place, p, chunk)
        dqt_ref[...] = dqt_ref[...] * SCALE
        for x, out in enumerate((dq0, dq1, dq2, dq3)):
            out[p] = dqt_ref[:, block_at(place[1] ^ x)].T.astype(BF16)
        return 0

    lax.fori_loop(0, 4, span, 0)
    for j in range(16):
        at = slice(j * BLK, (j + 1) * BLK)
        dkv_ref[j, :BLK, :] = (dk_ref[at, :] * SCALE).astype(BF16)
        dkv_ref[j, BLK:, :] = dv_ref[at, :].astype(BF16)


def dq_sum_kernel(place, d0, d1, d2, d3, e0, e1, e2, e3):
    for x, out in enumerate((e0, e1, e2, e3)):
        p = place[0] ^ x
        out[...] = sum(part[p].astype(F32) for part in (d0, d1, d2, d3)).astype(BF16)


def grads_kernel(place, e0, e1, e2, e3, dkv_ref, dq_ref, dk_ref, dv_ref):
    for x, part in enumerate((e0, e1, e2, e3)):
        dq_ref[:, block_at(place[0] ^ x)] = part[...]
    for h in range(4):
        total = sum(dkv_ref[4 * h + i].astype(F32) for i in range(4)).astype(BF16)
        at = slice(h * HEAD, (h + 1) * HEAD)
        dk_ref[:, at] = total[:BLK]
        dv_ref[:, at] = total[BLK:]


def layer_kernel(place, a0, a1, a2, a3, w_ref, l0, l1, l2, l3, rows_ref):
    step = pl.program_id(0)

    @pl.when(step == 0)
    def _():
        for x, part in enumerate((a0, a1, a2, a3)):
            rows_ref[:, block_at(place[0] ^ x)] = part[place[0]]

    for x, out in enumerate((l0, l1, l2, l3)):

        @pl.when(step == x)
        def _():
            out[...] = mm(rows_ref[...], w_ref[...]).astype(BF16)


def proj_kernel(place, a0, a1, a2, a3, c0, c1, c2, c3, out_ref, att_ref, cot_ref):
    for x, part in enumerate((a0, a1, a2, a3)):
        for p in range(4):
            att_ref[p * BLK : (p + 1) * BLK, block_at(place[0] ^ x)] = part[p]
    for y, part in enumerate((c0, c1, c2, c3)):
        cot_ref[block_at(place[3] ^ y), :] = part[...]
    for i in range(4):
        at = slice(i * 256, (i + 1) * 256)
        total = lax.dot_general(
            cot_ref[:, at], att_ref[...], (((0,), (0,)), ((), ())), preferred_element_type=F32
        )
        out_ref[4 * i : 4 * i + 4] = total.astype(BF16).reshape(4, 64, 512)


def like(*shape, dtype=BF16):
    return jax.ShapeDtypeStruct(shape, dtype)


def params():
    return pltpu.CompilerParams(vmem_limit_bytes=VMEM_LIMIT)


def cost(flops, moved):
    return pl.CostEstimate(flops=int(flops), bytes_accessed=int(moved), transcendentals=0)


def on_device(kernel, out_shape, scratch, flops, moved, placed=True):
    def call(*args):
        specs = [pl.BlockSpec(memory_space=pltpu.VMEM)] * len(args)
        if placed:
            specs[0] = pl.BlockSpec(memory_space=pltpu.SMEM)
        return pl.pallas_call(
            kernel,
            out_shape=out_shape,
            in_specs=specs,
            out_specs=jax.tree.map(lambda _: pl.BlockSpec(memory_space=pltpu.VMEM), out_shape),
            scratch_shapes=scratch,
            compiler_params=params(),
            cost_estimate=cost(flops, moved),
        )(*args)

    return call


def by_columns(kernel, out_shape, scratch, flops):
    def call(place, *args):
        whole = pl.BlockSpec(memory_space=pltpu.VMEM)
        return pl.pallas_call(
            kernel,
            out_shape=out_shape,
            grid_spec=pltpu.PrefetchScalarGridSpec(
                num_scalar_prefetch=1,
                grid=(4,),
                in_specs=[whole] * (len(args) - 1)
                + [pl.BlockSpec((512, 1024), lambda i, at: (0, at[3] ^ i))],
                out_specs=[whole] * len(out_shape),
                scratch_shapes=scratch,
            ),
            compiler_params=params(),
            cost_estimate=cost(flops, 6_000_000),
        )(place, *args)

    return call


def per_device(query_rows, key_rows, value_rows, out_proj, cotangent):
    c, f = lax.axis_index("ctx"), lax.axis_index("fsdp")
    p, y, r, z = c // 16, (c // 8) % 2, (c // 2) % 4, c % 2
    place = jnp.stack([p, r, z, f] + [y ^ ((p ^ i) & 1) for i in range(4)]).astype(jnp.int32)
    four = [like(BLK, HEAD)] * 4
    stacks = [like(4, BLK, HEAD)] * 4

    cots = [cotangent] + [
        lax.ppermute(cotangent, "fsdp", [(i, i ^ x) for i in range(4)]) for x in (1, 2, 3)
    ]
    *q_pieces, kv_pieces = on_device(
        prep_kernel, four + [like(16, 2 * BLK, HEAD)], [], 1e6, 1.6e6
    )(place, query_rows, key_rows, value_rows)
    kv = exchange(kv_pieces, key_groups())
    q = over_rows([jnp.stack(over_heads(q_pieces))] * 4)

    do_pieces = by_columns(grad_attn_kernel, four, [pltpu.VMEM((BLK, 512), F32)], 5.4e8)(
        place, *cots, out_proj
    )
    do = over_rows([jnp.stack(over_heads(do_pieces))] * 4)

    *o_part, lse_part = on_device(
        fwd_kernel,
        [like(4, PIECE, HEAD)] * 4 + [like(1, TOKENS, dtype=F32)],
        [
            pltpu.VMEM((16, BLK, HEAD), BF16),
            pltpu.VMEM((HEAD, TOKENS), BF16),
            pltpu.VMEM((1, SPAN), F32),
            pltpu.VMEM((1, SPAN), F32),
            pltpu.VMEM((HEAD, SPAN), F32),
        ],
        2e9,
        2.6e6,
    )(place, *q, kv)

    att_mine = on_device(merge_kernel, like(4, BLK, HEAD), [], 1e6, 7e5, placed=False)(
        *over_rows(o_part)
    )
    stats = on_device(delta_kernel, like(2, TOKENS, dtype=F32), [], 1e6, 1.1e6)(
        place, *do, *o_part, lse_part
    )
    stats = over_rows([stats] * 4)
    att = over_heads([att_mine] * 4)

    *dq_part, dkv_part = on_device(
        bwd_kernel,
        stacks + [like(16, 2 * BLK, HEAD)],
        [
            pltpu.VMEM((16, BLK, HEAD), BF16),
            pltpu.VMEM((16, BLK, HEAD), BF16),
            pltpu.VMEM((HEAD, TOKENS), BF16),
            pltpu.VMEM((1, TOKENS), F32),
            pltpu.VMEM((1, TOKENS), F32),
            pltpu.VMEM((HEAD, SPAN), F32),
            pltpu.VMEM((TOKENS, HEAD), F32),
            pltpu.VMEM((TOKENS, HEAD), F32),
        ],
        5e9,
        3.6e6,
    )(place, *q, *do, kv, *stats)

    dkv_home = exchange(dkv_part, key_groups())
    dq_pieces = on_device(dq_sum_kernel, four, [], 1e6, 6e5)(place, *over_rows(dq_part))
    dq_home = over_heads(dq_pieces)
    grad_query, grad_key, grad_value = on_device(
        grads_kernel, [like(BLK, 512)] * 3, [], 1e6, 1.6e6
    )(place, *dq_home, dkv_home)

    layer_parts = by_columns(
        layer_kernel, [like(BLK, 1024)] * 4, [pltpu.VMEM((BLK, 512), BF16)], 5.4e8
    )(place, *att, out_proj)
    layer_all = [layer_parts[0]] + [
        lax.ppermute(layer_parts[x], "fsdp", [(i, i ^ x) for i in range(4)]) for x in (1, 2, 3)
    ]
    layer_out = sum(part.astype(F32) for part in layer_all).astype(BF16)

    cot_cols = [cot_hop(cotangent, i) for i in range(4)]
    proj_part = on_device(
        proj_kernel,
        like(16, 64, 512),
        [pltpu.VMEM((4 * BLK, 512), BF16), pltpu.VMEM((4 * BLK, 1024), BF16)],
        5.4e8,
        2.6e6,
    )(place, *att, *cot_cols)
    proj_home = exchange(proj_part, [[16 * i + j for j in range(16)] for i in range(4)])
    proj_grad = jnp.sum(proj_home.astype(F32), axis=0)
    return (layer_out, grad_query, grad_key, grad_value, proj_grad)


def solution(mesh):
    spec = P("ctx", "fsdp")
    return jax.shard_map(
        per_device,
        mesh=mesh,
        in_specs=(spec, spec, spec, P("fsdp", None), spec),
        out_specs=(spec, spec, spec, spec, spec),
        check_vma=False,
    )
```

time: 251 us -> 224 us (0.89); the launches traced: 248 us -> 224 us
  starting transfers between devices: 58.6 us -> 98.9 us
  waiting for transfers between devices: 113 us -> 80.5 us
  blocking collectives: 17.3 us -> 0 us
  between operations: 14.2 us -> 0.91 us
  matrix products: 10.4 us -> 0 us
  Pallas kernels: 21.7 us -> 31.4 us
    ppermute x3 -> x37, starting transfers between devices: 3.58 us -> 80.7 us  [the longest x27 63.1 us: hop(): return lax.ppermute(block, 'ctx', [(i, i ^ step) for i in range(64)])]
    all_to_all x8 -> x3, waiting for transfers between devices: 71.3 us -> 0.01 us  [exchange(): lax.all_to_all(pieces, 'ctx', 0, 0, axis_index_groups=groups, tiled=True)]
    ppermute x3 -> x37, waiting for transfers between devices: 10.3 us -> 80.5 us  [the longest x27 58.8 us: hop(): return lax.ppermute(block, 'ctx', [(i, i ^ step) for i in range(64)])]
    all_to_all x8 -> x3, starting transfers between devices: 54.9 us -> 18.2 us  [exchange(): lax.all_to_all(pieces, 'ctx', 0, 0, axis_index_groups=groups, tiled=True)]
    all_gather x1 -> x0, waiting for transfers between devices: 30.3 us -> none  [per_device(): full_cot = lax.all_gather(cotangent, 'fsdp', axis=1, tiled=True)]
    all_to_all x1 -> x0, blocking collectives: 17.3 us -> none  [exchange(): lax.all_to_all(pieces, 'ctx', 0, 0, axis_index_groups=groups, tiled=True)]
    dot_general x3 -> x0, matrix products: 10.4 us -> none  [the longest x1 3.93 us: mm(): return jnp.dot(lhs, rhs, preferred_element_type=F32)]
    unnamed x5 -> x18, local copies, waits for them, and re-layouts: 2.33 us -> 8.95 us
  transfers between devices with their start and end apart: 13 -> 40, of which waited for: 10 -> 14; matrix products, arithmetic and copies ran while one was open for 8% -> 0% of each run, Pallas kernels for 9% -> 8%
where the time goes in v2:
time: 224 us
  starting transfers between devices  98.9 us (44%)
  waiting for transfers between devices  80.5 us (36%)
  Pallas kernels  31.4 us (14%)
  local copies, waits for them, and re-layouts  9.04 us (4%)
  other arithmetic  2.95 us (1%)
    ppermute x27, starting transfers between devices, hop(): return lax.ppermute(block, 'ctx', [(i, i ^ step) for i in range(64)])  63.1 us
    ppermute x27, waiting for transfers between devices, hop(): return lax.ppermute(block, 'ctx', [(i, i ^ step) for i in range(64)])  58.8 us
    pallas_call x8, Pallas kernels, call(): pl.pallas_call(kernel, out_shape=out_shape, in_specs=specs, out_specs=jax...  26.2 us
    all_to_all x3, starting transfers between devices, exchange(): lax.all_to_all(pieces, 'ctx', 0, 0, axis_index_groups=groups, tiled=True)  18.2 us
    ppermute x3, waiting for transfers between devices, per_device(): lax.ppermute(cotangent, 'fsdp', [(i, i ^ x) for i in range(4)])  16 us
    ppermute x4, starting transfers between devices, cot_hop(): return lax.ppermute(block, ('ctx', 'fsdp'), route)  10.8 us
    unnamed x18, local copies, waits for them, and re-layouts  8.95 us
    ppermute x4, waiting for transfers between devices, cot_hop(): return lax.ppermute(block, ('ctx', 'fsdp'), route)  5.77 us
  transfers between devices with their start and end apart: 40, of which 14 were waited for; matrix products, arithmetic and copies ran while one was open for 0% of the time, Pallas kernels for 8%

profile of v2, /device:TPU:32, one launch (start us, length us, event | category | flops | bytes accessed | tf_op | source)
XLA Modules:
  0.0 223.8 jit_solution(8676103785725709587)
XLA Ops:
  5.2 6.9 %all-to-all-start = ((bf16[16,256,128]{2,1,0:T(8,128)(2,1)}), bf16[16,256,128]{2,1,0:T(8,128)(2,1)S(1)}, u32[]{:S(2)}, u32[]{:S(2)}) async-start(bf16[16,256,128]{2,1,0:T(8,128)(2,1)} %get-tuple-element.39), calls=%async_computation | async-start | bytes 2097152 | tf_op jit(solution)/shard_map/all_to_all | solution.py:34
  12.1 2.8 %collective-permute-start.16 = (bf16[128,1024]{1,0:T(8,128)(2,1)}, bf16[128,1024]{1,0:T(8,128)(2,1)S(1)}, u32[]{:S(2)}, u32[]{:S(2)}) collective-permute-start(bf16[128,1024]{1,0:T(8,128)(2,1)} %c0.1), channel_id=1, source_target_pairs={{0,2},{1,3},{2,0},{3,1},{4,6},{5,7},{6,4},{7,5},{8,10},{9,11},{10,... | collective-permute-start | bytes 786440 | tf_op jit(solution)/shard_map/ppermute | solution.py:358
  15.4 3.6 %collective-permute-start.2 = (bf16[128,128]{1,0:T(8,128)(2,1)S(1)}, bf16[128,128]{1,0:T(8,128)(2,1)S(1)}, u32[]{:S(2)}, u32[]{:S(2)}) collective-permute-start(bf16[128,128]{1,0:T(8,128)(2,1)S(1)} %get-tuple-element.38), channel_id=1, source_target_pairs={{0,224},{4,228},{8,232},{12,236},{16,240},{20,244},{24,248},{28,25... | collective-permute-start | bytes 98312 | tf_op jit(solution)/shard_map/ppermute | solution.py:38
  20.2 13.3 %collective-permute-done.16.c2 = bf16[128,1024]{1,0:T(8,128)(2,1)S(1)} collective-permute-done((bf16[128,1024]{1,0:T(8,128)(2,1)}, bf16[128,1024]{1,0:T(8,128)(2,1)S(1)}, u32[]{:S(2)}, u32[]{:S(2)}) %collective-permute-start.16) | collective-permute-done | bytes 262176 | tf_op jit(solution)/shard_map/ppermute | solution.py:358
  33.4 2.7 %collective-permute-done.17.c3 = bf16[128,1024]{1,0:T(8,128)(2,1)S(1)} collective-permute-done((bf16[128,1024]{1,0:T(8,128)(2,1)}, bf16[128,1024]{1,0:T(8,128)(2,1)S(1)}, u32[]{:S(2)}, u32[]{:S(2)}) %collective-permute-start.17) | collective-permute-done | bytes 262176 | tf_op jit(solution)/shard_map/ppermute | solution.py:358
  39.3 3.0 %shard_map.96 = (bf16[128,128]{1,0:T(8,128)(2,1)S(1)}, bf16[128,128]{1,0:T(8,128)(2,1)S(1)}, bf16[128,128]{1,0:T(8,128)(2,1)S(1)}, bf16[128,128]{1,0:T(8,128)(2,1)S(1)}) custom-call(s32[8]{0:T(128)S(1)} %stack.65.place, bf16[128,1024]{1,0:T(8,128)(2,1)S(1)} %copy-done.2, bf16[128,1024]{1,0:T(8,128)(2,1)S(1)} %collective-permute-done.15.c1, ...), custom_call_target="tpu_custom_call" | custom-call | flops 540000000 | bytes 6000000 | tf_op jit(solution)/shard_map/pallas_call | solution.py:332
  42.2 3.7 %collective-permute-start.20 = (bf16[128,128]{1,0:T(8,128)(2,1)S(1)}, bf16[128,128]{1,0:T(8,128)(2,1)S(1)}, u32[]{:S(2)}, u32[]{:S(2)}) collective-permute-start(bf16[128,128]{1,0:T(8,128)(2,1)S(1)} %get-tuple-element.51), channel_id=1, source_target_pairs={{0,224},{4,228},{8,232},{12,236},{16,240},{20,244},{24,248},{28,25... | collective-permute-start | bytes 98312 | tf_op jit(solution)/shard_map/ppermute | solution.py:38
  47.4 3.4 %collective-permute-start.3 = (bf16[4,128,128]{2,1,0:T(8,128)(2,1)S(1)}, bf16[4,128,128]{2,1,0:T(8,128)(2,1)S(1)}, u32[]{:S(2)}, u32[]{:S(2)}) collective-permute-start(bf16[4,128,128]{2,1,0:T(8,128)(2,1)S(1)} %pad_maximum_fusion.qa), channel_id=1, source_target_pairs={{0,8},{4,12},{8,0},{12,4},{16,24},{20,28},{24,16},{28,20},{32,40},... | collective-permute-start | bytes 393224 | tf_op jit(solution)/shard_map/ppermute | solution.py:38
  50.8 4.5 %collective-permute-start.4 = (bf16[4,128,128]{2,1,0:T(8,128)(2,1)S(1)}, bf16[4,128,128]{2,1,0:T(8,128)(2,1)S(1)}, u32[]{:S(2)}, u32[]{:S(2)}) collective-permute-start(bf16[4,128,128]{2,1,0:T(8,128)(2,1)S(1)} %pad_maximum_fusion.qa), channel_id=1, source_target_pairs={{0,16},{4,20},{8,24},{12,28},{16,0},{20,4},{24,8},{28,12},{32,48},... | collective-permute-start | bytes 393224 | tf_op jit(solution)/shard_map/ppermute | solution.py:38
  57.4 4.5 %collective-permute-start.22 = (bf16[4,128,128]{2,1,0:T(8,128)(2,1)S(1)}, bf16[4,128,128]{2,1,0:T(8,128)(2,1)S(1)}, u32[]{:S(2)}, u32[]{:S(2)}) collective-permute-start(bf16[4,128,128]{2,1,0:T(8,128)(2,1)S(1)} %pad_maximum_fusion.1.d0.da), channel_id=1, source_target_pairs={{0,16},{4,20},{8,24},{12,28},{16,0},{20,4},{24,8},{28,12},{32,48},... | collective-permute-start | bytes 393224 | tf_op jit(solution)/shard_map/ppermute | solution.py:38
  61.9 9.5 %collective-permute-done.3.qb = bf16[4,128,128]{2,1,0:T(8,128)(2,1)S(1)} collective-permute-done((bf16[4,128,128]{2,1,0:T(8,128)(2,1)S(1)}, bf16[4,128,128]{2,1,0:T(8,128)(2,1)S(1)}, u32[]{:S(2)}, u32[]{:S(2)}) %collective-permute-start.3) | collective-permute-done | bytes 131104 | tf_op jit(solution)/shard_map/ppermute | solution.py:38
  71.4 5.3 %collective-permute-start.23 = (bf16[4,128,128]{2,1,0:T(8,128)(2,1)S(1)}, bf16[4,128,128]{2,1,0:T(8,128)(2,1)S(1)}, u32[]{:S(2)}, u32[]{:S(2)}) collective-permute-start(bf16[4,128,128]{2,1,0:T(8,128)(2,1)S(1)} %pad_maximum_fusion.1.d0.da), channel_id=1, source_target_pairs={{0,24},{4,28},{8,16},{12,20},{16,8},{20,12},{24,0},{28,4},{32,56},... | collective-permute-start | bytes 393224 | tf_op jit(solution)/shard_map/ppermute | solution.py:38
  76.7 8.5 %shard_map.93 = (bf16[4,144,128]{2,1,0:T(8,128)(2,1)S(1)}, bf16[4,144,128]{2,1,0:T(8,128)(2,1)S(1)}, bf16[4,144,128]{2,1,0:T(8,128)(2,1)S(1)}, bf16[4,144,128]{2,1,0:T(8,128)(2,1)S(1)}, f32[1,2048]{1,0:T(1,128)S(1)}) custom-call(s32[8]{0:T(128)S(1)} %stack.65.place, bf16[4,128,128]{2,1,0:T(8,128)(2,1)S(1)} %pad_maximum_fusion.qa, ...), custom_call_target="tpu_custom_call" | custom-call | flops 2000000000 | bytes 2600000 | tf_op jit(solution)/shard_map/pallas_call | solution.py:316
  88.9 4.1 %collective-permute-start.26 = (f32[2,2048]{1,0:T(2,128)S(1)}, f32[2,2048]{1,0:T(2,128)S(1)}, u32[]{:S(2)}, u32[]{:S(2)}) collective-permute-start(f32[2,2048]{1,0:T(2,128)S(1)} %shard_map.97.st0), channel_id=1, source_target_pairs={{0,24},{4,28},{8,16},{12,20},{16,8},{20,12},{24,0},{28,4},{32,56},... | collective-permute-start | bytes 49160 | tf_op jit(solution)/shard_map/ppermute | solution.py:38
  95.6 10.3 %shard_map.98 = (bf16[4,128,128]{2,1,0:T(8,128)(2,1)S(1)}, bf16[4,128,128]{2,1,0:T(8,128)(2,1)S(1)}, bf16[4,128,128]{2,1,0:T(8,128)(2,1)S(1)}, bf16[4,128,128]{2,1,0:T(8,128)(2,1)S(1)}, bf16[16,256,128]{2,1,0:T(8,128)(2,1)}) custom-call(s32[8]{0:T(128)S(1)} %stack.65.place, bf16[4,128,128]{2,1,0:T(8,128)(2,1)S(1)} %pad_maximum_fusion.qa, ...), custom_call_target="tpu_custom_call" | custom-call | flops 5000000000 | bytes 3600000 | tf_op jit(solution)/shard_map/pallas_call | solution.py:316
  106.0 5.6 %all-to-all-start.1 = ((bf16[16,256,128]{2,1,0:T(8,128)(2,1)}), bf16[16,256,128]{2,1,0:T(8,128)(2,1)S(1)}, u32[]{:S(2)}, u32[]{:S(2)}) async-start(bf16[16,256,128]{2,1,0:T(8,128)(2,1)} %get-tuple-element.61), calls=%async_computation.1 | async-start | bytes 2097152 | tf_op jit(solution)/shard_map/all_to_all | solution.py:34
  111.6 2.5 %collective-permute-start.6 = (bf16[4,144,128]{2,1,0:T(8,128)(2,1)S(1)}, bf16[4,144,128]{2,1,0:T(8,128)(2,1)S(1)}, u32[]{:S(2)}, u32[]{:S(2)}) collective-permute-start(bf16[4,144,128]{2,1,0:T(8,128)(2,1)S(1)} %get-tuple-element.41.o1), channel_id=1, source_target_pairs={{0,8},{4,12},{8,0},{12,4},{16,24},{20,28},{24,16},{28,20},{32,40},... | collective-permute-start | bytes 442376 | tf_op jit(solution)/shard_map/ppermute | solution.py:38
  114.1 4.0 %collective-permute-start.7 = (bf16[4,144,128]{2,1,0:T(8,128)(2,1)S(1)}, bf16[4,144,128]{2,1,0:T(8,128)(2,1)S(1)}, u32[]{:S(2)}, u32[]{:S(2)}) collective-permute-start(bf16[4,144,128]{2,1,0:T(8,128)(2,1)S(1)} %get-tuple-element.42.o2), channel_id=1, source_target_pairs={{0,16},{4,20},{8,24},{12,28},{16,0},{20,4},{24,8},{28,12},{32,48},... | collective-permute-start | bytes 442376 | tf_op jit(solution)/shard_map/ppermute | solution.py:38
  118.8 4.1 %collective-permute-start.34 = (bf16[128,1024]{1,0:T(8,128)(2,1)S(1)}, bf16[128,1024]{1,0:T(8,128)(2,1)S(1)}, u32[]{:S(2)}, u32[]{:S(2)}) collective-permute-start(bf16[128,1024]{1,0:T(8,128)(2,1)S(1)} %copy-done.3), channel_id=1, source_target_pairs={{0,1},{1,97},{2,129},{3,225},{4,5},{5,101},{6,133},{7,229},{8,9},{... | collective-permute-start | bytes 786440 | tf_op jit(solution)/shard_map/ppermute | solution.py:56
  122.9 11.0 %collective-permute-done.6.o1 = bf16[4,144,128]{2,1,0:T(8,128)(2,1)S(1)} collective-permute-done((bf16[4,144,128]{2,1,0:T(8,128)(2,1)S(1)}, bf16[4,144,128]{2,1,0:T(8,128)(2,1)S(1)}, u32[]{:S(2)}, u32[]{:S(2)}) %collective-permute-start.6) | collective-permute-done | bytes 147488 | tf_op jit(solution)/shard_map/ppermute | solution.py:38
  134.5 5.9 %collective-permute-start.36 = (bf16[128,1024]{1,0:T(8,128)(2,1)S(1)}, bf16[128,1024]{1,0:T(8,128)(2,1)S(1)}, u32[]{:S(2)}, u32[]{:S(2)}) collective-permute-start(bf16[128,1024]{1,0:T(8,128)(2,1)S(1)} %copy-done.3), channel_id=1, source_target_pairs={{0,3},{1,99},{2,131},{3,227},{4,7},{5,103},{6,135},{7,231},{8,11},... | collective-permute-start | bytes 786440 | tf_op jit(solution)/shard_map/ppermute | solution.py:56
  141.8 3.8 %collective-permute-start.11 = (bf16[4,128,128]{2,1,0:T(8,128)(2,1)S(1)}, bf16[4,128,128]{2,1,0:T(8,128)(2,1)S(1)}, u32[]{:S(2)}, u32[]{:S(2)}) collective-permute-start(bf16[4,128,128]{2,1,0:T(8,128)(2,1)S(1)} %shard_map.94.a0), channel_id=1, source_target_pairs={{0,224},{4,228},{8,232},{12,236},{16,240},{20,244},{24,248},{28,25... | collective-permute-start | bytes 393224 | tf_op jit(solution)/shard_map/ppermute | solution.py:38
  145.6 5.8 %collective-permute-done.36.c3 = bf16[128,1024]{1,0:T(8,128)(2,1)S(1)} collective-permute-done((bf16[128,1024]{1,0:T(8,128)(2,1)S(1)}, bf16[128,1024]{1,0:T(8,128)(2,1)S(1)}, u32[]{:S(2)}, u32[]{:S(2)}) %collective-permute-start.36) | collective-permute-done | bytes 262176 | tf_op jit(solution)/shard_map/ppermute | solution.py:56
  151.8 2.6 %collective-permute-done.11.a3 = bf16[4,128,128]{2,1,0:T(8,128)(2,1)S(1)} collective-permute-done((bf16[4,128,128]{2,1,0:T(8,128)(2,1)S(1)}, bf16[4,128,128]{2,1,0:T(8,128)(2,1)S(1)}, u32[]{:S(2)}, u32[]{:S(2)}) %collective-permute-start.11) | collective-permute-done | bytes 131104 | tf_op jit(solution)/shard_map/ppermute | solution.py:38
  154.3 2.4 %shard_map.101 = bf16[16,64,512]{2,1,0:T(8,128)(2,1)} custom-call(s32[8]{0:T(128)S(1)} %stack.65.place, bf16[4,128,128]{2,1,0:T(8,128)(2,1)S(1)} %shard_map.94.a0, bf16[4,128,128]{2,1,0:T(8,128)(2,1)S(1)} %collective-permute-done.9.a1, bf16[4,128,128]{2,1,0:T(8,128)(2,1)S(1)} %collective-permute-done.10.a2, ...), custom_call_target="tpu_custom_call" | custom-call | flops 540000000 | bytes 2600000 | tf_op jit(solution)/shard_map/pallas_call | solution.py:316
  156.7 5.7 %all-to-all-start.2 = ((bf16[16,64,512]{2,1,0:T(8,128)(2,1)}), bf16[16,64,512]{2,1,0:T(8,128)(2,1)}, u32[]{:S(2)}, u32[]{:S(2)}) async-start(bf16[16,64,512]{2,1,0:T(8,128)(2,1)} %shard_map.101), calls=%async_computation.2 | async-start | bytes 2097152 | tf_op jit(solution)/shard_map/all_to_all | solution.py:34
  172.7 2.6 %collective-permute-start.28 = (bf16[4,128,128]{2,1,0:T(8,128)(2,1)S(1)}, bf16[4,128,128]{2,1,0:T(8,128)(2,1)S(1)}, u32[]{:S(2)}, u32[]{:S(2)}) collective-permute-start(bf16[4,128,128]{2,1,0:T(8,128)(2,1)S(1)} %get-tuple-element.55), channel_id=1, source_target_pairs={{0,16},{4,20},{8,24},{12,28},{16,0},{20,4},{24,8},{28,12},{32,48},... | collective-permute-start | bytes 393224 | tf_op jit(solution)/shard_map/ppermute | solution.py:38
  175.3 21.6 %collective-permute-done.27.d1 = bf16[4,128,128]{2,1,0:T(8,128)(2,1)S(1)} collective-permute-done((bf16[4,128,128]{2,1,0:T(8,128)(2,1)S(1)}, bf16[4,128,128]{2,1,0:T(8,128)(2,1)S(1)}, u32[]{:S(2)}, u32[]{:S(2)}) %collective-permute-start.27) | collective-permute-done | bytes 131104 | tf_op jit(solution)/shard_map/ppermute | solution.py:38
  196.9 5.6 %collective-permute-start.29 = (bf16[4,128,128]{2,1,0:T(8,128)(2,1)S(1)}, bf16[4,128,128]{2,1,0:T(8,128)(2,1)S(1)}, u32[]{:S(2)}, u32[]{:S(2)}) collective-permute-start(bf16[4,128,128]{2,1,0:T(8,128)(2,1)S(1)} %get-tuple-element.56), channel_id=1, source_target_pairs={{0,24},{4,28},{8,16},{12,20},{16,8},{20,12},{24,0},{28,4},{32,56},... | collective-permute-start | bytes 393224 | tf_op jit(solution)/shard_map/ppermute | solution.py:38
  202.6 6.3 %collective-permute-done.29.d3 = bf16[4,128,128]{2,1,0:T(8,128)(2,1)S(1)} collective-permute-done((bf16[4,128,128]{2,1,0:T(8,128)(2,1)S(1)}, bf16[4,128,128]{2,1,0:T(8,128)(2,1)S(1)}, u32[]{:S(2)}, u32[]{:S(2)}) %collective-permute-start.29) | collective-permute-done | bytes 131104 | tf_op jit(solution)/shard_map/ppermute | solution.py:38
  209.5 2.7 %collective-permute-start.30 = (bf16[128,128]{1,0:T(8,128)(2,1)S(1)}, bf16[128,128]{1,0:T(8,128)(2,1)S(1)}, u32[]{:S(2)}, u32[]{:S(2)}) collective-permute-start(bf16[128,128]{1,0:T(8,128)(2,1)S(1)} %get-tuple-element.58), channel_id=1, source_target_pairs={{0,96},{4,100},{8,104},{12,108},{16,112},{20,116},{24,120},{28,124... | collective-permute-start | bytes 98312 | tf_op jit(solution)/shard_map/ppermute | solution.py:38
  216.2 4.1 %collective-permute-done.32.e3 = bf16[128,128]{1,0:T(8,128)(2,1)S(1)} collective-permute-done((bf16[128,128]{1,0:T(8,128)(2,1)S(1)}, bf16[128,128]{1,0:T(8,128)(2,1)S(1)}, u32[]{:S(2)}, u32[]{:S(2)}) %collective-permute-start.32) | collective-permute-done | bytes 32800 | tf_op jit(solution)/shard_map/ppermute | solution.py:38
  (81 shorter events, 40.4 us)
Async XLA Ops:
  5.2 71.5 %all-to-all-start = ((bf16[16,256,128]{2,1,0:T(8,128)(2,1)}), bf16[16,256,128]{2,1,0:T(8,128)(2,1)S(1)}, u32[]{:S(2)}, u32[]{:S(2)}) async-start(bf16[16,256,128]{2,1,0:T(8,128)(2,1)} %get-tuple-element.39), calls=%async_computation | async-start | bytes 2097152 | tf_op jit(solution)/shard_map/all_to_all | solution.py:34
  12.1 21.4 %collective-permute-start.16 = (bf16[128,1024]{1,0:T(8,128)(2,1)}, bf16[128,1024]{1,0:T(8,128)(2,1)S(1)}, u32[]{:S(2)}, u32[]{:S(2)}) collective-permute-start(bf16[128,1024]{1,0:T(8,128)(2,1)} %c0.1), channel_id=1, source_target_pairs={{0,2},{1,3},{2,0},{3,1},{4,6},{5,7},{6,4},{7,5},{8,10},{9,11},{10,... | collective-permute-start | bytes 786440 | tf_op jit(solution)/shard_map/ppermute | solution.py:358
  14.9 21.2 %collective-permute-start.17 = (bf16[128,1024]{1,0:T(8,128)(2,1)}, bf16[128,1024]{1,0:T(8,128)(2,1)S(1)}, u32[]{:S(2)}, u32[]{:S(2)}) collective-permute-start(bf16[128,1024]{1,0:T(8,128)(2,1)} %c0.1), channel_id=1, source_target_pairs={{0,3},{1,2},{2,1},{3,0},{4,7},{5,6},{6,5},{7,4},{8,11},{9,10},{10,... | collective-permute-start | bytes 786440 | tf_op jit(solution)/shard_map/ppermute | solution.py:358
  15.4 31.9 %collective-permute-start.2 = (bf16[128,128]{1,0:T(8,128)(2,1)S(1)}, bf16[128,128]{1,0:T(8,128)(2,1)S(1)}, u32[]{:S(2)}, u32[]{:S(2)}) collective-permute-start(bf16[128,128]{1,0:T(8,128)(2,1)S(1)} %get-tuple-element.38), channel_id=1, source_target_pairs={{0,224},{4,228},{8,232},{12,236},{16,240},{20,244},{24,248},{28,25... | collective-permute-start | bytes 98312 | tf_op jit(solution)/shard_map/ppermute | solution.py:38
  19.0 28.4 %collective-permute-start.1 = (bf16[128,128]{1,0:T(8,128)(2,1)S(1)}, bf16[128,128]{1,0:T(8,128)(2,1)S(1)}, u32[]{:S(2)}, u32[]{:S(2)}) collective-permute-start(bf16[128,128]{1,0:T(8,128)(2,1)S(1)} %get-tuple-element.37), channel_id=1, source_target_pairs={{0,128},{4,132},{8,136},{12,140},{16,144},{20,148},{24,152},{28,15... | collective-permute-start | bytes 98312 | tf_op jit(solution)/shard_map/ppermute | solution.py:38
  19.6 27.8 %collective-permute-start = (bf16[128,128]{1,0:T(8,128)(2,1)S(1)}, bf16[128,128]{1,0:T(8,128)(2,1)S(1)}, u32[]{:S(2)}, u32[]{:S(2)}) collective-permute-start(bf16[128,128]{1,0:T(8,128)(2,1)S(1)} %get-tuple-element.36), channel_id=1, source_target_pairs={{0,96},{4,100},{8,104},{12,108},{16,112},{20,116},{24,120},{28,124... | collective-permute-start | bytes 98312 | tf_op jit(solution)/shard_map/ppermute | solution.py:38
  42.2 13.0 %collective-permute-start.20 = (bf16[128,128]{1,0:T(8,128)(2,1)S(1)}, bf16[128,128]{1,0:T(8,128)(2,1)S(1)}, u32[]{:S(2)}, u32[]{:S(2)}) collective-permute-start(bf16[128,128]{1,0:T(8,128)(2,1)S(1)} %get-tuple-element.51), channel_id=1, source_target_pairs={{0,224},{4,228},{8,232},{12,236},{16,240},{20,244},{24,248},{28,25... | collective-permute-start | bytes 98312 | tf_op jit(solution)/shard_map/ppermute | solution.py:38
  45.9 9.3 %collective-permute-start.19 = (bf16[128,128]{1,0:T(8,128)(2,1)S(1)}, bf16[128,128]{1,0:T(8,128)(2,1)S(1)}, u32[]{:S(2)}, u32[]{:S(2)}) collective-permute-start(bf16[128,128]{1,0:T(8,128)(2,1)S(1)} %get-tuple-element.50), channel_id=1, source_target_pairs={{0,128},{4,132},{8,136},{12,140},{16,144},{20,148},{24,152},{28,15... | collective-permute-start | bytes 98312 | tf_op jit(solution)/shard_map/ppermute | solution.py:38
  47.4 24.0 %collective-permute-start.3 = (bf16[4,128,128]{2,1,0:T(8,128)(2,1)S(1)}, bf16[4,128,128]{2,1,0:T(8,128)(2,1)S(1)}, u32[]{:S(2)}, u32[]{:S(2)}) collective-permute-start(bf16[4,128,128]{2,1,0:T(8,128)(2,1)S(1)} %pad_maximum_fusion.qa), channel_id=1, source_target_pairs={{0,8},{4,12},{8,0},{12,4},{16,24},{20,28},{24,16},{28,20},{32,40},... | collective-permute-start | bytes 393224 | tf_op jit(solution)/shard_map/ppermute | solution.py:38
  50.8 25.9 %collective-permute-start.4 = (bf16[4,128,128]{2,1,0:T(8,128)(2,1)S(1)}, bf16[4,128,128]{2,1,0:T(8,128)(2,1)S(1)}, u32[]{:S(2)}, u32[]{:S(2)}) collective-permute-start(bf16[4,128,128]{2,1,0:T(8,128)(2,1)S(1)} %pad_maximum_fusion.qa), channel_id=1, source_target_pairs={{0,16},{4,20},{8,24},{12,28},{16,0},{20,4},{24,8},{28,12},{32,48},... | collective-permute-start | bytes 393224 | tf_op jit(solution)/shard_map/ppermute | solution.py:38
  55.3 21.4 %collective-permute-start.5 = (bf16[4,128,128]{2,1,0:T(8,128)(2,1)S(1)}, bf16[4,128,128]{2,1,0:T(8,128)(2,1)S(1)}, u32[]{:S(2)}, u32[]{:S(2)}) collective-permute-start(bf16[4,128,128]{2,1,0:T(8,128)(2,1)S(1)} %pad_maximum_fusion.qa), channel_id=1, source_target_pairs={{0,24},{4,28},{8,16},{12,20},{16,8},{20,12},{24,0},{28,4},{32,56},... | collective-permute-start | bytes 393224 | tf_op jit(solution)/shard_map/ppermute | solution.py:38
  55.3 29.9 %collective-permute-start.21 = (bf16[4,128,128]{2,1,0:T(8,128)(2,1)S(1)}, bf16[4,128,128]{2,1,0:T(8,128)(2,1)S(1)}, u32[]{:S(2)}, u32[]{:S(2)}) collective-permute-start(bf16[4,128,128]{2,1,0:T(8,128)(2,1)S(1)} %pad_maximum_fusion.1.d0.da), channel_id=1, source_target_pairs={{0,8},{4,12},{8,0},{12,4},{16,24},{20,28},{24,16},{28,20},{32,40},... | collective-permute-start | bytes 393224 | tf_op jit(solution)/shard_map/ppermute | solution.py:38
  57.4 27.9 %collective-permute-start.22 = (bf16[4,128,128]{2,1,0:T(8,128)(2,1)S(1)}, bf16[4,128,128]{2,1,0:T(8,128)(2,1)S(1)}, u32[]{:S(2)}, u32[]{:S(2)}) collective-permute-start(bf16[4,128,128]{2,1,0:T(8,128)(2,1)S(1)} %pad_maximum_fusion.1.d0.da), channel_id=1, source_target_pairs={{0,16},{4,20},{8,24},{12,28},{16,0},{20,4},{24,8},{28,12},{32,48},... | collective-permute-start | bytes 393224 | tf_op jit(solution)/shard_map/ppermute | solution.py:38
  71.4 13.9 %collective-permute-start.23 = (bf16[4,128,128]{2,1,0:T(8,128)(2,1)S(1)}, bf16[4,128,128]{2,1,0:T(8,128)(2,1)S(1)}, u32[]{:S(2)}, u32[]{:S(2)}) collective-permute-start(bf16[4,128,128]{2,1,0:T(8,128)(2,1)S(1)} %pad_maximum_fusion.1.d0.da), channel_id=1, source_target_pairs={{0,24},{4,28},{8,16},{12,20},{16,8},{20,12},{24,0},{28,4},{32,56},... | collective-permute-start | bytes 393224 | tf_op jit(solution)/shard_map/ppermute | solution.py:38
  106.0 50.8 %all-to-all-start.1 = ((bf16[16,256,128]{2,1,0:T(8,128)(2,1)}), bf16[16,256,128]{2,1,0:T(8,128)(2,1)S(1)}, u32[]{:S(2)}, u32[]{:S(2)}) async-start(bf16[16,256,128]{2,1,0:T(8,128)(2,1)} %get-tuple-element.61), calls=%async_computation.1 | async-start | bytes 2097152 | tf_op jit(solution)/shard_map/all_to_all | solution.py:34
  111.6 22.3 %collective-permute-start.6 = (bf16[4,144,128]{2,1,0:T(8,128)(2,1)S(1)}, bf16[4,144,128]{2,1,0:T(8,128)(2,1)S(1)}, u32[]{:S(2)}, u32[]{:S(2)}) collective-permute-start(bf16[4,144,128]{2,1,0:T(8,128)(2,1)S(1)} %get-tuple-element.41.o1), channel_id=1, source_target_pairs={{0,8},{4,12},{8,0},{12,4},{16,24},{20,28},{24,16},{28,20},{32,40},... | collective-permute-start | bytes 442376 | tf_op jit(solution)/shard_map/ppermute | solution.py:38
  114.1 20.4 %collective-permute-start.7 = (bf16[4,144,128]{2,1,0:T(8,128)(2,1)S(1)}, bf16[4,144,128]{2,1,0:T(8,128)(2,1)S(1)}, u32[]{:S(2)}, u32[]{:S(2)}) collective-permute-start(bf16[4,144,128]{2,1,0:T(8,128)(2,1)S(1)} %get-tuple-element.42.o2), channel_id=1, source_target_pairs={{0,16},{4,20},{8,24},{12,28},{16,0},{20,4},{24,8},{28,12},{32,48},... | collective-permute-start | bytes 442376 | tf_op jit(solution)/shard_map/ppermute | solution.py:38
  118.1 23.1 %collective-permute-start.33 = (bf16[128,1024]{1,0:T(8,128)(2,1)S(1)}, bf16[128,1024]{1,0:T(8,128)(2,1)S(1)}, u32[]{:S(2)}, u32[]{:S(2)}) collective-permute-start(bf16[128,1024]{1,0:T(8,128)(2,1)S(1)} %copy-done.3), channel_id=1, source_target_pairs={{0,0},{1,96},{2,128},{3,224},{4,4},{5,100},{6,132},{7,228},{8,8},{... | collective-permute-start | bytes 786440 | tf_op jit(solution)/shard_map/ppermute | solution.py:56
  118.8 23.0 %collective-permute-start.34 = (bf16[128,1024]{1,0:T(8,128)(2,1)S(1)}, bf16[128,1024]{1,0:T(8,128)(2,1)S(1)}, u32[]{:S(2)}, u32[]{:S(2)}) collective-permute-start(bf16[128,1024]{1,0:T(8,128)(2,1)S(1)} %copy-done.3), channel_id=1, source_target_pairs={{0,1},{1,97},{2,129},{3,225},{4,5},{5,101},{6,133},{7,229},{8,9},{... | collective-permute-start | bytes 786440 | tf_op jit(solution)/shard_map/ppermute | solution.py:56
  122.9 17.6 %collective-permute-start.8 = (bf16[4,144,128]{2,1,0:T(8,128)(2,1)S(1)}, bf16[4,144,128]{2,1,0:T(8,128)(2,1)S(1)}, u32[]{:S(2)}, u32[]{:S(2)}) collective-permute-start(bf16[4,144,128]{2,1,0:T(8,128)(2,1)S(1)} %get-tuple-element.43.o3), channel_id=1, source_target_pairs={{0,24},{4,28},{8,16},{12,20},{16,8},{20,12},{24,0},{28,4},{32,56},... | collective-permute-start | bytes 442376 | tf_op jit(solution)/shard_map/ppermute | solution.py:38
  133.9 11.7 %collective-permute-start.35 = (bf16[128,1024]{1,0:T(8,128)(2,1)S(1)}, bf16[128,1024]{1,0:T(8,128)(2,1)S(1)}, u32[]{:S(2)}, u32[]{:S(2)}) collective-permute-start(bf16[128,1024]{1,0:T(8,128)(2,1)S(1)} %copy-done.3), channel_id=1, source_target_pairs={{0,2},{1,98},{2,130},{3,226},{4,6},{5,102},{6,134},{7,230},{8,10},... | collective-permute-start | bytes 786440 | tf_op jit(solution)/shard_map/ppermute | solution.py:56
  134.5 16.8 %collective-permute-start.36 = (bf16[128,1024]{1,0:T(8,128)(2,1)S(1)}, bf16[128,1024]{1,0:T(8,128)(2,1)S(1)}, u32[]{:S(2)}, u32[]{:S(2)}) collective-permute-start(bf16[128,1024]{1,0:T(8,128)(2,1)S(1)} %copy-done.3), channel_id=1, source_target_pairs={{0,3},{1,99},{2,131},{3,227},{4,7},{5,103},{6,135},{7,231},{8,11},... | collective-permute-start | bytes 786440 | tf_op jit(solution)/shard_map/ppermute | solution.py:56
  140.8 11.0 %collective-permute-start.9 = (bf16[4,128,128]{2,1,0:T(8,128)(2,1)S(1)}, bf16[4,128,128]{2,1,0:T(8,128)(2,1)S(1)}, u32[]{:S(2)}, u32[]{:S(2)}) collective-permute-start(bf16[4,128,128]{2,1,0:T(8,128)(2,1)S(1)} %shard_map.94.a0), channel_id=1, source_target_pairs={{0,96},{4,100},{8,104},{12,108},{16,112},{20,116},{24,120},{28,124... | collective-permute-start | bytes 393224 | tf_op jit(solution)/shard_map/ppermute | solution.py:38
  141.2 10.6 %collective-permute-start.10 = (bf16[4,128,128]{2,1,0:T(8,128)(2,1)S(1)}, bf16[4,128,128]{2,1,0:T(8,128)(2,1)S(1)}, u32[]{:S(2)}, u32[]{:S(2)}) collective-permute-start(bf16[4,128,128]{2,1,0:T(8,128)(2,1)S(1)} %shard_map.94.a0), channel_id=1, source_target_pairs={{0,128},{4,132},{8,136},{12,140},{16,144},{20,148},{24,152},{28,15... | collective-permute-start | bytes 393224 | tf_op jit(solution)/shard_map/ppermute | solution.py:38
  141.8 12.5 %collective-permute-start.11 = (bf16[4,128,128]{2,1,0:T(8,128)(2,1)S(1)}, bf16[4,128,128]{2,1,0:T(8,128)(2,1)S(1)}, u32[]{:S(2)}, u32[]{:S(2)}) collective-permute-start(bf16[4,128,128]{2,1,0:T(8,128)(2,1)S(1)} %shard_map.94.a0), channel_id=1, source_target_pairs={{0,224},{4,228},{8,232},{12,236},{16,240},{20,244},{24,248},{28,25... | collective-permute-start | bytes 393224 | tf_op jit(solution)/shard_map/ppermute | solution.py:38
  156.7 65.0 %all-to-all-start.2 = ((bf16[16,64,512]{2,1,0:T(8,128)(2,1)}), bf16[16,64,512]{2,1,0:T(8,128)(2,1)}, u32[]{:S(2)}, u32[]{:S(2)}) async-start(bf16[16,64,512]{2,1,0:T(8,128)(2,1)} %shard_map.101), calls=%async_computation.2 | async-start | bytes 2097152 | tf_op jit(solution)/shard_map/all_to_all | solution.py:34
  162.4 34.5 %collective-permute-start.27 = (bf16[4,128,128]{2,1,0:T(8,128)(2,1)S(1)}, bf16[4,128,128]{2,1,0:T(8,128)(2,1)S(1)}, u32[]{:S(2)}, u32[]{:S(2)}) collective-permute-start(bf16[4,128,128]{2,1,0:T(8,128)(2,1)S(1)} %get-tuple-element.54), channel_id=1, source_target_pairs={{0,8},{4,12},{8,0},{12,4},{16,24},{20,28},{24,16},{28,20},{32,40},... | collective-permute-start | bytes 393224 | tf_op jit(solution)/shard_map/ppermute | solution.py:38
  169.2 45.1 %collective-permute-start.14 = (bf16[128,1024]{1,0:T(8,128)(2,1)S(1)}, bf16[128,1024]{1,0:T(8,128)(2,1)S(1)}, u32[]{:S(2)}, u32[]{:S(2)}) collective-permute-start(bf16[128,1024]{1,0:T(8,128)(2,1)S(1)} %get-tuple-element.47), channel_id=1, source_target_pairs={{0,3},{1,2},{2,1},{3,0},{4,7},{5,6},{6,5},{7,4},{8,11},{9,10},{10,... | collective-permute-start | bytes 786440 | tf_op jit(solution)/shard_map/ppermute | solution.py:422
  171.5 42.9 %collective-permute-start.13 = (bf16[128,1024]{1,0:T(8,128)(2,1)S(1)}, bf16[128,1024]{1,0:T(8,128)(2,1)S(1)}, u32[]{:S(2)}, u32[]{:S(2)}) collective-permute-start(bf16[128,1024]{1,0:T(8,128)(2,1)S(1)} %get-tuple-element.46), channel_id=1, source_target_pairs={{0,2},{1,3},{2,0},{3,1},{4,6},{5,7},{6,4},{7,5},{8,10},{9,11},{10,... | collective-permute-start | bytes 786440 | tf_op jit(solution)/shard_map/ppermute | solution.py:422
  172.6 41.7 %collective-permute-start.12 = (bf16[128,1024]{1,0:T(8,128)(2,1)S(1)}, bf16[128,1024]{1,0:T(8,128)(2,1)S(1)}, u32[]{:S(2)}, u32[]{:S(2)}) collective-permute-start(bf16[128,1024]{1,0:T(8,128)(2,1)S(1)} %get-tuple-element.45), channel_id=1, source_target_pairs={{0,1},{1,0},{2,3},{3,2},{4,5},{5,4},{6,7},{7,6},{8,9},{9,8},{10,11... | collective-permute-start | bytes 786440 | tf_op jit(solution)/shard_map/ppermute | solution.py:422
  172.7 29.9 %collective-permute-start.28 = (bf16[4,128,128]{2,1,0:T(8,128)(2,1)S(1)}, bf16[4,128,128]{2,1,0:T(8,128)(2,1)S(1)}, u32[]{:S(2)}, u32[]{:S(2)}) collective-permute-start(bf16[4,128,128]{2,1,0:T(8,128)(2,1)S(1)} %get-tuple-element.55), channel_id=1, source_target_pairs={{0,16},{4,20},{8,24},{12,28},{16,0},{20,4},{24,8},{28,12},{32,48},... | collective-permute-start | bytes 393224 | tf_op jit(solution)/shard_map/ppermute | solution.py:38
  196.9 11.9 %collective-permute-start.29 = (bf16[4,128,128]{2,1,0:T(8,128)(2,1)S(1)}, bf16[4,128,128]{2,1,0:T(8,128)(2,1)S(1)}, u32[]{:S(2)}, u32[]{:S(2)}) collective-permute-start(bf16[4,128,128]{2,1,0:T(8,128)(2,1)S(1)} %get-tuple-element.56), channel_id=1, source_target_pairs={{0,24},{4,28},{8,16},{12,20},{16,8},{20,12},{24,0},{28,4},{32,56},... | collective-permute-start | bytes 393224 | tf_op jit(solution)/shard_map/ppermute | solution.py:38
  (17 other events, 101.1 us)

commit v3 on v2

v3 whole, which is shorter than its diff:
```python
import functools

import jax
import jax.numpy as jnp
from jax import lax
from jax.experimental import pallas as pl
from jax.experimental.pallas import tpu as pltpu
from jax.sharding import PartitionSpec as P

HEAD = 128
BLK = 128
SPAN = 4 * BLK
TOKENS = 16 * BLK
SCALE = HEAD ** -0.5
LOG2E = 1.4426950408889634
NEG_BIG = -1e30
F32 = jnp.float32
BF16 = jnp.bfloat16
VMEM_LIMIT = 64 * 1024 * 1024

R, Z = 2, 1
HEAD_STEP = (0, 24, 32, 56)
ROW_STEP = (0, R, 2 * R, 3 * R)
HALVES = [(y, z) for y in range(2) for z in range(2)]


def device(p, y, r, z):
    return 16 * p + 8 * (y ^ (p & 1)) + R * r + Z * z


def key_groups():
    return [[device(p, y ^ (p & 1), r, z) for p in range(4) for y, z in HALVES] for r in range(4)]


def query_groups():
    return [[device(p, y, r, z) for p in range(4) for r in range(4)] for y, z in HALVES]


def z_groups():
    return [[8 * i + z for z in range(8)] for i in range(8)]


def xy_groups():
    return [[8 * i + z for i in range(8)] for z in range(8)]


def exchange(pieces, groups):
    return lax.all_to_all(pieces, "ctx", 0, 0, axis_index_groups=groups, tiled=True)


def hop(block, step):
    return lax.ppermute(block, "ctx", [(i, i ^ step) for i in range(64)])


def over_heads(blocks):
    return [blocks[0]] + [hop(blocks[x], HEAD_STEP[x]) for x in (1, 2, 3)]


def over_rows(blocks):
    return [blocks[0]] + [hop(blocks[x], ROW_STEP[x]) for x in (1, 2, 3)]


def mm(lhs, rhs):
    return jnp.dot(lhs, rhs, preferred_element_type=F32)


def mm_nt(lhs, rhs):
    return lax.dot_general(lhs, rhs, (((1,), (1,)), ((), ())), preferred_element_type=F32)


def block_at(index, size=BLK):
    return pl.ds(pl.multiple_of(index * size, size), size)


def fetch(src, dst, sem):
    copy = pltpu.make_async_copy(src, dst, sem)
    copy.start()
    return copy


def prep_kernel(place, q_ref, k_ref, v_ref, q0, q1, q2, q3, kv_ref):
    for x, out in enumerate((q0, q1, q2, q3)):
        out[...] = q_ref[:, block_at(place[0] ^ x)]
    for j in range(16):
        at = slice((j // 4) * HEAD, (j // 4 + 1) * HEAD)
        kv_ref[j, :BLK, :] = k_ref[:, at]
        kv_ref[j, BLK:, :] = v_ref[:, at]


def w_columns(place, w_hbm, w_ref, sem):
    return [
        fetch(w_hbm.at[:, block_at(place[3] ^ x, 1024)], w_ref.at[x], sem.at[x]) for x in range(4)
    ]


def grad_attn_kernel(
    place, c0, c1, c2, c3, w_hbm, do_hbm, cot_hbm, c_ref, w_ref, do_ref, c_sem, w_sem, out_sem
):
    cots = [fetch(c, c_ref.at[x], c_sem.at[x]) for x, c in enumerate((c0, c1, c2, c3))]
    columns = w_columns(place, w_hbm, w_ref, w_sem)
    total = 0.0
    outs = []
    for x in range(4):
        cots[x].wait()
        for half in range(2):
            outs.append(
                fetch(
                    c_ref.at[x, :, 512 * half : 512 * (half + 1)],
                    cot_hbm.at[2 * (place[3] ^ x) + half],
                    out_sem.at[2 * x + half],
                )
            )
        columns[x].wait()
        total = total + mm_nt(c_ref[x], w_ref[x])
    for j in range(16):
        at = slice((j // 4) * HEAD, (j // 4 + 1) * HEAD)
        do_ref[j] = total[:, at].astype(BF16)
    outs.append(fetch(do_ref, do_hbm, out_sem.at[8]))
    for out in outs:
        out.wait()


def sort_rows(place, parts, out_ref):
    for x, part in enumerate(parts):
        for i in range(4):
            out_ref[4 * (place[0] ^ i) + (place[1] ^ x)] = part[i]


def causal(place, p):
    row = lax.broadcasted_iota(jnp.int32, (SPAN, SPAN), 0)
    row = (
        8 * BLK * (row // (2 * BLK)) + Z * BLK * (row // BLK % 2) + R * BLK * place[1] + row % BLK
    )
    col = lax.broadcasted_iota(jnp.int32, (1, SPAN), 1)
    col = R * BLK * (col // BLK) + BLK * (8 * place[4 + p] + Z * place[2]) + col % BLK
    return row <= col


def fwd_kernel(place, qa, qb, qc, qd, kv_ref, o0, o1, o2, o3, lse_ref, q_ref, vt_ref, out_ref):
    sort_rows(place, (qa, qb, qc, qd), q_ref)
    for j in range(16):
        vt_ref[:, j * BLK : (j + 1) * BLK] = kv_ref[j, BLK:, :].T
    for p in range(4):
        q = q_ref[4 * p : 4 * p + 4].reshape(SPAN, HEAD)
        mask = causal(place, p)
        scores = []
        for i in range(p + 1):
            k = kv_ref[4 * i : 4 * i + 4, :BLK, :].reshape(SPAN, HEAD)
            s = mm_nt(k, q) * (SCALE * LOG2E)
            scores.append(jnp.where(mask, s, NEG_BIG) if i == p else s)
        top = functools.reduce(jnp.maximum, [jnp.max(s, axis=0, keepdims=True) for s in scores])
        total, out = 0.0, 0.0
        for i, s in enumerate(scores):
            w = jnp.exp2(s - top)
            if i == p:
                w = jnp.where(mask, w, 0.0)
            total = total + jnp.sum(w, axis=0, keepdims=True)
            out = out + mm(vt_ref[:, i * SPAN : (i + 1) * SPAN], w.astype(BF16))
        some = total > 0.0
        safe = jnp.where(some, total, 1.0)
        lse = jnp.where(some, top + jnp.log2(safe), NEG_BIG)
        out_ref[...] = out * jnp.where(some, 1.0 / safe, 0.0)
        for r in range(4):
            lse_ref[4 * p + r : 4 * p + r + 1, :] = lse[:, r * BLK : (r + 1) * BLK]
        for x, to in enumerate((o0, o1, o2, o3)):
            to[p] = out_ref[:, block_at(place[1] ^ x)].T.astype(BF16)


def three_parts(value):
    high = value.astype(BF16)
    rest = value - high.astype(F32)
    mid = rest.astype(BF16)
    return high, mid, (rest - mid.astype(F32)).astype(BF16)


def pack_kernel(place, do_ref, o0, o1, o2, o3, lse_ref, p0, p1, p2, p3, delta_ref):
    for x, out in enumerate((o0, o1, o2, o3)):
        for p in range(4):
            j = 4 * p + (place[1] ^ x)
            prod = do_ref[j].astype(F32) * out[p].astype(F32)
            delta_ref[pl.ds(j, 1), :] = jnp.sum(prod.T, axis=0, keepdims=True)
    parts = three_parts(lse_ref[...]) + three_parts(delta_ref[...])
    for pack, out in zip((p0, p1, p2, p3), (o0, o1, o2, o3)):
        pack[:SPAN, :] = out[...].reshape(SPAN, HEAD)
        for i, part in enumerate(parts):
            pack[SPAN + 16 * i : SPAN + 16 * (i + 1), :] = part


def unpacked(pack, which):
    at = SPAN + 48 * which
    parts = [pack[at + 16 * i : at + 16 * (i + 1), :].astype(F32) for i in range(3)]
    return parts[0] + parts[1] + parts[2]


def log_totals(parts):
    top = functools.reduce(jnp.maximum, parts)
    return top + jnp.log2(sum(jnp.exp2(part - top) for part in parts))


def merge_kernel(place, p0, p1, p2, p3, out_ref, share_ref):
    packs = (p0, p1, p2, p3)
    parts = [unpacked(pack, 0) for pack in packs]
    total = log_totals(parts)
    for i, part in enumerate(parts):
        share_ref[i] = jnp.exp2(part - total)
    for p in range(4):
        merged = 0.0
        for i, pack in enumerate(packs):
            share = share_ref[i, pl.ds(4 * p + place[1], 1), :]
            share = jnp.broadcast_to(share, (BLK, HEAD)).T
            merged = merged + share * pack[p * BLK : (p + 1) * BLK, :].astype(F32)
        out_ref[p] = merged.astype(BF16)


def bwd_kernel(
    place, qa, qb, qc, qd, do_ref, kv_ref, p0, p1, p2, p3, dq0, dq1, dq2, dq3, dkv_ref,
    q_ref, kt_ref, lse_ref, delta_ref, dqt_ref, dk_ref, dv_ref
):
    sort_rows(place, (qa, qb, qc, qd), q_ref)
    parts = [unpacked(pack, 0) for pack in (p0, p1, p2, p3)]
    lse = log_totals(parts)
    lse_ref[...] = lse
    deltas = [unpacked(pack, 1) for pack in (p0, p1, p2, p3)]
    delta_ref[...] = sum(jnp.exp2(part - lse) * delta for part, delta in zip(parts, deltas))
    for j in range(16):
        kt_ref[:, j * BLK : (j + 1) * BLK] = kv_ref[j, :BLK, :].T
    for p in range(4):
        q = q_ref[4 * p : 4 * p + 4].reshape(SPAN, HEAD)
        do = do_ref[4 * p : 4 * p + 4].reshape(SPAN, HEAD)
        lse_now = jnp.concatenate([lse_ref[4 * p + r : 4 * p + r + 1, :] for r in range(4)], axis=1)
        delta_now = jnp.concatenate(
            [delta_ref[4 * p + r : 4 * p + r + 1, :] for r in range(4)], axis=1
        )
        dqt = 0.0
        for i in range(p + 1):
            rows = slice(i * SPAN, (i + 1) * SPAN)
            k = kv_ref[4 * i : 4 * i + 4, :BLK, :].reshape(SPAN, HEAD)
            v = kv_ref[4 * i : 4 * i + 4, BLK:, :].reshape(SPAN, HEAD)
            w = jnp.exp2(mm_nt(k, q) * (SCALE * LOG2E) - lse_now)
            if i == p:
                w = jnp.where(causal(place, p), w, 0.0)
            ds = (w * (mm_nt(v, do) - delta_now)).astype(BF16)
            dv, dk = mm(w.astype(BF16), do), mm(ds, q)
            dv_ref[rows, :] = dv if i == p else dv_ref[rows, :] + dv
            dk_ref[rows, :] = dk if i == p else dk_ref[rows, :] + dk
            dqt = dqt + mm(kt_ref[:, rows], ds)
        dqt_ref[...] = dqt * SCALE
        for x, out in enumerate((dq0, dq1, dq2, dq3)):
            out[p] = dqt_ref[:, block_at(place[1] ^ x)].T.astype(BF16)
    for j in range(16):
        at = slice(j * BLK, (j + 1) * BLK)
        dkv_ref[j, :BLK, :] = (dk_ref[at, :] * SCALE).astype(BF16)
        dkv_ref[j, BLK:, :] = dv_ref[at, :].astype(BF16)


def dq_sum_kernel(place, d0, d1, d2, d3, e0, e1, e2, e3):
    for x, out in enumerate((e0, e1, e2, e3)):
        p = place[0] ^ x
        out[...] = sum(part[p].astype(F32) for part in (d0, d1, d2, d3)).astype(BF16)


def last_kernel(
    place, e0, e1, e2, e3, dkv_ref, mine_ref, far_ref, proj_ref,
    layer_ref, dq_ref, dk_ref, dv_ref, sum_ref
):
    for x, part in enumerate((e0, e1, e2, e3)):
        dq_ref[:, block_at(place[0] ^ x)] = part[...]
    for h in range(4):
        total = sum(dkv_ref[4 * h + i].astype(F32) for i in range(4)).astype(BF16)
        at = slice(h * HEAD, (h + 1) * HEAD)
        dk_ref[:, at] = total[:BLK]
        dv_ref[:, at] = total[BLK:]
    layer_ref[...] = (mine_ref[...] + far_ref[...].astype(F32)).astype(BF16)
    sum_ref[...] = sum(proj_ref[i].astype(F32) for i in range(8))


def layer_kernel(
    place, a0, a1, a2, a3, w_hbm, kept_hbm, given_hbm, a_ref, rows_ref, w_ref, out_ref,
    a_sem, w_sem, out_sem
):
    parts = [fetch(a.at[place[0]], a_ref.at[x], a_sem.at[x]) for x, a in enumerate((a0, a1, a2, a3))]
    columns = w_columns(place, w_hbm, w_ref, w_sem)
    for x in range(4):
        parts[x].wait()
        rows_ref[:, block_at(place[0] ^ x)] = a_ref[x]
    outs = []
    for x in range(4):
        columns[x].wait()
        out_ref[x] = mm(rows_ref[...], w_ref[x]).astype(BF16)
        out = given_hbm if x & 1 else kept_hbm
        outs.append(fetch(out_ref.at[x], out.at[x >> 1], out_sem.at[x]))
    for out in outs:
        out.wait()


def pair_kernel(place, kept_ref, come_ref, mine_ref, other_ref):
    total = kept_ref[...].astype(F32) + come_ref[...].astype(F32)
    mine_ref[...] = total[0]
    other_ref[...] = total[1].astype(BF16)


def proj_kernel(place, a0, a1, a2, a3, others, cot_ref, out_ref, att_ref):
    for x, part in enumerate((a0, a1, a2, a3)):
        for p in range(4):
            cols = block_at(place[0] ^ x)
            att_ref[block_at(2 * p + place[4 + p]), cols] = part[p]
            att_ref[block_at(2 * p + (place[4 + p] ^ 1)), cols] = others[x, p]
    cot = cot_ref[...].reshape(8 * BLK, 512)
    for i in range(2):
        at = slice(i * 256, (i + 1) * 256)
        total = lax.dot_general(
            cot[:, at], att_ref[...], (((0,), (0,)), ((), ())), preferred_element_type=F32
        )
        out_ref[4 * i : 4 * i + 4] = total.astype(BF16).reshape(4, 64, 512)


def like(*shape, dtype=BF16):
    return jax.ShapeDtypeStruct(shape, dtype)


def params():
    return pltpu.CompilerParams(vmem_limit_bytes=VMEM_LIMIT)


def cost(flops, moved):
    return pl.CostEstimate(flops=int(flops), bytes_accessed=int(moved), transcendentals=0)


def raw(kernel, out_shape, scratch, flops, moved):
    def call(place, *args):
        return pl.pallas_call(
            kernel,
            out_shape=out_shape,
            in_specs=[pl.BlockSpec(memory_space=pltpu.SMEM)]
            + [pl.BlockSpec(memory_space=pltpu.HBM)] * len(args),
            out_specs=[pl.BlockSpec(memory_space=pltpu.HBM)] * len(out_shape),
            scratch_shapes=scratch,
            compiler_params=params(),
            cost_estimate=cost(flops, moved),
        )(place, *args)

    return call


def on_device(kernel, out_shape, scratch, flops, moved):
    def call(place, *args):
        return pl.pallas_call(
            kernel,
            out_shape=out_shape,
            in_specs=[pl.BlockSpec(memory_space=pltpu.SMEM)]
            + [pl.BlockSpec(memory_space=pltpu.VMEM)] * len(args),
            out_specs=[pl.BlockSpec(memory_space=pltpu.VMEM)] * len(out_shape),
            scratch_shapes=scratch,
            compiler_params=params(),
            cost_estimate=cost(flops, moved),
        )(place, *args)

    return call


def per_device(query_rows, key_rows, value_rows, out_proj, cotangent):
    c, f = lax.axis_index("ctx"), lax.axis_index("fsdp")
    p, y, r, z = c // 16, (c // 8) % 2, (c // 2) % 4, c % 2
    place = jnp.stack([p, r, z, f] + [y ^ ((p ^ i) & 1) for i in range(4)]).astype(jnp.int32)
    four = [like(BLK, HEAD)] * 4

    def swap(block, x):
        return lax.ppermute(block, "fsdp", [(i, i ^ x) for i in range(4)])

    far = swap(cotangent, 2)
    *q_pieces, kv_pieces = on_device(prep_kernel, four + [like(16, 2 * BLK, HEAD)], [], 1e6, 2e6)(
        place, query_rows, key_rows, value_rows
    )
    q_mine = jnp.stack(over_heads(q_pieces))
    kv_pieces, far, q_mine = lax.optimization_barrier((kv_pieces, far, q_mine))
    kv = exchange(kv_pieces, key_groups())
    q = over_rows([q_mine] * 4)
    cots = [cotangent, swap(cotangent, 1), far, swap(far, 1)]

    do_pieces, cot_pieces = raw(
        grad_attn_kernel,
        [like(16, BLK, HEAD), like(8, BLK, 512)],
        [
            pltpu.VMEM((4, BLK, 1024), BF16),
            pltpu.VMEM((4, 512, 1024), BF16),
            pltpu.VMEM((16, BLK, HEAD), BF16),
            pltpu.SemaphoreType.DMA((4,)),
            pltpu.SemaphoreType.DMA((4,)),
            pltpu.SemaphoreType.DMA((9,)),
        ],
        5.4e8,
        7e6,
    )(place, *cots, out_proj)
    do_pieces, kv, q = lax.optimization_barrier((do_pieces, kv, q))
    do = exchange(do_pieces, query_groups())

    *o_part, lse_part = on_device(
        fwd_kernel,
        [like(4, BLK, HEAD)] * 4 + [like(16, BLK, dtype=F32)],
        [
            pltpu.VMEM((16, BLK, HEAD), BF16),
            pltpu.VMEM((HEAD, TOKENS), BF16),
            pltpu.VMEM((HEAD, SPAN), F32),
        ],
        2e9,
        2.6e6,
    )(place, *q, kv)

    packs = on_device(
        pack_kernel, [like(SPAN + 96, HEAD)] * 4, [pltpu.VMEM((16, BLK), F32)], 1e6, 1.6e6
    )(place, do, *o_part, lse_part)
    packs, cot_pieces = lax.optimization_barrier((packs, cot_pieces))
    packs = over_rows(packs)
    (att_mine,) = on_device(
        merge_kernel, [like(4, BLK, HEAD)], [pltpu.VMEM((4, 16, BLK), F32)], 1e6, 7e5
    )(place, *packs)
    cot_cols = exchange(cot_pieces, xy_groups())
    packs, att_mine, cot_cols = lax.optimization_barrier((packs, att_mine, cot_cols))
    att = over_heads([att_mine] * 4)

    *dq_part, dkv_part = on_device(
        bwd_kernel,
        [like(4, BLK, HEAD)] * 4 + [like(16, 2 * BLK, HEAD)],
        [
            pltpu.VMEM((16, BLK, HEAD), BF16),
            pltpu.VMEM((HEAD, TOKENS), BF16),
            pltpu.VMEM((16, BLK), F32),
            pltpu.VMEM((16, BLK), F32),
            pltpu.VMEM((HEAD, SPAN), F32),
            pltpu.VMEM((TOKENS, HEAD), F32),
            pltpu.VMEM((TOKENS, HEAD), F32),
        ],
        5e9,
        3.6e6,
    )(place, *q, do, kv, *packs)

    att, cot_cols, dkv_part = lax.optimization_barrier((att, cot_cols, dkv_part))
    dkv_home = exchange(dkv_part, key_groups())
    kept, given = raw(
        layer_kernel,
        [like(2, BLK, 1024)] * 2,
        [
            pltpu.VMEM((4, BLK, HEAD), BF16),
            pltpu.VMEM((BLK, 512), BF16),
            pltpu.VMEM((4, 512, 1024), BF16),
            pltpu.VMEM((4, BLK, 1024), BF16),
            pltpu.SemaphoreType.DMA((4,)),
            pltpu.SemaphoreType.DMA((4,)),
            pltpu.SemaphoreType.DMA((4,)),
        ],
        5.4e8,
        6e6,
    )(place, *att, out_proj)
    (proj_part,) = on_device(
        proj_kernel, [like(8, 64, 512)], [pltpu.VMEM((8 * BLK, 512), BF16)], 5.4e8, 2.6e6
    )(place, *att, hop(jnp.stack(att), 8), cot_cols)
    dq_all = over_rows(dq_part)
    dq_all, proj_part, kept = lax.optimization_barrier((dq_all, proj_part, kept))

    mine, other = on_device(
        pair_kernel, [like(BLK, 1024, dtype=F32), like(BLK, 1024)], [], 1e6, 2e6
    )(place, kept, swap(given, 1))

    proj_part, dkv_home, dq_all = lax.optimization_barrier((proj_part, dkv_home, dq_all))
    proj_home = exchange(proj_part, z_groups())
    dq_pieces = on_device(dq_sum_kernel, four, [], 1e6, 6e5)(place, *dq_all)
    dq_home = over_heads(dq_pieces)
    layer_out, grad_query, grad_key, grad_value, proj_grad = on_device(
        last_kernel,
        [like(BLK, 1024)] + [like(BLK, 512)] * 3 + [like(64, 512, dtype=F32)],
        [],
        1e6,
        3.6e6,
    )(place, *dq_home, dkv_home, mine, swap(other, 2), proj_home)
    return (layer_out, grad_query, grad_key, grad_value, proj_grad)


def solution(mesh):
    spec = P("ctx", "fsdp")
    return jax.shard_map(
        per_device,
        mesh=mesh,
        in_specs=(spec, spec, spec, P("fsdp", None), spec),
        out_specs=(spec, spec, spec, spec, spec),
        check_vma=False,
    )
```

time: 224 us -> 162 us (0.72)
  waiting for transfers between devices: 80.5 us -> 43.5 us
  starting transfers between devices: 98.9 us -> 70.3 us
  Pallas kernels: 31.4 us -> 43 us
  local copies, waits for them, and re-layouts: 9.04 us -> 0.63 us
    ppermute x27 -> x19, waiting for transfers between devices: 58.8 us -> 31.1 us  [hop(): return lax.ppermute(block, 'ctx', [(i, i ^ step) for i in range(64)])]
    ppermute x27 -> x19, starting transfers between devices: 63.1 us -> 37.2 us  [hop(): return lax.ppermute(block, 'ctx', [(i, i ^ step) for i in range(64)])]
    ppermute x10 -> x5, waiting for transfers between devices: 21.7 us -> 4.06 us  [swap(): return lax.ppermute(block, 'fsdp', [(i, i ^ x) for i in range(4)])]
    ppermute x10 -> x5, starting transfers between devices: 17.6 us -> 5.71 us  [swap(): return lax.ppermute(block, 'fsdp', [(i, i ^ x) for i in range(4)])]
    pallas_call x10 -> x11, Pallas kernels: 31.4 us -> 43 us  [call(): pl.pallas_call(kernel, out_shape=out_shape, in_specs=[pl.BlockSpec(memory...]
    all_to_all x3 -> x5, starting transfers between devices: 18.2 us -> 27.5 us  [exchange(): lax.all_to_all(pieces, 'ctx', 0, 0, axis_index_groups=groups, tiled=True)]
    unnamed x18 -> x0, local copies, waits for them, and re-layouts: 8.95 us -> none
    all_to_all x3 -> x5, waiting for transfers between devices: 0.01 us -> 8.33 us  [exchange(): lax.all_to_all(pieces, 'ctx', 0, 0, axis_index_groups=groups, tiled=True)]
  transfers between devices with their start and end apart: 40 -> 29, of which waited for: 14 -> 14; matrix products, arithmetic and copies ran while one was open for 0% -> 2% of each run, Pallas kernels for 8% -> 23%
where the time goes in v3:
time: 162 us
  starting transfers between devices  70.3 us (43%)
  waiting for transfers between devices  43.5 us (27%)
  Pallas kernels  43 us (27%)
  other arithmetic  3.38 us (2%)
    pallas_call x11, Pallas kernels, call(): pl.pallas_call(kernel, out_shape=out_shape, in_specs=[pl.BlockSpec(memory...  43 us
    ppermute x19, starting transfers between devices, hop(): return lax.ppermute(block, 'ctx', [(i, i ^ step) for i in range(64)])  37.2 us
    ppermute x19, waiting for transfers between devices, hop(): return lax.ppermute(block, 'ctx', [(i, i ^ step) for i in range(64)])  31.1 us
    all_to_all x5, starting transfers between devices, exchange(): lax.all_to_all(pieces, 'ctx', 0, 0, axis_index_groups=groups, tiled=True)  27.5 us
    all_to_all x5, waiting for transfers between devices, exchange(): lax.all_to_all(pieces, 'ctx', 0, 0, axis_index_groups=groups, tiled=True)  8.33 us
    ppermute x5, starting transfers between devices, swap(): return lax.ppermute(block, 'fsdp', [(i, i ^ x) for i in range(4)])  5.71 us
    ppermute x5, waiting for transfers between devices, swap(): return lax.ppermute(block, 'fsdp', [(i, i ^ x) for i in range(4)])  4.06 us
  transfers between devices with their start and end apart: 29, of which 14 were waited for; matrix products, arithmetic and copies ran while one was open for 2% of the time, Pallas kernels for 23%

profile of v3, /device:TPU:32, one launch (start us, length us, event | category | flops | bytes accessed | tf_op | source)
XLA Modules:
  0.0 161.6 jit_solution(3429720298470199238)
XLA Ops:
  0.6 3.1 %collective-permute-start.1 = (bf16[128,1024]{1,0:T(8,128)(2,1)}, bf16[128,1024]{1,0:T(8,128)(2,1)}, u32[]{:S(2)}, u32[]{:S(2)}) collective-permute-start(bf16[128,1024]{1,0:T(8,128)(2,1)} %c0.1), channel_id=1, source_target_pairs={{0,2},{1,3},{2,0},{3,1},{4,6},{5,7},{6,4},{7,5},{8,10},{9,11},{10,... | collective-permute-start | bytes 786440 | tf_op jit(solution)/shard_map/ppermute | solution.py:368
  4.4 2.2 %shard_map.92 = (bf16[128,128]{1,0:T(8,128)(2,1)}, bf16[128,128]{1,0:T(8,128)(2,1)}, bf16[128,128]{1,0:T(8,128)(2,1)}, bf16[128,128]{1,0:T(8,128)(2,1)}, bf16[16,256,128]{2,1,0:T(8,128)(2,1)}) custom-call(s32[8]{0:T(128)} %stack.65.place, bf16[128,512]{1,0:T(8,128)(2,1)} %q_ref.1, bf16[128,512]{1,0:T(8,128)(2,1)} %k_ref.1, bf16[128,512]{1,0:T(8,128)(2,1)} %v_ref.1), custom_call_target="tpu_custom_call" | custom-call | flops 1000000 | bytes 2000000 | tf_op jit(solution)/shard_map/pallas_call | solution.py:347
  6.5 3.0 %collective-permute-start.2 = (bf16[128,128]{1,0:T(8,128)(2,1)}, bf16[128,128]{1,0:T(8,128)(2,1)S(1)}, u32[]{:S(2)}, u32[]{:S(2)}) collective-permute-start(bf16[128,128]{1,0:T(8,128)(2,1)} %get-tuple-element.74), channel_id=1, source_target_pairs={{0,96},{4,100},{8,104},{12,108},{16,112},{20,116},{24,120},{28,124... | collective-permute-start | bytes 98312 | tf_op jit(solution)/shard_map/ppermute | solution.py:52
  13.7 2.7 %collective-permute-done.4 = bf16[128,128]{1,0:T(8,128)(2,1)S(1)} collective-permute-done((bf16[128,128]{1,0:T(8,128)(2,1)}, bf16[128,128]{1,0:T(8,128)(2,1)S(1)}, u32[]{:S(2)}, u32[]{:S(2)}) %collective-permute-start.4) | collective-permute-done | bytes 32800 | tf_op jit(solution)/shard_map/ppermute | solution.py:52
  17.8 4.2 %all-to-all-start = ((bf16[16,256,128]{2,1,0:T(8,128)(2,1)}), bf16[16,256,128]{2,1,0:T(8,128)(2,1)}, u32[]{:S(2)}, u32[]{:S(2)}) async-start(bf16[16,256,128]{2,1,0:T(8,128)(2,1)} %get-tuple-element.79), calls=%async_computation | async-start | bytes 2097152 | tf_op jit(solution)/shard_map/all_to_all | solution.py:48
  22.6 6.2 %collective-permute-start.8 = (bf16[4,128,128]{2,1,0:T(8,128)(2,1)}, bf16[4,128,128]{2,1,0:T(8,128)(2,1)}, u32[]{:S(2)}, u32[]{:S(2)}) collective-permute-start(bf16[4,128,128]{2,1,0:T(8,128)(2,1)} %pad_maximum_fusion.1.qa), channel_id=1, source_target_pairs={{0,24},{4,28},{8,16},{12,20},{16,8},{20,12},{24,0},{28,4},{32,56},... | collective-permute-start | bytes 393224 | tf_op jit(solution)/shard_map/ppermute | solution.py:52
  31.2 4.9 %shard_map.93 = (bf16[16,128,128]{2,1,0:T(8,128)(2,1)}, bf16[8,128,512]{2,1,0:T(8,128)(2,1)}) custom-call(s32[8]{0:T(128)} %stack.65.place, bf16[128,1024]{1,0:T(8,128)(2,1)} %c0.1, bf16[128,1024]{1,0:T(8,128)(2,1)} %collective-permute-done.c1, bf16[128,1024]{1,0:T(8,128)(2,1)} %collective-permute-done.1.c2, bf16[128,1024]{1,0:T(8,128)(2,1)} %collective-permute-done.5.c3, ...), custom_call_target="tpu_custom_call" | custom-call | flops 540000000 | bytes 7000000 | tf_op jit(solution)/shard_map/pallas_call | solution.py:331
  36.1 4.2 %collective-permute-done.8.qd = bf16[4,128,128]{2,1,0:T(8,128)(2,1)} collective-permute-done((bf16[4,128,128]{2,1,0:T(8,128)(2,1)}, bf16[4,128,128]{2,1,0:T(8,128)(2,1)}, u32[]{:S(2)}, u32[]{:S(2)}) %collective-permute-start.8) | collective-permute-done | bytes 131104 | tf_op jit(solution)/shard_map/ppermute | solution.py:52
  40.3 10.2 %collective-permute-done.7.qc = bf16[4,128,128]{2,1,0:T(8,128)(2,1)} collective-permute-done((bf16[4,128,128]{2,1,0:T(8,128)(2,1)}, bf16[4,128,128]{2,1,0:T(8,128)(2,1)}, u32[]{:S(2)}, u32[]{:S(2)}) %collective-permute-start.7) | collective-permute-done | bytes 131104 | tf_op jit(solution)/shard_map/ppermute | solution.py:52
  50.5 6.0 %all-to-all-start.1 = ((bf16[16,128,128]{2,1,0:T(8,128)(2,1)}), bf16[16,128,128]{2,1,0:T(8,128)(2,1)}, u32[]{:S(2)}, u32[]{:S(2)}) async-start(bf16[16,128,128]{2,1,0:T(8,128)(2,1)} %get-tuple-element.85), calls=%async_computation.1 | async-start | bytes 1048576 | tf_op jit(solution)/shard_map/all_to_all | solution.py:48
  56.5 7.2 %shard_map.94 = (bf16[4,128,128]{2,1,0:T(8,128)(2,1)}, bf16[4,128,128]{2,1,0:T(8,128)(2,1)}, bf16[4,128,128]{2,1,0:T(8,128)(2,1)}, bf16[4,128,128]{2,1,0:T(8,128)(2,1)}, f32[16,128]{1,0:T(8,128)}) custom-call(s32[8]{0:T(128)} %stack.65.place, bf16[4,128,128]{2,1,0:T(8,128)(2,1)} %pad_maximum_fusion.1.qa, bf16[4,128,128]{2,1,0:T(8,128)(2,1)} %collective-permute-done.6.qb, ...), custom_call_target="tpu_custom_call" | custom-call | flops 2000000000 | bytes 2600000 | tf_op jit(solution)/shard_map/pallas_call | solution.py:347
  63.7 8.3 %all-to-all-done.1.do_ref = bf16[16,128,128]{2,1,0:T(8,128)(2,1)} async-done(((bf16[16,128,128]{2,1,0:T(8,128)(2,1)}), bf16[16,128,128]{2,1,0:T(8,128)(2,1)}, u32[]{:S(2)}, u32[]{:S(2)}) %all-to-all-start.1) | async-done | bytes 524320 | tf_op jit(solution)/shard_map/all_to_all | solution.py:48
  72.0 2.5 %shard_map.95 = (bf16[608,128]{1,0:T(8,128)(2,1)}, bf16[608,128]{1,0:T(8,128)(2,1)}, bf16[608,128]{1,0:T(8,128)(2,1)}, bf16[608,128]{1,0:T(8,128)(2,1)}) custom-call(s32[8]{0:T(128)} %stack.65.place, bf16[16,128,128]{2,1,0:T(8,128)(2,1)} %all-to-all-done.1.do_ref, bf16[4,128,128]{2,1,0:T(8,128)(2,1)} %get-tuple-element.87.o0, ...), custom_call_target="tpu_custom_call" | custom-call | flops 1000000 | bytes 1600000 | tf_op jit(solution)/shard_map/pallas_call | solution.py:347
  74.4 4.2 %all-to-all-start.2 = ((bf16[8,128,512]{2,1,0:T(8,128)(2,1)}), bf16[8,128,512]{2,1,0:T(8,128)(2,1)}, u32[]{:S(2)}, u32[]{:S(2)}) async-start(bf16[8,128,512]{2,1,0:T(8,128)(2,1)} %get-tuple-element.101), calls=%async_computation.2 | async-start | bytes 2097152 | tf_op jit(solution)/shard_map/all_to_all | solution.py:48
  80.0 5.3 %collective-permute-start.11 = (bf16[608,128]{1,0:T(8,128)(2,1)}, bf16[608,128]{1,0:T(8,128)(2,1)}, u32[]{:S(2)}, u32[]{:S(2)}) collective-permute-start(bf16[608,128]{1,0:T(8,128)(2,1)} %get-tuple-element.100), channel_id=1, source_target_pairs={{0,24},{4,28},{8,16},{12,20},{16,8},{20,12},{24,0},{28,4},{32,56},... | collective-permute-start | bytes 466952 | tf_op jit(solution)/shard_map/ppermute | solution.py:52
  85.4 3.9 %collective-permute-done.10.p2 = bf16[608,128]{1,0:T(8,128)(2,1)} collective-permute-done((bf16[608,128]{1,0:T(8,128)(2,1)}, bf16[608,128]{1,0:T(8,128)(2,1)}, u32[]{:S(2)}, u32[]{:S(2)}) %collective-permute-start.10) | collective-permute-done | bytes 155680 | tf_op jit(solution)/shard_map/ppermute | solution.py:52
  89.4 4.4 %collective-permute-done.11.p3 = bf16[608,128]{1,0:T(8,128)(2,1)} collective-permute-done((bf16[608,128]{1,0:T(8,128)(2,1)}, bf16[608,128]{1,0:T(8,128)(2,1)}, u32[]{:S(2)}, u32[]{:S(2)}) %collective-permute-start.11) | collective-permute-done | bytes 155680 | tf_op jit(solution)/shard_map/ppermute | solution.py:52
  93.8 2.2 %shard_map.96.a0 = bf16[4,128,128]{2,1,0:T(8,128)(2,1)} custom-call(s32[8]{0:T(128)} %stack.65.place, bf16[608,128]{1,0:T(8,128)(2,1)} %get-tuple-element.102.p0, bf16[608,128]{1,0:T(8,128)(2,1)} %collective-permute-done.9.p1, bf16[608,128]{1,0:T(8,128)(2,1)} %collective-permute-done.10.p2, bf16[608,128]{1,0:T(8,128)(2,1)} %collective-permute-done.11.p3), custom_call_target="tpu_custom_call" | custom-call | flops 1000000 | bytes 700000 | tf_op jit(solution)/shard_map/pallas_call | solution.py:347
  96.0 4.0 %collective-permute-start.17 = (bf16[4,128,128]{2,1,0:T(8,128)(2,1)}, bf16[4,128,128]{2,1,0:T(8,128)(2,1)}, u32[]{:S(2)}, u32[]{:S(2)}) collective-permute-start(bf16[4,128,128]{2,1,0:T(8,128)(2,1)} %shard_map.96.a0), channel_id=1, source_target_pairs={{0,224},{4,228},{8,232},{12,236},{16,240},{20,244},{24,248},{28,25... | collective-permute-start | bytes 393224 | tf_op jit(solution)/shard_map/ppermute | solution.py:52
  100.7 9.7 %shard_map.97 = (bf16[4,128,128]{2,1,0:T(8,128)(2,1)}, bf16[4,128,128]{2,1,0:T(8,128)(2,1)}, bf16[4,128,128]{2,1,0:T(8,128)(2,1)}, bf16[4,128,128]{2,1,0:T(8,128)(2,1)}, bf16[16,256,128]{2,1,0:T(8,128)(2,1)}) custom-call(s32[8]{0:T(128)} %stack.65.place, bf16[4,128,128]{2,1,0:T(8,128)(2,1)} %pad_maximum_fusion.1.qa, ...), custom_call_target="tpu_custom_call" | custom-call | flops 5000000000 | bytes 3600000 | tf_op jit(solution)/shard_map/pallas_call | solution.py:347
  110.4 6.7 %all-to-all-start.3 = ((bf16[16,256,128]{2,1,0:T(8,128)(2,1)}), bf16[16,256,128]{2,1,0:T(8,128)(2,1)}, u32[]{:S(2)}, u32[]{:S(2)}) async-start(bf16[16,256,128]{2,1,0:T(8,128)(2,1)} %get-tuple-element.120), calls=%async_computation.3 | async-start | bytes 2097152 | tf_op jit(solution)/shard_map/all_to_all | solution.py:48
  121.4 2.1 %collective-permute-start.13 = (bf16[4,128,128]{2,1,0:T(8,128)(2,1)}, bf16[4,128,128]{2,1,0:T(8,128)(2,1)}, u32[]{:S(2)}, u32[]{:S(2)}) collective-permute-start(bf16[4,128,128]{2,1,0:T(8,128)(2,1)} %get-tuple-element.108), channel_id=1, source_target_pairs={{0,16},{4,20},{8,24},{12,28},{16,0},{20,4},{24,8},{28,12},{32,48},... | collective-permute-start | bytes 393224 | tf_op jit(solution)/shard_map/ppermute | solution.py:52
  123.5 3.5 %collective-permute-start.14 = (bf16[4,128,128]{2,1,0:T(8,128)(2,1)}, bf16[4,128,128]{2,1,0:T(8,128)(2,1)}, u32[]{:S(2)}, u32[]{:S(2)}) collective-permute-start(bf16[4,128,128]{2,1,0:T(8,128)(2,1)} %get-tuple-element.109), channel_id=1, source_target_pairs={{0,24},{4,28},{8,16},{12,20},{16,8},{20,12},{24,0},{28,4},{32,56},... | collective-permute-start | bytes 393224 | tf_op jit(solution)/shard_map/ppermute | solution.py:52
  127.0 4.5 %shard_map.99 = (bf16[2,128,1024]{2,1,0:T(8,128)(2,1)}, bf16[2,128,1024]{2,1,0:T(8,128)(2,1)}) custom-call(s32[8]{0:T(128)} %stack.65.place, bf16[4,128,128]{2,1,0:T(8,128)(2,1)} %shard_map.96.a0, bf16[4,128,128]{2,1,0:T(8,128)(2,1)} %collective-permute-done.15.a1, bf16[4,128,128]{2,1,0:T(8,128)(2,1)} %collective-permute-done.16.a2, ...), custom_call_target="tpu_custom_call" | custom-call | flops 540000000 | bytes 6000000 | tf_op jit(solution)/shard_map/pallas_call | solution.py:331
  131.8 3.4 %shard_map.98 = bf16[8,64,512]{2,1,0:T(8,128)(2,1)} custom-call(s32[8]{0:T(128)} %stack.65.place, bf16[4,128,128]{2,1,0:T(8,128)(2,1)} %shard_map.96.a0, bf16[4,128,128]{2,1,0:T(8,128)(2,1)} %collective-permute-done.15.a1, bf16[4,128,128]{2,1,0:T(8,128)(2,1)} %collective-permute-done.16.a2, bf16[4,128,128]{2,1,0:T(8,128)(2,1)} %collective-permute-done.17.a3, ...), custom_call_target="tpu_custom_call" | custom-call | flops 540000000 | bytes 2600000 | tf_op jit(solution)/shard_map/pallas_call | solution.py:347
  135.2 6.3 %all-to-all-start.4 = ((bf16[8,64,512]{2,1,0:T(8,128)(2,1)}), bf16[8,64,512]{2,1,0:T(8,128)(2,1)}, u32[]{:S(2)}, u32[]{:S(2)}) async-start(bf16[8,64,512]{2,1,0:T(8,128)(2,1)} %shard_map.98), calls=%async_computation.4 | async-start | bytes 1048576 | tf_op jit(solution)/shard_map/all_to_all | solution.py:48
  141.5 2.2 %collective-permute-done.22.come_ref = bf16[2,128,1024]{2,1,0:T(8,128)(2,1)} collective-permute-done((bf16[2,128,1024]{2,1,0:T(8,128)(2,1)}, bf16[2,128,1024]{2,1,0:T(8,128)(2,1)}, u32[]{:S(2)}, u32[]{:S(2)}) %collective-permute-start.22) | collective-permute-done | bytes 524320 | tf_op jit(solution)/shard_map/ppermute | solution.py:368
  143.7 2.1 %shard_map.101 = (f32[128,1024]{1,0:T(8,128)}, bf16[128,1024]{1,0:T(8,128)(2,1)}) custom-call(s32[8]{0:T(128)} %stack.65.place, bf16[2,128,1024]{2,1,0:T(8,128)(2,1)} %get-tuple-element.134.kept_ref, bf16[2,128,1024]{2,1,0:T(8,128)(2,1)} %collective-permute-done.22.come_ref), custom_call_target="tpu_custom_call" | custom-call | flops 1000000 | bytes 2000000 | tf_op jit(solution)/shard_map/pallas_call | solution.py:347
  145.8 2.0 %collective-permute-start.23 = (bf16[128,1024]{1,0:T(8,128)(2,1)}, bf16[128,1024]{1,0:T(8,128)(2,1)}, u32[]{:S(2)}, u32[]{:S(2)}) collective-permute-start(bf16[128,1024]{1,0:T(8,128)(2,1)} %get-tuple-element.137), channel_id=1, source_target_pairs={{0,2},{1,3},{2,0},{3,1},{4,6},{5,7},{6,4},{7,5},{8,10},{9,11},{10,... | collective-permute-start | bytes 786440 | tf_op jit(solution)/shard_map/ppermute | solution.py:368
  149.6 2.1 %collective-permute-start.19 = (bf16[128,128]{1,0:T(8,128)(2,1)}, bf16[128,128]{1,0:T(8,128)(2,1)}, u32[]{:S(2)}, u32[]{:S(2)}) collective-permute-start(bf16[128,128]{1,0:T(8,128)(2,1)} %get-tuple-element.130), channel_id=1, source_target_pairs={{0,96},{4,100},{8,104},{12,108},{16,112},{20,116},{24,120},{28,124... | collective-permute-start | bytes 98312 | tf_op jit(solution)/shard_map/ppermute | solution.py:52
  156.4 2.6 %collective-permute-done.21.e3 = bf16[128,128]{1,0:T(8,128)(2,1)} collective-permute-done((bf16[128,128]{1,0:T(8,128)(2,1)}, bf16[128,128]{1,0:T(8,128)(2,1)}, u32[]{:S(2)}, u32[]{:S(2)}) %collective-permute-start.21) | collective-permute-done | bytes 32800 | tf_op jit(solution)/shard_map/ppermute | solution.py:52
  159.0 2.6 %shard_map.102 = (bf16[128,1024]{1,0:T(8,128)(2,1)}, bf16[128,512]{1,0:T(8,128)(2,1)}, bf16[128,512]{1,0:T(8,128)(2,1)}, bf16[128,512]{1,0:T(8,128)(2,1)}, f32[64,512]{1,0:T(8,128)}) custom-call(s32[8]{0:T(128)} %stack.65.place, bf16[128,128]{1,0:T(8,128)(2,1)} %get-tuple-element.129.e0, bf16[128,128]{1,0:T(8,128)(2,1)} %collective-permute-done.19.e1, ...), custom_call_target="tpu_custom_call" | custom-call | flops 1000000 | bytes 3600000 | tf_op jit(solution)/shard_map/pallas_call | solution.py:347
  (40 shorter events, 22.3 us)
Async XLA Ops:
  0.6 17.2 %collective-permute-start.1 = (bf16[128,1024]{1,0:T(8,128)(2,1)}, bf16[128,1024]{1,0:T(8,128)(2,1)}, u32[]{:S(2)}, u32[]{:S(2)}) collective-permute-start(bf16[128,1024]{1,0:T(8,128)(2,1)} %c0.1), channel_id=1, source_target_pairs={{0,2},{1,3},{2,0},{3,1},{4,6},{5,7},{6,4},{7,5},{8,10},{9,11},{10,... | collective-permute-start | bytes 786440 | tf_op jit(solution)/shard_map/ppermute | solution.py:368
  6.5 5.3 %collective-permute-start.2 = (bf16[128,128]{1,0:T(8,128)(2,1)}, bf16[128,128]{1,0:T(8,128)(2,1)S(1)}, u32[]{:S(2)}, u32[]{:S(2)}) collective-permute-start(bf16[128,128]{1,0:T(8,128)(2,1)} %get-tuple-element.74), channel_id=1, source_target_pairs={{0,96},{4,100},{8,104},{12,108},{16,112},{20,116},{24,120},{28,124... | collective-permute-start | bytes 98312 | tf_op jit(solution)/shard_map/ppermute | solution.py:52
  9.5 4.1 %collective-permute-start.3 = (bf16[128,128]{1,0:T(8,128)(2,1)}, bf16[128,128]{1,0:T(8,128)(2,1)S(1)}, u32[]{:S(2)}, u32[]{:S(2)}) collective-permute-start(bf16[128,128]{1,0:T(8,128)(2,1)} %get-tuple-element.75), channel_id=1, source_target_pairs={{0,128},{4,132},{8,136},{12,140},{16,144},{20,148},{24,152},{28,15... | collective-permute-start | bytes 98312 | tf_op jit(solution)/shard_map/ppermute | solution.py:52
  10.1 6.2 %collective-permute-start.4 = (bf16[128,128]{1,0:T(8,128)(2,1)}, bf16[128,128]{1,0:T(8,128)(2,1)S(1)}, u32[]{:S(2)}, u32[]{:S(2)}) collective-permute-start(bf16[128,128]{1,0:T(8,128)(2,1)} %get-tuple-element.76), channel_id=1, source_target_pairs={{0,224},{4,228},{8,232},{12,236},{16,240},{20,244},{24,248},{28,25... | collective-permute-start | bytes 98312 | tf_op jit(solution)/shard_map/ppermute | solution.py:52
  17.8 32.7 %all-to-all-start = ((bf16[16,256,128]{2,1,0:T(8,128)(2,1)}), bf16[16,256,128]{2,1,0:T(8,128)(2,1)}, u32[]{:S(2)}, u32[]{:S(2)}) async-start(bf16[16,256,128]{2,1,0:T(8,128)(2,1)} %get-tuple-element.79), calls=%async_computation | async-start | bytes 2097152 | tf_op jit(solution)/shard_map/all_to_all | solution.py:48
  22.0 9.1 %collective-permute-start = (bf16[128,1024]{1,0:T(8,128)(2,1)}, bf16[128,1024]{1,0:T(8,128)(2,1)}, u32[]{:S(2)}, u32[]{:S(2)}) collective-permute-start(bf16[128,1024]{1,0:T(8,128)(2,1)} %c0.1), channel_id=1, source_target_pairs={{0,1},{1,0},{2,3},{3,2},{4,5},{5,4},{6,7},{7,6},{8,9},{9,8},{10,11... | collective-permute-start | bytes 786440 | tf_op jit(solution)/shard_map/ppermute | solution.py:368
  22.1 9.0 %collective-permute-start.5 = (bf16[128,1024]{1,0:T(8,128)(2,1)}, bf16[128,1024]{1,0:T(8,128)(2,1)}, u32[]{:S(2)}, u32[]{:S(2)}) collective-permute-start(bf16[128,1024]{1,0:T(8,128)(2,1)} %collective-permute-done.1.c2), channel_id=1, source_target_pairs={{0,1},{1,0},{2,3},{3,2},{4,5},{5,4},{6,7},{7,6},{8,9},{9,8},{10,11... | collective-permute-start | bytes 786440 | tf_op jit(solution)/shard_map/ppermute | solution.py:368
  22.6 17.7 %collective-permute-start.8 = (bf16[4,128,128]{2,1,0:T(8,128)(2,1)}, bf16[4,128,128]{2,1,0:T(8,128)(2,1)}, u32[]{:S(2)}, u32[]{:S(2)}) collective-permute-start(bf16[4,128,128]{2,1,0:T(8,128)(2,1)} %pad_maximum_fusion.1.qa), channel_id=1, source_target_pairs={{0,24},{4,28},{8,16},{12,20},{16,8},{20,12},{24,0},{28,4},{32,56},... | collective-permute-start | bytes 393224 | tf_op jit(solution)/shard_map/ppermute | solution.py:52
  28.8 21.7 %collective-permute-start.7 = (bf16[4,128,128]{2,1,0:T(8,128)(2,1)}, bf16[4,128,128]{2,1,0:T(8,128)(2,1)}, u32[]{:S(2)}, u32[]{:S(2)}) collective-permute-start(bf16[4,128,128]{2,1,0:T(8,128)(2,1)} %pad_maximum_fusion.1.qa), channel_id=1, source_target_pairs={{0,16},{4,20},{8,24},{12,28},{16,0},{20,4},{24,8},{28,12},{32,48},... | collective-permute-start | bytes 393224 | tf_op jit(solution)/shard_map/ppermute | solution.py:52
  29.7 20.8 %collective-permute-start.6 = (bf16[4,128,128]{2,1,0:T(8,128)(2,1)}, bf16[4,128,128]{2,1,0:T(8,128)(2,1)}, u32[]{:S(2)}, u32[]{:S(2)}) collective-permute-start(bf16[4,128,128]{2,1,0:T(8,128)(2,1)} %pad_maximum_fusion.1.qa), channel_id=1, source_target_pairs={{0,8},{4,12},{8,0},{12,4},{16,24},{20,28},{24,16},{28,20},{32,40},... | collective-permute-start | bytes 393224 | tf_op jit(solution)/shard_map/ppermute | solution.py:52
  50.5 21.5 %all-to-all-start.1 = ((bf16[16,128,128]{2,1,0:T(8,128)(2,1)}), bf16[16,128,128]{2,1,0:T(8,128)(2,1)}, u32[]{:S(2)}, u32[]{:S(2)}) async-start(bf16[16,128,128]{2,1,0:T(8,128)(2,1)} %get-tuple-element.85), calls=%async_computation.1 | async-start | bytes 1048576 | tf_op jit(solution)/shard_map/all_to_all | solution.py:48
  74.4 21.6 %all-to-all-start.2 = ((bf16[8,128,512]{2,1,0:T(8,128)(2,1)}), bf16[8,128,512]{2,1,0:T(8,128)(2,1)}, u32[]{:S(2)}, u32[]{:S(2)}) async-start(bf16[8,128,512]{2,1,0:T(8,128)(2,1)} %get-tuple-element.101), calls=%async_computation.2 | async-start | bytes 2097152 | tf_op jit(solution)/shard_map/all_to_all | solution.py:48
  78.7 6.7 %collective-permute-start.9 = (bf16[608,128]{1,0:T(8,128)(2,1)}, bf16[608,128]{1,0:T(8,128)(2,1)}, u32[]{:S(2)}, u32[]{:S(2)}) collective-permute-start(bf16[608,128]{1,0:T(8,128)(2,1)} %get-tuple-element.98), channel_id=1, source_target_pairs={{0,8},{4,12},{8,0},{12,4},{16,24},{20,28},{24,16},{28,20},{32,40},... | collective-permute-start | bytes 466952 | tf_op jit(solution)/shard_map/ppermute | solution.py:52
  79.1 10.2 %collective-permute-start.10 = (bf16[608,128]{1,0:T(8,128)(2,1)}, bf16[608,128]{1,0:T(8,128)(2,1)}, u32[]{:S(2)}, u32[]{:S(2)}) collective-permute-start(bf16[608,128]{1,0:T(8,128)(2,1)} %get-tuple-element.99), channel_id=1, source_target_pairs={{0,16},{4,20},{8,24},{12,28},{16,0},{20,4},{24,8},{28,12},{32,48},... | collective-permute-start | bytes 466952 | tf_op jit(solution)/shard_map/ppermute | solution.py:52
  80.0 13.8 %collective-permute-start.11 = (bf16[608,128]{1,0:T(8,128)(2,1)}, bf16[608,128]{1,0:T(8,128)(2,1)}, u32[]{:S(2)}, u32[]{:S(2)}) collective-permute-start(bf16[608,128]{1,0:T(8,128)(2,1)} %get-tuple-element.100), channel_id=1, source_target_pairs={{0,24},{4,28},{8,16},{12,20},{16,8},{20,12},{24,0},{28,4},{32,56},... | collective-permute-start | bytes 466952 | tf_op jit(solution)/shard_map/ppermute | solution.py:52
  96.0 14.4 %collective-permute-start.17 = (bf16[4,128,128]{2,1,0:T(8,128)(2,1)}, bf16[4,128,128]{2,1,0:T(8,128)(2,1)}, u32[]{:S(2)}, u32[]{:S(2)}) collective-permute-start(bf16[4,128,128]{2,1,0:T(8,128)(2,1)} %shard_map.96.a0), channel_id=1, source_target_pairs={{0,224},{4,228},{8,232},{12,236},{16,240},{20,244},{24,248},{28,25... | collective-permute-start | bytes 393224 | tf_op jit(solution)/shard_map/ppermute | solution.py:52
  100.0 10.4 %collective-permute-start.16 = (bf16[4,128,128]{2,1,0:T(8,128)(2,1)}, bf16[4,128,128]{2,1,0:T(8,128)(2,1)}, u32[]{:S(2)}, u32[]{:S(2)}) collective-permute-start(bf16[4,128,128]{2,1,0:T(8,128)(2,1)} %shard_map.96.a0), channel_id=1, source_target_pairs={{0,128},{4,132},{8,136},{12,140},{16,144},{20,148},{24,152},{28,15... | collective-permute-start | bytes 393224 | tf_op jit(solution)/shard_map/ppermute | solution.py:52
  100.5 9.9 %collective-permute-start.15 = (bf16[4,128,128]{2,1,0:T(8,128)(2,1)}, bf16[4,128,128]{2,1,0:T(8,128)(2,1)}, u32[]{:S(2)}, u32[]{:S(2)}) collective-permute-start(bf16[4,128,128]{2,1,0:T(8,128)(2,1)} %shard_map.96.a0), channel_id=1, source_target_pairs={{0,96},{4,100},{8,104},{12,108},{16,112},{20,116},{24,120},{28,124... | collective-permute-start | bytes 393224 | tf_op jit(solution)/shard_map/ppermute | solution.py:52
  110.4 24.8 %all-to-all-start.3 = ((bf16[16,256,128]{2,1,0:T(8,128)(2,1)}), bf16[16,256,128]{2,1,0:T(8,128)(2,1)}, u32[]{:S(2)}, u32[]{:S(2)}) async-start(bf16[16,256,128]{2,1,0:T(8,128)(2,1)} %get-tuple-element.120), calls=%async_computation.3 | async-start | bytes 2097152 | tf_op jit(solution)/shard_map/all_to_all | solution.py:48
  119.1 12.7 %collective-permute-start.18 = (bf16[4,4,128,128]{3,2,1,0:T(8,128)(2,1)}, bf16[4,4,128,128]{3,2,1,0:T(8,128)(2,1)}, u32[]{:S(2)}, u32[]{:S(2)}) collective-permute-start(bf16[4,4,128,128]{3,2,1,0:T(8,128)(2,1)} %pad_maximum_fusion), channel_id=1, source_target_pairs={{0,32},{4,36},{8,40},{12,44},{16,48},{20,52},{24,56},{28,60},{32,0... | collective-permute-start | bytes 1572872 | tf_op jit(solution)/shard_map/ppermute | solution.py:52
  120.5 14.6 %collective-permute-start.12 = (bf16[4,128,128]{2,1,0:T(8,128)(2,1)}, bf16[4,128,128]{2,1,0:T(8,128)(2,1)}, u32[]{:S(2)}, u32[]{:S(2)}) collective-permute-start(bf16[4,128,128]{2,1,0:T(8,128)(2,1)} %get-tuple-element.107), channel_id=1, source_target_pairs={{0,8},{4,12},{8,0},{12,4},{16,24},{20,28},{24,16},{28,20},{32,40},... | collective-permute-start | bytes 393224 | tf_op jit(solution)/shard_map/ppermute | solution.py:52
  121.4 13.8 %collective-permute-start.13 = (bf16[4,128,128]{2,1,0:T(8,128)(2,1)}, bf16[4,128,128]{2,1,0:T(8,128)(2,1)}, u32[]{:S(2)}, u32[]{:S(2)}) collective-permute-start(bf16[4,128,128]{2,1,0:T(8,128)(2,1)} %get-tuple-element.108), channel_id=1, source_target_pairs={{0,16},{4,20},{8,24},{12,28},{16,0},{20,4},{24,8},{28,12},{32,48},... | collective-permute-start | bytes 393224 | tf_op jit(solution)/shard_map/ppermute | solution.py:52
  123.5 11.7 %collective-permute-start.14 = (bf16[4,128,128]{2,1,0:T(8,128)(2,1)}, bf16[4,128,128]{2,1,0:T(8,128)(2,1)}, u32[]{:S(2)}, u32[]{:S(2)}) collective-permute-start(bf16[4,128,128]{2,1,0:T(8,128)(2,1)} %get-tuple-element.109), channel_id=1, source_target_pairs={{0,24},{4,28},{8,16},{12,20},{16,8},{20,12},{24,0},{28,4},{32,56},... | collective-permute-start | bytes 393224 | tf_op jit(solution)/shard_map/ppermute | solution.py:52
  135.2 23.8 %all-to-all-start.4 = ((bf16[8,64,512]{2,1,0:T(8,128)(2,1)}), bf16[8,64,512]{2,1,0:T(8,128)(2,1)}, u32[]{:S(2)}, u32[]{:S(2)}) async-start(bf16[8,64,512]{2,1,0:T(8,128)(2,1)} %shard_map.98), calls=%async_computation.4 | async-start | bytes 1048576 | tf_op jit(solution)/shard_map/all_to_all | solution.py:48
  141.5 2.3 %collective-permute-start.22 = (bf16[2,128,1024]{2,1,0:T(8,128)(2,1)}, bf16[2,128,1024]{2,1,0:T(8,128)(2,1)}, u32[]{:S(2)}, u32[]{:S(2)}) collective-permute-start(bf16[2,128,1024]{2,1,0:T(8,128)(2,1)} %get-tuple-element.135), channel_id=1, source_target_pairs={{0,1},{1,0},{2,3},{3,2},{4,5},{5,4},{6,7},{7,6},{8,9},{9,8},{10,11... | collective-permute-start | bytes 1572872 | tf_op jit(solution)/shard_map/ppermute | solution.py:368
  145.8 10.3 %collective-permute-start.23 = (bf16[128,1024]{1,0:T(8,128)(2,1)}, bf16[128,1024]{1,0:T(8,128)(2,1)}, u32[]{:S(2)}, u32[]{:S(2)}) collective-permute-start(bf16[128,1024]{1,0:T(8,128)(2,1)} %get-tuple-element.137), channel_id=1, source_target_pairs={{0,2},{1,3},{2,0},{3,1},{4,6},{5,7},{6,4},{7,5},{8,10},{9,11},{10,... | collective-permute-start | bytes 786440 | tf_op jit(solution)/shard_map/ppermute | solution.py:368
  149.6 6.5 %collective-permute-start.19 = (bf16[128,128]{1,0:T(8,128)(2,1)}, bf16[128,128]{1,0:T(8,128)(2,1)}, u32[]{:S(2)}, u32[]{:S(2)}) collective-permute-start(bf16[128,128]{1,0:T(8,128)(2,1)} %get-tuple-element.130), channel_id=1, source_target_pairs={{0,96},{4,100},{8,104},{12,108},{16,112},{20,116},{24,120},{28,124... | collective-permute-start | bytes 98312 | tf_op jit(solution)/shard_map/ppermute | solution.py:52
  151.7 4.7 %collective-permute-start.20 = (bf16[128,128]{1,0:T(8,128)(2,1)}, bf16[128,128]{1,0:T(8,128)(2,1)}, u32[]{:S(2)}, u32[]{:S(2)}) collective-permute-start(bf16[128,128]{1,0:T(8,128)(2,1)} %get-tuple-element.131), channel_id=1, source_target_pairs={{0,128},{4,132},{8,136},{12,140},{16,144},{20,148},{24,152},{28,15... | collective-permute-start | bytes 98312 | tf_op jit(solution)/shard_map/ppermute | solution.py:52
  152.6 6.3 %collective-permute-start.21 = (bf16[128,128]{1,0:T(8,128)(2,1)}, bf16[128,128]{1,0:T(8,128)(2,1)}, u32[]{:S(2)}, u32[]{:S(2)}) collective-permute-start(bf16[128,128]{1,0:T(8,128)(2,1)} %get-tuple-element.132), channel_id=1, source_target_pairs={{0,224},{4,228},{8,232},{12,236},{16,240},{20,244},{24,248},{28,25... | collective-permute-start | bytes 98312 | tf_op jit(solution)/shard_map/ppermute | solution.py:52

commit v4 on v3

--- a/solution.py
+++ b/solution.py
@@ -259,10 +259,7 @@
         out[...] = sum(part[p].astype(F32) for part in (d0, d1, d2, d3)).astype(BF16)
 
 
-def last_kernel(
-    place, e0, e1, e2, e3, dkv_ref, mine_ref, far_ref, proj_ref,
-    layer_ref, dq_ref, dk_ref, dv_ref, sum_ref
-):
+def grads_kernel(place, e0, e1, e2, e3, dkv_ref, dq_ref, dk_ref, dv_ref):
     for x, part in enumerate((e0, e1, e2, e3)):
         dq_ref[:, block_at(place[0] ^ x)] = part[...]
     for h in range(4):
@@ -270,8 +267,6 @@
         at = slice(h * HEAD, (h + 1) * HEAD)
         dk_ref[:, at] = total[:BLK]
         dv_ref[:, at] = total[BLK:]
-    layer_ref[...] = (mine_ref[...] + far_ref[...].astype(F32)).astype(BF16)
-    sum_ref[...] = sum(proj_ref[i].astype(F32) for i in range(8))
 
 
 def layer_kernel(
@@ -465,13 +460,11 @@
     proj_home = exchange(proj_part, z_groups())
     dq_pieces = on_device(dq_sum_kernel, four, [], 1e6, 6e5)(place, *dq_all)
     dq_home = over_heads(dq_pieces)
-    layer_out, grad_query, grad_key, grad_value, proj_grad = on_device(
-        last_kernel,
-        [like(BLK, 1024)] + [like(BLK, 512)] * 3 + [like(64, 512, dtype=F32)],
-        [],
-        1e6,
-        3.6e6,
-    )(place, *dq_home, dkv_home, mine, swap(other, 2), proj_home)
+    layer_out = (mine + swap(other, 2).astype(F32)).astype(BF16)
+    grad_query, grad_key, grad_value = on_device(
+        grads_kernel, [like(BLK, 512)] * 3, [], 1e6, 1.6e6
+    )(place, *dq_home, dkv_home)
+    proj_grad = jnp.sum(proj_home.astype(F32), axis=0)
     return (layer_out, grad_query, grad_key, grad_value, proj_grad)
 
 

time: 162 us -> 161 us (level)
  waiting for transfers between devices: 43.5 us -> 39.2 us
  other arithmetic: 3.38 us -> 7.02 us
    ppermute x5, waiting for transfers between devices: 4.06 us -> 0.23 us  [swap(): return lax.ppermute(block, 'fsdp', [(i, i ^ x) for i in range(4)])]
    convert_element_type x0 -> x1, other arithmetic: none -> 1.87 us  [per_device(): layer_out = (mine + swap(other, 2).astype(F32)).astype(BF16)]
    reduce_sum x0 -> x1, other arithmetic: none -> 1.78 us  [per_device(): proj_grad = jnp.sum(proj_home.astype(F32), axis=0)]
  transfers between devices with their start and end apart: 29 -> 29, of which waited for: 14 -> 12; matrix products, arithmetic and copies ran while one was open for 2% -> 4% of each run, Pallas kernels for 23% -> 25%
where the time goes in v4:
time: 161 us
  starting transfers between devices  70.5 us (44%)
  Pallas kernels  42.6 us (26%)
  waiting for transfers between devices  39.2 us (24%)
  other arithmetic  7.02 us (4%)
    pallas_call x11, Pallas kernels, call(): pl.pallas_call(kernel, out_shape=out_shape, in_specs=[pl.BlockSpec(memory...  42.6 us
    ppermute x19, starting transfers between devices, hop(): return lax.ppermute(block, 'ctx', [(i, i ^ step) for i in range(64)])  37.1 us
    ppermute x19, waiting for transfers between devices, hop(): return lax.ppermute(block, 'ctx', [(i, i ^ step) for i in range(64)])  30.6 us
    all_to_all x5, starting transfers between devices, exchange(): lax.all_to_all(pieces, 'ctx', 0, 0, axis_index_groups=groups, tiled=True)  27.5 us
    all_to_all x5, waiting for transfers between devices, exchange(): lax.all_to_all(pieces, 'ctx', 0, 0, axis_index_groups=groups, tiled=True)  8.33 us
    ppermute x5, starting transfers between devices, swap(): return lax.ppermute(block, 'fsdp', [(i, i ^ x) for i in range(4)])  5.8 us
  transfers between devices with their start and end apart: 29, of which 12 were waited for; matrix products, arithmetic and copies ran while one was open for 4% of the time, Pallas kernels for 25%

profile of v4, /device:TPU:32, one launch (start us, length us, event | category | flops | bytes accessed | tf_op | source)
XLA Modules:
  0.0 160.6 jit_solution(17010745385548620921)
XLA Ops:
  0.6 3.1 %collective-permute-start.1 = (bf16[128,1024]{1,0:T(8,128)(2,1)}, bf16[128,1024]{1,0:T(8,128)(2,1)}, u32[]{:S(2)}, u32[]{:S(2)}) collective-permute-start(bf16[128,1024]{1,0:T(8,128)(2,1)} %c0.1), channel_id=1, source_target_pairs={{0,2},{1,3},{2,0},{3,1},{4,6},{5,7},{6,4},{7,5},{8,10},{9,11},{10,... | collective-permute-start | bytes 786440 | tf_op jit(solution)/shard_map/ppermute | solution.py:363
  4.3 2.2 %shard_map.92 = (bf16[128,128]{1,0:T(8,128)(2,1)}, bf16[128,128]{1,0:T(8,128)(2,1)}, bf16[128,128]{1,0:T(8,128)(2,1)}, bf16[128,128]{1,0:T(8,128)(2,1)}, bf16[16,256,128]{2,1,0:T(8,128)(2,1)}) custom-call(s32[8]{0:T(128)} %stack.65.place, bf16[128,512]{1,0:T(8,128)(2,1)} %q_ref.1, bf16[128,512]{1,0:T(8,128)(2,1)} %k_ref.1, bf16[128,512]{1,0:T(8,128)(2,1)} %v_ref.1), custom_call_target="tpu_custom_call" | custom-call | flops 1000000 | bytes 2000000 | tf_op jit(solution)/shard_map/pallas_call | solution.py:342
  6.5 3.0 %collective-permute-start.2 = (bf16[128,128]{1,0:T(8,128)(2,1)}, bf16[128,128]{1,0:T(8,128)(2,1)S(1)}, u32[]{:S(2)}, u32[]{:S(2)}) collective-permute-start(bf16[128,128]{1,0:T(8,128)(2,1)} %get-tuple-element.77), channel_id=1, source_target_pairs={{0,96},{4,100},{8,104},{12,108},{16,112},{20,116},{24,120},{28,124... | collective-permute-start | bytes 98312 | tf_op jit(solution)/shard_map/ppermute | solution.py:52
  13.6 2.7 %collective-permute-done.4 = bf16[128,128]{1,0:T(8,128)(2,1)S(1)} collective-permute-done((bf16[128,128]{1,0:T(8,128)(2,1)}, bf16[128,128]{1,0:T(8,128)(2,1)S(1)}, u32[]{:S(2)}, u32[]{:S(2)}) %collective-permute-start.4) | collective-permute-done | bytes 32800 | tf_op jit(solution)/shard_map/ppermute | solution.py:52
  17.8 4.2 %all-to-all-start = ((bf16[16,256,128]{2,1,0:T(8,128)(2,1)}), bf16[16,256,128]{2,1,0:T(8,128)(2,1)}, u32[]{:S(2)}, u32[]{:S(2)}) async-start(bf16[16,256,128]{2,1,0:T(8,128)(2,1)} %get-tuple-element.82), calls=%async_computation | async-start | bytes 2097152 | tf_op jit(solution)/shard_map/all_to_all | solution.py:48
  22.6 6.1 %collective-permute-start.8 = (bf16[4,128,128]{2,1,0:T(8,128)(2,1)}, bf16[4,128,128]{2,1,0:T(8,128)(2,1)}, u32[]{:S(2)}, u32[]{:S(2)}) collective-permute-start(bf16[4,128,128]{2,1,0:T(8,128)(2,1)} %pad_maximum_fusion.1.qa), channel_id=1, source_target_pairs={{0,24},{4,28},{8,16},{12,20},{16,8},{20,12},{24,0},{28,4},{32,56},... | collective-permute-start | bytes 393224 | tf_op jit(solution)/shard_map/ppermute | solution.py:52
  31.1 4.9 %shard_map.93 = (bf16[16,128,128]{2,1,0:T(8,128)(2,1)}, bf16[8,128,512]{2,1,0:T(8,128)(2,1)}) custom-call(s32[8]{0:T(128)} %stack.65.place, bf16[128,1024]{1,0:T(8,128)(2,1)} %c0.1, bf16[128,1024]{1,0:T(8,128)(2,1)} %collective-permute-done.c1, bf16[128,1024]{1,0:T(8,128)(2,1)} %collective-permute-done.1.c2, bf16[128,1024]{1,0:T(8,128)(2,1)} %collective-permute-done.5.c3, ...), custom_call_target="tpu_custom_call" | custom-call | flops 540000000 | bytes 7000000 | tf_op jit(solution)/shard_map/pallas_call | solution.py:326
  36.1 4.2 %collective-permute-done.8.qd = bf16[4,128,128]{2,1,0:T(8,128)(2,1)} collective-permute-done((bf16[4,128,128]{2,1,0:T(8,128)(2,1)}, bf16[4,128,128]{2,1,0:T(8,128)(2,1)}, u32[]{:S(2)}, u32[]{:S(2)}) %collective-permute-start.8) | collective-permute-done | bytes 131104 | tf_op jit(solution)/shard_map/ppermute | solution.py:52
  40.3 10.2 %collective-permute-done.7.qc = bf16[4,128,128]{2,1,0:T(8,128)(2,1)} collective-permute-done((bf16[4,128,128]{2,1,0:T(8,128)(2,1)}, bf16[4,128,128]{2,1,0:T(8,128)(2,1)}, u32[]{:S(2)}, u32[]{:S(2)}) %collective-permute-start.7) | collective-permute-done | bytes 131104 | tf_op jit(solution)/shard_map/ppermute | solution.py:52
  50.4 6.0 %all-to-all-start.1 = ((bf16[16,128,128]{2,1,0:T(8,128)(2,1)}), bf16[16,128,128]{2,1,0:T(8,128)(2,1)}, u32[]{:S(2)}, u32[]{:S(2)}) async-start(bf16[16,128,128]{2,1,0:T(8,128)(2,1)} %get-tuple-element.88), calls=%async_computation.1 | async-start | bytes 1048576 | tf_op jit(solution)/shard_map/all_to_all | solution.py:48
  56.5 7.2 %shard_map.94 = (bf16[4,128,128]{2,1,0:T(8,128)(2,1)}, bf16[4,128,128]{2,1,0:T(8,128)(2,1)}, bf16[4,128,128]{2,1,0:T(8,128)(2,1)}, bf16[4,128,128]{2,1,0:T(8,128)(2,1)}, f32[16,128]{1,0:T(8,128)}) custom-call(s32[8]{0:T(128)} %stack.65.place, bf16[4,128,128]{2,1,0:T(8,128)(2,1)} %pad_maximum_fusion.1.qa, bf16[4,128,128]{2,1,0:T(8,128)(2,1)} %collective-permute-done.6.qb, ...), custom_call_target="tpu_custom_call" | custom-call | flops 2000000000 | bytes 2600000 | tf_op jit(solution)/shard_map/pallas_call | solution.py:342
  63.6 8.3 %all-to-all-done.1.do_ref = bf16[16,128,128]{2,1,0:T(8,128)(2,1)} async-done(((bf16[16,128,128]{2,1,0:T(8,128)(2,1)}), bf16[16,128,128]{2,1,0:T(8,128)(2,1)}, u32[]{:S(2)}, u32[]{:S(2)}) %all-to-all-start.1) | async-done | bytes 524320 | tf_op jit(solution)/shard_map/all_to_all | solution.py:48
  71.9 2.5 %shard_map.95 = (bf16[608,128]{1,0:T(8,128)(2,1)}, bf16[608,128]{1,0:T(8,128)(2,1)}, bf16[608,128]{1,0:T(8,128)(2,1)}, bf16[608,128]{1,0:T(8,128)(2,1)}) custom-call(s32[8]{0:T(128)} %stack.65.place, bf16[16,128,128]{2,1,0:T(8,128)(2,1)} %all-to-all-done.1.do_ref, bf16[4,128,128]{2,1,0:T(8,128)(2,1)} %get-tuple-element.90.o0, ...), custom_call_target="tpu_custom_call" | custom-call | flops 1000000 | bytes 1600000 | tf_op jit(solution)/shard_map/pallas_call | solution.py:342
  74.4 4.3 %all-to-all-start.2 = ((bf16[8,128,512]{2,1,0:T(8,128)(2,1)}), bf16[8,128,512]{2,1,0:T(8,128)(2,1)}, u32[]{:S(2)}, u32[]{:S(2)}) async-start(bf16[8,128,512]{2,1,0:T(8,128)(2,1)} %get-tuple-element.104), calls=%async_computation.2 | async-start | bytes 2097152 | tf_op jit(solution)/shard_map/all_to_all | solution.py:48
  79.9 5.3 %collective-permute-start.11 = (bf16[608,128]{1,0:T(8,128)(2,1)}, bf16[608,128]{1,0:T(8,128)(2,1)}, u32[]{:S(2)}, u32[]{:S(2)}) collective-permute-start(bf16[608,128]{1,0:T(8,128)(2,1)} %get-tuple-element.103), channel_id=1, source_target_pairs={{0,24},{4,28},{8,16},{12,20},{16,8},{20,12},{24,0},{28,4},{32,56},... | collective-permute-start | bytes 466952 | tf_op jit(solution)/shard_map/ppermute | solution.py:52
  85.4 3.9 %collective-permute-done.10.p2 = bf16[608,128]{1,0:T(8,128)(2,1)} collective-permute-done((bf16[608,128]{1,0:T(8,128)(2,1)}, bf16[608,128]{1,0:T(8,128)(2,1)}, u32[]{:S(2)}, u32[]{:S(2)}) %collective-permute-start.10) | collective-permute-done | bytes 155680 | tf_op jit(solution)/shard_map/ppermute | solution.py:52
  89.3 4.4 %collective-permute-done.11.p3 = bf16[608,128]{1,0:T(8,128)(2,1)} collective-permute-done((bf16[608,128]{1,0:T(8,128)(2,1)}, bf16[608,128]{1,0:T(8,128)(2,1)}, u32[]{:S(2)}, u32[]{:S(2)}) %collective-permute-start.11) | collective-permute-done | bytes 155680 | tf_op jit(solution)/shard_map/ppermute | solution.py:52
  93.8 2.2 %shard_map.96.a0 = bf16[4,128,128]{2,1,0:T(8,128)(2,1)} custom-call(s32[8]{0:T(128)} %stack.65.place, bf16[608,128]{1,0:T(8,128)(2,1)} %get-tuple-element.105.p0, bf16[608,128]{1,0:T(8,128)(2,1)} %collective-permute-done.9.p1, bf16[608,128]{1,0:T(8,128)(2,1)} %collective-permute-done.10.p2, bf16[608,128]{1,0:T(8,128)(2,1)} %collective-permute-done.11.p3), custom_call_target="tpu_custom_call" | custom-call | flops 1000000 | bytes 700000 | tf_op jit(solution)/shard_map/pallas_call | solution.py:342
  96.0 4.0 %collective-permute-start.17 = (bf16[4,128,128]{2,1,0:T(8,128)(2,1)}, bf16[4,128,128]{2,1,0:T(8,128)(2,1)}, u32[]{:S(2)}, u32[]{:S(2)}) collective-permute-start(bf16[4,128,128]{2,1,0:T(8,128)(2,1)} %shard_map.96.a0), channel_id=1, source_target_pairs={{0,224},{4,228},{8,232},{12,236},{16,240},{20,244},{24,248},{28,25... | collective-permute-start | bytes 393224 | tf_op jit(solution)/shard_map/ppermute | solution.py:52
  100.7 9.7 %shard_map.97 = (bf16[4,128,128]{2,1,0:T(8,128)(2,1)}, bf16[4,128,128]{2,1,0:T(8,128)(2,1)}, bf16[4,128,128]{2,1,0:T(8,128)(2,1)}, bf16[4,128,128]{2,1,0:T(8,128)(2,1)}, bf16[16,256,128]{2,1,0:T(8,128)(2,1)}) custom-call(s32[8]{0:T(128)} %stack.65.place, bf16[4,128,128]{2,1,0:T(8,128)(2,1)} %pad_maximum_fusion.1.qa, ...), custom_call_target="tpu_custom_call" | custom-call | flops 5000000000 | bytes 3600000 | tf_op jit(solution)/shard_map/pallas_call | solution.py:342
  110.4 6.7 %all-to-all-start.3 = ((bf16[16,256,128]{2,1,0:T(8,128)(2,1)}), bf16[16,256,128]{2,1,0:T(8,128)(2,1)}, u32[]{:S(2)}, u32[]{:S(2)}) async-start(bf16[16,256,128]{2,1,0:T(8,128)(2,1)} %get-tuple-element.127), calls=%async_computation.3 | async-start | bytes 2097152 | tf_op jit(solution)/shard_map/all_to_all | solution.py:48
  117.1 1.9 %pad_maximum_fusion = bf16[4,4,128,128]{3,2,1,0:T(8,128)(2,1)} fusion(bf16[1,4,128,128]{3,2,1,0:T(8,128)(2,1)} %bitcast.15, bf16[1,4,128,128]{3,2,1,0:T(8,128)(2,1)} %bitcast.14, bf16[1,4,128,128]{3,2,1,0:T(8,128)(2,1)} %bitcast.13, bf16[1,4,128,128]{3,2,1,0:T(8,128)(2,1)} %bitcast.16), kind=kLoop, calls=%fused_computation.1 | loop fusion | flops 786432 | bytes 1048576 | tf_op jit(solution)/shard_map/stack | solution.py:451
  121.4 2.1 %collective-permute-start.13 = (bf16[4,128,128]{2,1,0:T(8,128)(2,1)}, bf16[4,128,128]{2,1,0:T(8,128)(2,1)}, u32[]{:S(2)}, u32[]{:S(2)}) collective-permute-start(bf16[4,128,128]{2,1,0:T(8,128)(2,1)} %get-tuple-element.111), channel_id=1, source_target_pairs={{0,16},{4,20},{8,24},{12,28},{16,0},{20,4},{24,8},{28,12},{32,48},... | collective-permute-start | bytes 393224 | tf_op jit(solution)/shard_map/ppermute | solution.py:52
  123.5 3.5 %collective-permute-start.14 = (bf16[4,128,128]{2,1,0:T(8,128)(2,1)}, bf16[4,128,128]{2,1,0:T(8,128)(2,1)}, u32[]{:S(2)}, u32[]{:S(2)}) collective-permute-start(bf16[4,128,128]{2,1,0:T(8,128)(2,1)} %get-tuple-element.112), channel_id=1, source_target_pairs={{0,24},{4,28},{8,16},{12,20},{16,8},{20,12},{24,0},{28,4},{32,56},... | collective-permute-start | bytes 393224 | tf_op jit(solution)/shard_map/ppermute | solution.py:52
  127.0 4.6 %shard_map.99 = (bf16[2,128,1024]{2,1,0:T(8,128)(2,1)}, bf16[2,128,1024]{2,1,0:T(8,128)(2,1)}) custom-call(s32[8]{0:T(128)} %stack.65.place, bf16[4,128,128]{2,1,0:T(8,128)(2,1)} %shard_map.96.a0, bf16[4,128,128]{2,1,0:T(8,128)(2,1)} %collective-permute-done.15.a1, bf16[4,128,128]{2,1,0:T(8,128)(2,1)} %collective-permute-done.16.a2, ...), custom_call_target="tpu_custom_call" | custom-call | flops 540000000 | bytes 6000000 | tf_op jit(solution)/shard_map/pallas_call | solution.py:326
  131.8 3.4 %shard_map.98 = bf16[8,64,512]{2,1,0:T(8,128)(2,1)} custom-call(s32[8]{0:T(128)} %stack.65.place, bf16[4,128,128]{2,1,0:T(8,128)(2,1)} %shard_map.96.a0, bf16[4,128,128]{2,1,0:T(8,128)(2,1)} %collective-permute-done.15.a1, bf16[4,128,128]{2,1,0:T(8,128)(2,1)} %collective-permute-done.16.a2, bf16[4,128,128]{2,1,0:T(8,128)(2,1)} %collective-permute-done.17.a3, ...), custom_call_target="tpu_custom_call" | custom-call | flops 540000000 | bytes 2600000 | tf_op jit(solution)/shard_map/pallas_call | solution.py:342
  135.2 6.3 %all-to-all-start.4 = ((bf16[8,64,512]{2,1,0:T(8,128)(2,1)}), bf16[8,64,512]{2,1,0:T(8,128)(2,1)}, u32[]{:S(2)}, u32[]{:S(2)}) async-start(bf16[8,64,512]{2,1,0:T(8,128)(2,1)} %shard_map.98), calls=%async_computation.4 | async-start | bytes 1048576 | tf_op jit(solution)/shard_map/all_to_all | solution.py:48
  141.4 2.1 %shard_map.100 = (f32[128,1024]{1,0:T(8,128)}, bf16[128,1024]{1,0:T(8,128)(2,1)}) custom-call(s32[8]{0:T(128)} %stack.65.place, bf16[2,128,1024]{2,1,0:T(8,128)(2,1)} %get-tuple-element.122.kept_ref, bf16[2,128,1024]{2,1,0:T(8,128)(2,1)} %collective-permute-done.19.come_ref), custom_call_target="tpu_custom_call" | custom-call | flops 1000000 | bytes 2000000 | tf_op jit(solution)/shard_map/pallas_call | solution.py:342
  143.6 2.0 %collective-permute-start.20 = (bf16[128,1024]{1,0:T(8,128)(2,1)}, bf16[128,1024]{1,0:T(8,128)(2,1)}, u32[]{:S(2)}, u32[]{:S(2)}) collective-permute-start(bf16[128,1024]{1,0:T(8,128)(2,1)} %get-tuple-element.125), channel_id=1, source_target_pairs={{0,2},{1,3},{2,0},{3,1},{4,6},{5,7},{6,4},{7,5},{8,10},{9,11},{10,... | collective-permute-start | bytes 786440 | tf_op jit(solution)/shard_map/ppermute | solution.py:363
  147.4 2.1 %collective-permute-start.21 = (bf16[128,128]{1,0:T(8,128)(2,1)}, bf16[128,128]{1,0:T(8,128)(2,1)}, u32[]{:S(2)}, u32[]{:S(2)}) collective-permute-start(bf16[128,128]{1,0:T(8,128)(2,1)} %get-tuple-element.137), channel_id=1, source_target_pairs={{0,96},{4,100},{8,104},{12,108},{16,112},{20,116},{24,120},{28,124... | collective-permute-start | bytes 98312 | tf_op jit(solution)/shard_map/ppermute | solution.py:52
  154.2 2.5 %collective-permute-done.23.e3 = bf16[128,128]{1,0:T(8,128)(2,1)} collective-permute-done((bf16[128,128]{1,0:T(8,128)(2,1)}, bf16[128,128]{1,0:T(8,128)(2,1)}, u32[]{:S(2)}, u32[]{:S(2)}) %collective-permute-start.23) | collective-permute-done | bytes 32800 | tf_op jit(solution)/shard_map/ppermute | solution.py:52
  156.7 2.1 %shard_map.102 = (bf16[128,512]{1,0:T(8,128)(2,1)}, bf16[128,512]{1,0:T(8,128)(2,1)}, bf16[128,512]{1,0:T(8,128)(2,1)}) custom-call(s32[8]{0:T(128)} %stack.65.place, bf16[128,128]{1,0:T(8,128)(2,1)} %get-tuple-element.136.e0, bf16[128,128]{1,0:T(8,128)(2,1)} %collective-permute-done.21.e1, bf16[128,128]{1,0:T(8,128)(2,1)} %collective-permute-done.22.e2, ...), custom_call_target="tpu_custom_call" | custom-call | flops 1000000 | bytes 1600000 | tf_op jit(solution)/shard_map/pallas_call | solution.py:342
  (42 shorter events, 22.1 us)
Async XLA Ops:
  0.6 17.1 %collective-permute-start.1 = (bf16[128,1024]{1,0:T(8,128)(2,1)}, bf16[128,1024]{1,0:T(8,128)(2,1)}, u32[]{:S(2)}, u32[]{:S(2)}) collective-permute-start(bf16[128,1024]{1,0:T(8,128)(2,1)} %c0.1), channel_id=1, source_target_pairs={{0,2},{1,3},{2,0},{3,1},{4,6},{5,7},{6,4},{7,5},{8,10},{9,11},{10,... | collective-permute-start | bytes 786440 | tf_op jit(solution)/shard_map/ppermute | solution.py:363
  6.5 5.3 %collective-permute-start.2 = (bf16[128,128]{1,0:T(8,128)(2,1)}, bf16[128,128]{1,0:T(8,128)(2,1)S(1)}, u32[]{:S(2)}, u32[]{:S(2)}) collective-permute-start(bf16[128,128]{1,0:T(8,128)(2,1)} %get-tuple-element.77), channel_id=1, source_target_pairs={{0,96},{4,100},{8,104},{12,108},{16,112},{20,116},{24,120},{28,124... | collective-permute-start | bytes 98312 | tf_op jit(solution)/shard_map/ppermute | solution.py:52
  9.5 4.1 %collective-permute-start.3 = (bf16[128,128]{1,0:T(8,128)(2,1)}, bf16[128,128]{1,0:T(8,128)(2,1)S(1)}, u32[]{:S(2)}, u32[]{:S(2)}) collective-permute-start(bf16[128,128]{1,0:T(8,128)(2,1)} %get-tuple-element.78), channel_id=1, source_target_pairs={{0,128},{4,132},{8,136},{12,140},{16,144},{20,148},{24,152},{28,15... | collective-permute-start | bytes 98312 | tf_op jit(solution)/shard_map/ppermute | solution.py:52
  10.1 6.2 %collective-permute-start.4 = (bf16[128,128]{1,0:T(8,128)(2,1)}, bf16[128,128]{1,0:T(8,128)(2,1)S(1)}, u32[]{:S(2)}, u32[]{:S(2)}) collective-permute-start(bf16[128,128]{1,0:T(8,128)(2,1)} %get-tuple-element.79), channel_id=1, source_target_pairs={{0,224},{4,228},{8,232},{12,236},{16,240},{20,244},{24,248},{28,25... | collective-permute-start | bytes 98312 | tf_op jit(solution)/shard_map/ppermute | solution.py:52
  17.8 32.6 %all-to-all-start = ((bf16[16,256,128]{2,1,0:T(8,128)(2,1)}), bf16[16,256,128]{2,1,0:T(8,128)(2,1)}, u32[]{:S(2)}, u32[]{:S(2)}) async-start(bf16[16,256,128]{2,1,0:T(8,128)(2,1)} %get-tuple-element.82), calls=%async_computation | async-start | bytes 2097152 | tf_op jit(solution)/shard_map/all_to_all | solution.py:48
  22.0 9.1 %collective-permute-start = (bf16[128,1024]{1,0:T(8,128)(2,1)}, bf16[128,1024]{1,0:T(8,128)(2,1)}, u32[]{:S(2)}, u32[]{:S(2)}) collective-permute-start(bf16[128,1024]{1,0:T(8,128)(2,1)} %c0.1), channel_id=1, source_target_pairs={{0,1},{1,0},{2,3},{3,2},{4,5},{5,4},{6,7},{7,6},{8,9},{9,8},{10,11... | collective-permute-start | bytes 786440 | tf_op jit(solution)/shard_map/ppermute | solution.py:363
  22.1 9.0 %collective-permute-start.5 = (bf16[128,1024]{1,0:T(8,128)(2,1)}, bf16[128,1024]{1,0:T(8,128)(2,1)}, u32[]{:S(2)}, u32[]{:S(2)}) collective-permute-start(bf16[128,1024]{1,0:T(8,128)(2,1)} %collective-permute-done.1.c2), channel_id=1, source_target_pairs={{0,1},{1,0},{2,3},{3,2},{4,5},{5,4},{6,7},{7,6},{8,9},{9,8},{10,11... | collective-permute-start | bytes 786440 | tf_op jit(solution)/shard_map/ppermute | solution.py:363
  22.6 17.6 %collective-permute-start.8 = (bf16[4,128,128]{2,1,0:T(8,128)(2,1)}, bf16[4,128,128]{2,1,0:T(8,128)(2,1)}, u32[]{:S(2)}, u32[]{:S(2)}) collective-permute-start(bf16[4,128,128]{2,1,0:T(8,128)(2,1)} %pad_maximum_fusion.1.qa), channel_id=1, source_target_pairs={{0,24},{4,28},{8,16},{12,20},{16,8},{20,12},{24,0},{28,4},{32,56},... | collective-permute-start | bytes 393224 | tf_op jit(solution)/shard_map/ppermute | solution.py:52
  28.8 21.7 %collective-permute-start.7 = (bf16[4,128,128]{2,1,0:T(8,128)(2,1)}, bf16[4,128,128]{2,1,0:T(8,128)(2,1)}, u32[]{:S(2)}, u32[]{:S(2)}) collective-permute-start(bf16[4,128,128]{2,1,0:T(8,128)(2,1)} %pad_maximum_fusion.1.qa), channel_id=1, source_target_pairs={{0,16},{4,20},{8,24},{12,28},{16,0},{20,4},{24,8},{28,12},{32,48},... | collective-permute-start | bytes 393224 | tf_op jit(solution)/shard_map/ppermute | solution.py:52
  29.7 20.8 %collective-permute-start.6 = (bf16[4,128,128]{2,1,0:T(8,128)(2,1)}, bf16[4,128,128]{2,1,0:T(8,128)(2,1)}, u32[]{:S(2)}, u32[]{:S(2)}) collective-permute-start(bf16[4,128,128]{2,1,0:T(8,128)(2,1)} %pad_maximum_fusion.1.qa), channel_id=1, source_target_pairs={{0,8},{4,12},{8,0},{12,4},{16,24},{20,28},{24,16},{28,20},{32,40},... | collective-permute-start | bytes 393224 | tf_op jit(solution)/shard_map/ppermute | solution.py:52
  50.4 21.5 %all-to-all-start.1 = ((bf16[16,128,128]{2,1,0:T(8,128)(2,1)}), bf16[16,128,128]{2,1,0:T(8,128)(2,1)}, u32[]{:S(2)}, u32[]{:S(2)}) async-start(bf16[16,128,128]{2,1,0:T(8,128)(2,1)} %get-tuple-element.88), calls=%async_computation.1 | async-start | bytes 1048576 | tf_op jit(solution)/shard_map/all_to_all | solution.py:48
  74.4 21.6 %all-to-all-start.2 = ((bf16[8,128,512]{2,1,0:T(8,128)(2,1)}), bf16[8,128,512]{2,1,0:T(8,128)(2,1)}, u32[]{:S(2)}, u32[]{:S(2)}) async-start(bf16[8,128,512]{2,1,0:T(8,128)(2,1)} %get-tuple-element.104), calls=%async_computation.2 | async-start | bytes 2097152 | tf_op jit(solution)/shard_map/all_to_all | solution.py:48
  78.7 6.7 %collective-permute-start.9 = (bf16[608,128]{1,0:T(8,128)(2,1)}, bf16[608,128]{1,0:T(8,128)(2,1)}, u32[]{:S(2)}, u32[]{:S(2)}) collective-permute-start(bf16[608,128]{1,0:T(8,128)(2,1)} %get-tuple-element.101), channel_id=1, source_target_pairs={{0,8},{4,12},{8,0},{12,4},{16,24},{20,28},{24,16},{28,20},{32,40},... | collective-permute-start | bytes 466952 | tf_op jit(solution)/shard_map/ppermute | solution.py:52
  79.1 10.2 %collective-permute-start.10 = (bf16[608,128]{1,0:T(8,128)(2,1)}, bf16[608,128]{1,0:T(8,128)(2,1)}, u32[]{:S(2)}, u32[]{:S(2)}) collective-permute-start(bf16[608,128]{1,0:T(8,128)(2,1)} %get-tuple-element.102), channel_id=1, source_target_pairs={{0,16},{4,20},{8,24},{12,28},{16,0},{20,4},{24,8},{28,12},{32,48},... | collective-permute-start | bytes 466952 | tf_op jit(solution)/shard_map/ppermute | solution.py:52
  79.9 13.8 %collective-permute-start.11 = (bf16[608,128]{1,0:T(8,128)(2,1)}, bf16[608,128]{1,0:T(8,128)(2,1)}, u32[]{:S(2)}, u32[]{:S(2)}) collective-permute-start(bf16[608,128]{1,0:T(8,128)(2,1)} %get-tuple-element.103), channel_id=1, source_target_pairs={{0,24},{4,28},{8,16},{12,20},{16,8},{20,12},{24,0},{28,4},{32,56},... | collective-permute-start | bytes 466952 | tf_op jit(solution)/shard_map/ppermute | solution.py:52
  96.0 14.4 %collective-permute-start.17 = (bf16[4,128,128]{2,1,0:T(8,128)(2,1)}, bf16[4,128,128]{2,1,0:T(8,128)(2,1)}, u32[]{:S(2)}, u32[]{:S(2)}) collective-permute-start(bf16[4,128,128]{2,1,0:T(8,128)(2,1)} %shard_map.96.a0), channel_id=1, source_target_pairs={{0,224},{4,228},{8,232},{12,236},{16,240},{20,244},{24,248},{28,25... | collective-permute-start | bytes 393224 | tf_op jit(solution)/shard_map/ppermute | solution.py:52
  99.9 10.4 %collective-permute-start.16 = (bf16[4,128,128]{2,1,0:T(8,128)(2,1)}, bf16[4,128,128]{2,1,0:T(8,128)(2,1)}, u32[]{:S(2)}, u32[]{:S(2)}) collective-permute-start(bf16[4,128,128]{2,1,0:T(8,128)(2,1)} %shard_map.96.a0), channel_id=1, source_target_pairs={{0,128},{4,132},{8,136},{12,140},{16,144},{20,148},{24,152},{28,15... | collective-permute-start | bytes 393224 | tf_op jit(solution)/shard_map/ppermute | solution.py:52
  100.5 9.9 %collective-permute-start.15 = (bf16[4,128,128]{2,1,0:T(8,128)(2,1)}, bf16[4,128,128]{2,1,0:T(8,128)(2,1)}, u32[]{:S(2)}, u32[]{:S(2)}) collective-permute-start(bf16[4,128,128]{2,1,0:T(8,128)(2,1)} %shard_map.96.a0), channel_id=1, source_target_pairs={{0,96},{4,100},{8,104},{12,108},{16,112},{20,116},{24,120},{28,124... | collective-permute-start | bytes 393224 | tf_op jit(solution)/shard_map/ppermute | solution.py:52
  110.4 24.8 %all-to-all-start.3 = ((bf16[16,256,128]{2,1,0:T(8,128)(2,1)}), bf16[16,256,128]{2,1,0:T(8,128)(2,1)}, u32[]{:S(2)}, u32[]{:S(2)}) async-start(bf16[16,256,128]{2,1,0:T(8,128)(2,1)} %get-tuple-element.127), calls=%async_computation.3 | async-start | bytes 2097152 | tf_op jit(solution)/shard_map/all_to_all | solution.py:48
  119.0 12.7 %collective-permute-start.18 = (bf16[4,4,128,128]{3,2,1,0:T(8,128)(2,1)}, bf16[4,4,128,128]{3,2,1,0:T(8,128)(2,1)}, u32[]{:S(2)}, u32[]{:S(2)}) collective-permute-start(bf16[4,4,128,128]{3,2,1,0:T(8,128)(2,1)} %pad_maximum_fusion), channel_id=1, source_target_pairs={{0,32},{4,36},{8,40},{12,44},{16,48},{20,52},{24,56},{28,60},{32,0... | collective-permute-start | bytes 1572872 | tf_op jit(solution)/shard_map/ppermute | solution.py:52
  120.5 14.6 %collective-permute-start.12 = (bf16[4,128,128]{2,1,0:T(8,128)(2,1)}, bf16[4,128,128]{2,1,0:T(8,128)(2,1)}, u32[]{:S(2)}, u32[]{:S(2)}) collective-permute-start(bf16[4,128,128]{2,1,0:T(8,128)(2,1)} %get-tuple-element.110), channel_id=1, source_target_pairs={{0,8},{4,12},{8,0},{12,4},{16,24},{20,28},{24,16},{28,20},{32,40},... | collective-permute-start | bytes 393224 | tf_op jit(solution)/shard_map/ppermute | solution.py:52
  121.4 13.8 %collective-permute-start.13 = (bf16[4,128,128]{2,1,0:T(8,128)(2,1)}, bf16[4,128,128]{2,1,0:T(8,128)(2,1)}, u32[]{:S(2)}, u32[]{:S(2)}) collective-permute-start(bf16[4,128,128]{2,1,0:T(8,128)(2,1)} %get-tuple-element.111), channel_id=1, source_target_pairs={{0,16},{4,20},{8,24},{12,28},{16,0},{20,4},{24,8},{28,12},{32,48},... | collective-permute-start | bytes 393224 | tf_op jit(solution)/shard_map/ppermute | solution.py:52
  123.5 11.6 %collective-permute-start.14 = (bf16[4,128,128]{2,1,0:T(8,128)(2,1)}, bf16[4,128,128]{2,1,0:T(8,128)(2,1)}, u32[]{:S(2)}, u32[]{:S(2)}) collective-permute-start(bf16[4,128,128]{2,1,0:T(8,128)(2,1)} %get-tuple-element.112), channel_id=1, source_target_pairs={{0,24},{4,28},{8,16},{12,20},{16,8},{20,12},{24,0},{28,4},{32,56},... | collective-permute-start | bytes 393224 | tf_op jit(solution)/shard_map/ppermute | solution.py:52
  131.6 9.8 %collective-permute-start.19 = (bf16[2,128,1024]{2,1,0:T(8,128)(2,1)}, bf16[2,128,1024]{2,1,0:T(8,128)(2,1)}, u32[]{:S(2)}, u32[]{:S(2)}) collective-permute-start(bf16[2,128,1024]{2,1,0:T(8,128)(2,1)} %get-tuple-element.123), channel_id=1, source_target_pairs={{0,1},{1,0},{2,3},{3,2},{4,5},{5,4},{6,7},{7,6},{8,9},{9,8},{10,11... | collective-permute-start | bytes 1572872 | tf_op jit(solution)/shard_map/ppermute | solution.py:363
  135.2 23.7 %all-to-all-start.4 = ((bf16[8,64,512]{2,1,0:T(8,128)(2,1)}), bf16[8,64,512]{2,1,0:T(8,128)(2,1)}, u32[]{:S(2)}, u32[]{:S(2)}) async-start(bf16[8,64,512]{2,1,0:T(8,128)(2,1)} %shard_map.98), calls=%async_computation.4 | async-start | bytes 1048576 | tf_op jit(solution)/shard_map/all_to_all | solution.py:48
  143.6 8.7 %collective-permute-start.20 = (bf16[128,1024]{1,0:T(8,128)(2,1)}, bf16[128,1024]{1,0:T(8,128)(2,1)}, u32[]{:S(2)}, u32[]{:S(2)}) collective-permute-start(bf16[128,1024]{1,0:T(8,128)(2,1)} %get-tuple-element.125), channel_id=1, source_target_pairs={{0,2},{1,3},{2,0},{3,1},{4,6},{5,7},{6,4},{7,5},{8,10},{9,11},{10,... | collective-permute-start | bytes 786440 | tf_op jit(solution)/shard_map/ppermute | solution.py:363
  147.4 6.8 %collective-permute-start.21 = (bf16[128,128]{1,0:T(8,128)(2,1)}, bf16[128,128]{1,0:T(8,128)(2,1)}, u32[]{:S(2)}, u32[]{:S(2)}) collective-permute-start(bf16[128,128]{1,0:T(8,128)(2,1)} %get-tuple-element.137), channel_id=1, source_target_pairs={{0,96},{4,100},{8,104},{12,108},{16,112},{20,116},{24,120},{28,124... | collective-permute-start | bytes 98312 | tf_op jit(solution)/shard_map/ppermute | solution.py:52
  149.4 4.7 %collective-permute-start.22 = (bf16[128,128]{1,0:T(8,128)(2,1)}, bf16[128,128]{1,0:T(8,128)(2,1)}, u32[]{:S(2)}, u32[]{:S(2)}) collective-permute-start(bf16[128,128]{1,0:T(8,128)(2,1)} %get-tuple-element.138), channel_id=1, source_target_pairs={{0,128},{4,132},{8,136},{12,140},{16,144},{20,148},{24,152},{28,15... | collective-permute-start | bytes 98312 | tf_op jit(solution)/shard_map/ppermute | solution.py:52
  150.3 6.3 %collective-permute-start.23 = (bf16[128,128]{1,0:T(8,128)(2,1)}, bf16[128,128]{1,0:T(8,128)(2,1)}, u32[]{:S(2)}, u32[]{:S(2)}) collective-permute-start(bf16[128,128]{1,0:T(8,128)(2,1)} %get-tuple-element.139), channel_id=1, source_target_pairs={{0,224},{4,228},{8,232},{12,236},{16,240},{20,244},{24,248},{28,25... | collective-permute-start | bytes 98312 | tf_op jit(solution)/shard_map/ppermute | solution.py:52
